TPU v7x, 128 devices: a whole 4x4x4 slice. The times are simulated.
128 devices in a mesh: dp: 16 (over y_lo, x, core), tensor: 8 (over z, y_hi).
Axes of the slice: x: 4, y: 4 (y_hi: 2, y_lo: 2; y = y_hi * 2 + y_lo), z: 4, core: 2. Of those that a mesh axis runs over, the one named last changes fastest.
Arguments:
- tokens: bfloat16 [2560, 4096], P('dp', 'tensor'), may hold values from -6 to 6
- gate_pre: bfloat16 [2560, 16384], P('dp', 'tensor'), may hold values from -10 to 10
- up_pre: bfloat16 [2560, 16384], P('dp', 'tensor'), may hold values from -6 to 6
- d_hidden: bfloat16 [2560, 16384], P('dp', 'tensor'), may hold values from -6 to 6
- gate_weight: bfloat16 [4096, 16384], P('dp', 'tensor'), may hold values from -0.046875 to 0.046875
- up_weight: bfloat16 [4096, 16384], P('dp', 'tensor'), may hold values from -0.046875 to 0.046875
Outputs:
- d_tokens: bfloat16 [2560, 4096], P('dp', 'tensor')
- d_gate_weight: bfloat16 [4096, 16384], P('dp', 'tensor')
- d_up_weight: bfloat16 [4096, 16384], P('dp', 'tensor')
All inputs are finite; a program needn't handle non-finite values.
Results may differ from a plain program's by a relative error of at most 0.022.
Values may be sent and summed in bfloat16 or wider, within the bound.
No kernel may reach another device: no remote copies, remote signals or barrier semaphores. Data moves between devices by JAX's collectives and lax.ppermute only.
A program may use at most 128 MiB of HBM per device.

v0:
```python
import jax
import jax.numpy as jnp
from jax import lax
from jax.sharding import PartitionSpec as P


def finish(partial_sum):
    return lax.psum_scatter(
        partial_sum.astype(jnp.bfloat16), "tensor", scatter_dimension=1, tiled=True
    )


def gather_tokens(tokens):
    return lax.all_gather(tokens, "tensor", axis=1, tiled=True)


def input_grads(d_gate, d_up, gate_weight, up_weight):
    contract = (((1,), (1,)), ((), ()))
    pieces = lax.all_gather((d_gate, d_up), "dp", axis=0, tiled=True)
    first = lax.dot_general(pieces[0], gate_weight, contract, preferred_element_type=jnp.float32)
    spread = first + lax.dot_general(
        pieces[1], up_weight, contract, preferred_element_type=jnp.float32
    )
    partial_sum = lax.all_to_all(
        spread.astype(jnp.bfloat16), "dp", split_axis=0, concat_axis=1, tiled=True
    ).astype(spread.dtype)
    return finish(partial_sum)


def weight_grads(tokens, d_gate, d_up):
    whole = gather_tokens(tokens)
    both = jnp.concatenate([d_gate, d_up], axis=1)
    summed = lax.psum_scatter(
        lax.dot_general(
            whole, both, (((0,), (0,)), ((), ())), preferred_element_type=jnp.float32
        ).astype(jnp.bfloat16),
        "dp",
        scatter_dimension=0,
        tiled=True,
    )
    width = d_gate.shape[1]
    return (summed[:, :width], summed[:, width:])


def local(tokens, gate_pre, up_pre, d_hidden, gate_weight, up_weight):
    gated = gate_pre.astype(jnp.float32)
    sigma = jax.nn.sigmoid(gated)
    upstream = d_hidden.astype(jnp.float32)
    d_up = (upstream * gated * sigma).astype(jnp.bfloat16)
    d_gate = (upstream * up_pre.astype(jnp.float32) * sigma * (1.0 + gated * (1.0 - sigma))).astype(
        jnp.bfloat16
    )
    d_tokens = input_grads(d_gate, d_up, gate_weight, up_weight)
    grad_gate, grad_up = weight_grads(tokens, d_gate, d_up)
    return (d_tokens, grad_gate, grad_up)


def solution(mesh):
    placed = (
        P("dp", "tensor"),
        P("dp", "tensor"),
        P("dp", "tensor"),
        P("dp", "tensor"),
        P("dp", "tensor"),
        P("dp", "tensor"),
    )
    return jax.shard_map(
        local,
        mesh=mesh,
        in_specs=placed,
        out_specs=(P("dp", "tensor"), P("dp", "tensor"), P("dp", "tensor")),
        check_vma=False,
    )
```

profile of v0, /device:TPU:48, one launch (start us, length us, event | category | flops | bytes accessed | tf_op | source)
XLA Modules:
  0.0 467.2 jit_solution(2082507134920944425)
XLA Ops:
  7.2 0.0 copy-start
  7.2 0.0 all-gather.8.cloned.1.call-start
  7.2 0.7 all-gather.8.cloned.1.call-update
  7.9 0.0 all-gather.4.cloned.1.call-start
  8.0 3.2 fusion.9
  11.2 0.0 copy-start.2
  11.2 0.0 copy-start.3
  11.2 0.0 all-gather.4.cloned.1.call-update
  11.2 0.0 all-gather.6.cloned.1.call-start
  11.3 0.7 all-gather.6.cloned.1.call-update
  12.0 0.0 reduce-scatter.5.cloned.1.call-start
  12.0 43.9 %all-gather.8.cloned.1.call-done = bf16[160,4096]{1,0:T(8,128)(2,1)} async-done(((bf16[160,512]{1,0:T(8,128)(2,1)}), bf16[160,4096]{1,0:T(8,128)(2,1)}) %all-gather.8.cloned.1.call-update) | async-done | bytes 1310736 | tf_op jit(solution)/shard_map/all_gather | solution.py:14
  55.9 0.0 copy-done.2
  55.9 0.0 copy-done.3
  55.9 15.2 %convert_bitcast_fusion = bf16[4096,4096]{0,1:T(8,128)(2,1)} fusion(bf16[160,4096]{1,0:T(8,128)(2,1)} %all-gather.8.cloned.1.call-done, bf16[160,2048]{1,0:T(8,128)(2,1)S(1)} %copy-done.2, bf16[160,2048]{1,0:T(8,128)(2,1)S(1)} %copy-done.3), kind=kOutput, calls=%fused_computation | convolution fusion | flops 5388107776 | bytes 36175872 | tf_op jit(solution)/shard_map/dot_general | solution.py:34
  71.1 0.0 reduce-scatter.5.cloned.1.call-update
  71.1 0.0 copy-start.4
  71.2 0.0 reduce-scatter.3.cloned.1.call-start
  71.2 50.5 %all-gather.4.cloned.1.call-done = bf16[2560,2048]{1,0:T(8,128)(2,1)} async-done(((bf16[160,2048]{1,0:T(8,128)(2,1)}), bf16[2560,2048]{1,0:T(8,128)(2,1)}) %all-gather.4.cloned.1.call-update) | async-done | bytes 10485776 | tf_op jit(solution)/shard_map/all_gather | solution.py:19
  121.7 0.0 copy-done
  121.7 8.4 %fusion.15 = f32[2560,256]{1,0:T(8,128)} fusion(bf16[2560,2048]{1,0:T(8,128)(2,1)} %all-gather.4.cloned.1.call-done, bf16[256,2048]{1,0:T(8,128)(2,1)S(1)} %copy-done), kind=kOutput, calls=%fused_computation.21 | convolution fusion | flops 2684354560 | bytes 14155776 | tf_op jit(solution)/shard_map/dot_general | solution.py:20
  130.1 56.7 %all-gather.6.cloned.1.call-done = bf16[2560,2048]{1,0:T(8,128)(2,1)} async-done(((bf16[160,2048]{1,0:T(8,128)(2,1)}), bf16[2560,2048]{1,0:T(8,128)(2,1)}) %all-gather.6.cloned.1.call-update) | async-done | bytes 10485776 | tf_op jit(solution)/shard_map/all_gather | solution.py:19
  186.8 0.0 copy-done.4
  186.8 7.7 %fusion = bf16[2560,256]{1,0:T(8,128)(2,1)S(1)} fusion(f32[2560,256]{1,0:T(8,128)} %fusion.15, bf16[2560,2048]{1,0:T(8,128)(2,1)} %all-gather.6.cloned.1.call-done, bf16[256,2048]{1,0:T(8,128)(2,1)S(1)} %copy-done.4), kind=kOutput, calls=%fused_computation.2 | convolution fusion | flops 2685665280 | bytes 15466496 | tf_op jit(solution)/shard_map/dot_general | solution.py:21
  194.5 29.5 %all_to_all.19 = bf16[16,160,256]{2,1,0:T(8,128)(2,1)S(1)} all-to-all(bf16[16,160,256]{2,1,0:T(8,128)(2,1)S(1)} %bitcast.13), channel_id=1, replica_groups=mesh['dp'=16,'tensor'=8] {'dp'}, dimensions={0} | all-to-all | bytes 2621440 | tf_op jit(solution)/shard_map/all_to_all | solution.py:24
  224.0 1.2 copy.12
  225.2 0.0 reduce-scatter.3.cloned.1.call-update
  225.3 161.2 %reduce-scatter.5.cloned.1.call-done = bf16[256,4096]{0,1:T(8,128)(2,1)} async-done(((bf16[4096,4096]{0,1:T(8,128)(2,1)}), bf16[256,4096]{0,1:T(8,128)(2,1)}) %reduce-scatter.5.cloned.1.call-update) | async-done | bytes 2097168 | tf_op jit(solution)/shard_map/reduce_scatter | solution.py:33
  386.4 1.7 fusion.14
  388.1 0.0 copy-start.1
  388.1 1.4 copy.11
  389.5 1.4 copy.10
  391.0 69.7 %reduce-scatter.3.cloned.1.call-done = bf16[160,512]{1,0:T(8,128)(2,1)} async-done(((bf16[160,4096]{1,0:T(8,128)(2,1)}), bf16[160,512]{1,0:T(8,128)(2,1)}) %reduce-scatter.3.cloned.1.call-update) | async-done | bytes 163856 | tf_op jit(solution)/shard_map/reduce_scatter | solution.py:8
  460.6 0.0 copy-done.1
Async XLA Ops:
  7.2 114.5 %copy-start = (bf16[256,2048]{1,0:T(8,128)(2,1)S(1)}, bf16[256,2048]{1,0:T(8,128)(2,1)}, u32[]{:S(2)}) copy-start(bf16[256,2048]{1,0:T(8,128)(2,1)} %param.10) | copy-start | bytes 3145732
  7.2 48.7 %all-gather.8.cloned.1.call-start = ((), (), s32[]{:S(2)}) async-start(), calls=%async_computation.6 | async-start | bytes 1474560 | tf_op jit(solution)/shard_map/all_gather | solution.py:14
  7.9 113.8 %all-gather.4.cloned.1.call-start = ((), (), s32[]{:S(2)}) async-start(), calls=%async_computation.3 | async-start | bytes 11141120 | tf_op jit(solution)/shard_map/all_gather | solution.py:19
  11.2 44.7 %copy-start.2 = (bf16[160,2048]{1,0:T(8,128)(2,1)S(1)}, bf16[160,2048]{1,0:T(8,128)(2,1)}, u32[]{:S(2)}) copy-start(bf16[160,2048]{1,0:T(8,128)(2,1)} %get-tuple-element.8) | copy-start | bytes 1966084
  11.2 44.7 %copy-start.3 = (bf16[160,2048]{1,0:T(8,128)(2,1)S(1)}, bf16[160,2048]{1,0:T(8,128)(2,1)}, u32[]{:S(2)}) copy-start(bf16[160,2048]{1,0:T(8,128)(2,1)} %get-tuple-element.9) | copy-start | bytes 1966084
  11.2 175.6 %all-gather.6.cloned.1.call-start = ((), (), s32[]{:S(2)}) async-start(), calls=%async_computation.4 | async-start | bytes 11141120 | tf_op jit(solution)/shard_map/all_gather | solution.py:19
  12.0 374.5 %reduce-scatter.5.cloned.1.call-start = ((), (), s32[]{:S(2)}) async-start(), calls=%async_computation.7 | async-start | bytes 35651584 | tf_op jit(solution)/shard_map/reduce_scatter | solution.py:33
  71.1 115.7 %copy-start.4 = (bf16[256,2048]{1,0:T(8,128)(2,1)S(1)}, bf16[256,2048]{1,0:T(8,128)(2,1)}, u32[]{:S(2)}) copy-start(bf16[256,2048]{1,0:T(8,128)(2,1)} %param.11) | copy-start | bytes 3145732
  71.2 389.5 %reduce-scatter.3.cloned.1.call-start = ((), (), s32[]{:S(2)}) async-start(), calls=%async_computation.5 | async-start | bytes 1474560 | tf_op jit(solution)/shard_map/reduce_scatter | solution.py:8
  388.1 72.5 %copy-start.1 = (bf16[256,2048]{1,0:T(8,128)(2,1)S(1)}, bf16[256,2048]{1,0:T(8,128)(2,1)}, u32[]{:S(2)}) copy-start(bf16[256,2048]{1,0:T(8,128)(2,1)} %param.10) | copy-start | bytes 3145732
Sparse Core Ops, SparseCore 0:
  10.2 45.6 all-gather.7
  58.2 63.4 all-gather.3
  124.0 62.8 all-gather.5
  189.1 197.2 reduce-scatter.4
  390.5 70.0 reduce-scatter.2
where the time goes:
time: 471 us; the launch traced here: 467 us
  waiting for transfers between devices  383 us (81%)
  matrix products  31.3 us (7%)
  blocking collectives  29.5 us (6%)
  between operations  13.8 us (3%)
  local copies, waits for them, and re-layouts  5.75 us (1%)
    reduce_scatter x1, waiting for transfers between devices, weight_grads(): lax.psum_scatter(lax.dot_general(whole, both, (((0,), (0,)), ((), ())), p...  161 us
    all_gather x2, waiting for transfers between devices, input_grads(): pieces = lax.all_gather((d_gate, d_up), 'dp', axis=0, tiled=True)  107 us
    reduce_scatter x1, waiting for transfers between devices, finish(): lax.psum_scatter(partial_sum.astype(jnp.bfloat16), 'tensor', scatter_dime...  69.7 us
    all_gather x1, waiting for transfers between devices, gather_tokens(): return lax.all_gather(tokens, 'tensor', axis=1, tiled=True)  43.9 us
    all_to_all x1, blocking collectives, input_grads(): lax.all_to_all(spread.astype(jnp.bfloat16), 'dp', split_axis=0, concat_ax...  29.5 us
    dot_general x1, matrix products, weight_grads(): lax.dot_general(whole, both, (((0,), (0,)), ((), ())), preferred_element_...  15.2 us
  transfers between devices with their start and end apart: 5, of which 5 were waited for; matrix products, arithmetic and copies ran while one was open for 9% of the time, Pallas kernels for 0%

commit v1 on v0

v1 whole, which is shorter than its diff:
```python
import jax
import jax.numpy as jnp
from jax import lax
from jax.sharding import Mesh
from jax.sharding import PartitionSpec as P

ALL = ("yl", "x", "c", "z", "yh")
TENSOR = ("z", "yh")
BF16 = jnp.bfloat16
F32 = jnp.float32
RIGHT = [(i, (i + 1) % 4) for i in range(4)]
LEFT = [(i, (i + 3) % 4) for i in range(4)]
SWAP = [(0, 1), (1, 0)]


def flat(q, c, t):
    return (q * 2 + c) * 8 + t


def group_at(q, place):
    return ((q >> 2) ^ (place >> 2)) * 4 + ((q & 3) + (place & 3)) % 4


TO_OWNER = [
    (flat(q, c, t), flat(group_at(q, t), c, q))
    for q in range(8)
    for c in range(2)
    for t in range(8)
]
TO_WORKER = [(b, a) for a, b in TO_OWNER]


def gather_tokens(tokens):
    mine = lax.ppermute(tokens, ALL, TO_WORKER)
    return lax.all_gather(mine, TENSOR, axis=0, tiled=False)


def right(v):
    return lax.ppermute(v, "x", RIGHT)


def left(v):
    return lax.ppermute(v, "x", LEFT)


def across(v):
    return lax.ppermute(v, "yl", SWAP)


def gather_groups(a, b):
    la, rb, ya = right(a), left(b), across(a)
    ra, lb, yb = left(a), right(b), across(b)
    oa, ob = right(la), left(rb)
    yla, yra, yoa = across(la), left(ya), across(oa)
    ylb, yrb = right(yb), across(rb)
    yob = right(ylb)
    return (a, ra, oa, la, ya, yra, yoa, yla), (b, rb, ob, lb, yb, yrb, yob, ylb)


def owner_sum(partial):
    rows = partial.shape[0] // 8
    parts = lax.all_to_all(partial.astype(BF16), TENSOR, split_axis=0, concat_axis=0, tiled=True)
    total = jnp.sum(parts.reshape(8, rows, -1).astype(F32), axis=0)
    return lax.ppermute(total.astype(BF16), ALL, TO_OWNER)


def local(tokens, gate_pre, up_pre, d_hidden, gate_weight, up_weight):
    core = lax.axis_index("c")
    held = jnp.concatenate([gate_weight, up_weight], axis=1)
    other = lax.ppermute(held, "c", SWAP)
    weights = jnp.where(
        core == 0,
        jnp.concatenate([held, other], axis=0),
        jnp.concatenate([other, held], axis=0),
    )
    features = gather_tokens(tokens)

    gated = gate_pre.astype(F32)
    sigma = jax.nn.sigmoid(gated)
    upstream = d_hidden.astype(F32)
    d_up = (upstream * gated * sigma).astype(BF16)
    d_gate = (upstream * up_pre.astype(F32) * sigma * (1.0 + gated * (1.0 - sigma))).astype(BF16)
    both = jnp.concatenate([d_gate, d_up], axis=1)
    half = both.shape[0] // 2
    upper, lower = gather_groups(both[:half], both[half:])

    d_tokens = []
    d_weight = None
    for part, (start, pieces) in enumerate(((0, upper), (half, lower))):
        rows = jnp.concatenate(pieces, axis=0)
        partial = lax.dot_general(
            rows, weights, (((1,), (1,)), ((), ())), preferred_element_type=F32
        )
        d_tokens.append(owner_sum(partial))
        chosen = features[:, start : start + half].reshape(8 * half, -1)
        term = lax.dot_general(
            chosen, rows, (((0,), (0,)), ((), ())), preferred_element_type=F32
        )
        d_weight = term if d_weight is None else d_weight + term

    count = held.shape[0]
    keep = lax.dynamic_slice_in_dim(d_weight, core * count, count, 0)
    send = lax.dynamic_slice_in_dim(d_weight, (1 - core) * count, count, 0)
    came = lax.ppermute(send.astype(BF16), "c", SWAP)
    total = (keep + came.astype(F32)).astype(BF16)
    width = gate_weight.shape[1]
    return jnp.concatenate(d_tokens, axis=0), total[:, :width], total[:, width:]


def solution(mesh):
    split = Mesh(mesh.devices.reshape(2, 4, 2, 4, 2), ALL)
    placed = P(("yl", "x", "c"), TENSOR)
    return jax.shard_map(
        local,
        mesh=split,
        in_specs=(placed,) * 6,
        out_specs=(placed,) * 3,
        check_vma=False,
    )
```

time: 471 us -> 210 us (0.45)
  waiting for transfers between devices: 383 us -> 91.5 us
  starting transfers between devices: 0.2 us -> 44 us
  blocking collectives: 29.5 us -> 0 us
  local copies, waits for them, and re-layouts: 5.75 us -> 24.4 us
  matrix products: 31.3 us -> 23.3 us
  other arithmetic: 3.24 us -> 8.13 us
    reduce_scatter x2 -> x0, waiting for transfers between devices: 231 us -> none  [the longest x1 161 us: weight_grads(): lax.psum_scatter(lax.dot_general(whole, both, (((0,), (0,)), ((), ())), p...]
    all_gather x3 -> x1, waiting for transfers between devices: 151 us -> 0.01 us  [gather_tokens(): return lax.all_gather(mine, TENSOR, axis=0, tiled=False)]
    ppermute x0 -> x19, waiting for transfers between devices: none -> 81.7 us  [the longest x5 31.7 us: right(): return lax.ppermute(v, 'x', RIGHT)]
    all_to_all x1 -> x0, blocking collectives: 29.5 us -> none  [input_grads(): lax.all_to_all(spread.astype(jnp.bfloat16), 'dp', split_axis=0, concat_ax...]
    ppermute x0 -> x19, starting transfers between devices: none -> 27.2 us  [the longest x4 11 us: left(): return lax.ppermute(v, 'x', LEFT)]
    unnamed x12 -> x31, local copies, waits for them, and re-layouts: 2.87 us -> 20.5 us
    all_to_all x0 -> x2, starting transfers between devices: none -> 16.8 us  [owner_sum(): lax.all_to_all(partial.astype(BF16), TENSOR, split_axis=0, concat_axis=0,...]
    all_to_all x0 -> x2, waiting for transfers between devices: none -> 9.81 us  [owner_sum(): lax.all_to_all(partial.astype(BF16), TENSOR, split_axis=0, concat_axis=0,...]
  transfers between devices with their start and end apart: 5 -> 22, of which waited for: 5 -> 7; matrix products, arithmetic and copies ran while one was open for 9% -> 20% of each run, Pallas kernels for 0% -> 0%
where the time goes in v1:
time: 210 us; the launch traced here: 206 us
  waiting for transfers between devices  91.5 us (44%)
  starting transfers between devices  44 us (21%)
  local copies, waits for them, and re-layouts  24.4 us (12%)
  matrix products  23.3 us (11%)
  between operations  14.3 us (7%)
  other arithmetic  8.13 us (4%)
    ppermute x5, waiting for transfers between devices, right(): return lax.ppermute(v, 'x', RIGHT)  31.7 us
    ppermute x1, waiting for transfers between devices, gather_tokens(): mine = lax.ppermute(tokens, ALL, TO_WORKER)  27.3 us
    unnamed x31, local copies, waits for them, and re-layouts  20.5 us
    ppermute x4, waiting for transfers between devices, left(): return lax.ppermute(v, 'x', LEFT)  18.7 us
    all_to_all x2, starting transfers between devices, owner_sum(): lax.all_to_all(partial.astype(BF16), TENSOR, split_axis=0, concat_axis=0,...  16.8 us
    dot_general x2, matrix products, local(): lax.dot_general(rows, weights, (((1,), (1,)), ((), ())), preferred_elemen...  14.2 us
    ppermute x4, starting transfers between devices, left(): return lax.ppermute(v, 'x', LEFT)  11 us
    all_to_all x2, waiting for transfers between devices, owner_sum(): lax.all_to_all(partial.astype(BF16), TENSOR, split_axis=0, concat_axis=0,...  9.81 us
  transfers between devices with their start and end apart: 22, of which 7 were waited for; matrix products, arithmetic and copies ran while one was open for 20% of the time, Pallas kernels for 0%

profile of v1, /device:TPU:48, one launch (start us, length us, event | category | flops | bytes accessed | tf_op | source)
XLA Modules:
  0.0 205.7 jit_solution(5260178497623622583)
XLA Ops:
  7.2 2.3 %fusion.4 = (bf16[160,2048]{1,0:T(8,128)(2,1)S(1)}, bf16[160,2048]{1,0:T(8,128)(2,1)S(1)}) fusion(bf16[160,2048]{1,0:T(8,128)(2,1)} %param.9, bf16[160,2048]{1,0:T(8,128)(2,1)} %param.7, bf16[160,2048]{1,0:T(8,128)(2,1)} %param.8), kind=kLoop, calls=%fused_computation.14 | loop fusion | flops 5242880 | bytes 3276800 | tf_op jit(solution)/shard_map/convert_element_type | solution.py:82
  9.6 1.6 constant_dynamic-update-slice_fusion.7
  11.2 2.8 %collective-permute-start.9 = (bf16[80,4096]{1,0:T(8,128)(2,1)}, bf16[80,4096]{1,0:T(8,128)(2,1)S(1)}, u32[]{:S(2)}, u32[]{:S(2)}) collective-permute-start(bf16[80,4096]{1,0:T(8,128)(2,1)} %get-tuple-element.15), channel_id=1, source_target_pairs={{0,48},{16,0},{32,16},{48,32},{1,49},{17,1},{33,17},{49,33},{2,50}... | collective-permute-start | bytes 1966088 | tf_op jit(solution)/shard_map/ppermute | solution.py:43
  13.9 1.3 collective-permute-start.12
  15.2 3.2 %collective-permute-start = (bf16[80,4096]{1,0:T(8,128)(2,1)}, bf16[80,4096]{1,0:T(8,128)(2,1)}, u32[]{:S(2)}, u32[]{:S(2)}) collective-permute-start(bf16[80,4096]{1,0:T(8,128)(2,1)} %get-tuple-element.7), channel_id=1, source_target_pairs={{0,48},{16,0},{32,16},{48,32},{1,49},{17,1},{33,17},{49,33},{2,50}... | collective-permute-start | bytes 1966088 | tf_op jit(solution)/shard_map/ppermute | solution.py:43
  18.5 1.9 collective-permute-start.17
  20.6 1.3 copy-done.3
  22.0 27.3 %collective-permute-done.17 = bf16[160,512]{1,0:T(8,128)(2,1)} collective-permute-done((bf16[160,512]{1,0:T(8,128)(2,1)}, bf16[160,512]{1,0:T(8,128)(2,1)}, u32[]{:S(2)}, u32[]{:S(2)}) %collective-permute-start.17) | collective-permute-done | bytes 163872 | tf_op jit(solution)/shard_map/ppermute | solution.py:34
  49.4 3.3 %collective-permute-start.10 = (bf16[80,4096]{1,0:T(8,128)(2,1)S(1)}, bf16[80,4096]{1,0:T(8,128)(2,1)S(1)}, u32[]{:S(2)}, u32[]{:S(2)}) collective-permute-start(bf16[80,4096]{1,0:T(8,128)(2,1)S(1)} %collective-permute-done.9), channel_id=1, source_target_pairs={{0,48},{16,0},{32,16},{48,32},{1,49},{17,1},{33,17},{49,33},{2,50}... | collective-permute-start | bytes 1966088 | tf_op jit(solution)/shard_map/ppermute | solution.py:43
  52.7 0.9 constant_dynamic-update-slice_fusion.16
  53.5 1.3 collective-permute-start.3
  54.8 2.0 constant_dynamic-update-slice_fusion.6
  56.8 8.7 %collective-permute-done.10 = bf16[80,4096]{1,0:T(8,128)(2,1)S(1)} collective-permute-done((bf16[80,4096]{1,0:T(8,128)(2,1)S(1)}, bf16[80,4096]{1,0:T(8,128)(2,1)S(1)}, u32[]{:S(2)}, u32[]{:S(2)}) %collective-permute-start.10) | collective-permute-done | bytes 655392 | tf_op jit(solution)/shard_map/ppermute | solution.py:43
  65.5 0.9 constant_dynamic-update-slice_fusion.15
  66.4 1.3 collective-permute-start.13
  67.7 2.2 %collective-permute-start.2 = (bf16[80,4096]{1,0:T(8,128)(2,1)S(1)}, bf16[80,4096]{1,0:T(8,128)(2,1)S(1)}, u32[]{:S(2)}, u32[]{:S(2)}) collective-permute-start(bf16[80,4096]{1,0:T(8,128)(2,1)S(1)} %collective-permute-done.1), channel_id=1, source_target_pairs={{0,16},{16,32},{32,48},{48,0},{1,17},{17,33},{33,49},{49,1},{2,18}... | collective-permute-start | bytes 1966088 | tf_op jit(solution)/shard_map/ppermute | solution.py:39
  69.8 2.0 constant_dynamic-update-slice_fusion.14
  71.8 0.9 constant_dynamic-update-slice_fusion.13
  72.8 0.7 collective-permute-start.6
  73.5 27.0 %collective-permute-done.2 = bf16[80,4096]{1,0:T(8,128)(2,1)S(1)} collective-permute-done((bf16[80,4096]{1,0:T(8,128)(2,1)S(1)}, bf16[80,4096]{1,0:T(8,128)(2,1)S(1)}, u32[]{:S(2)}, u32[]{:S(2)}) %collective-permute-start.2) | collective-permute-done | bytes 655392 | tf_op jit(solution)/shard_map/ppermute | solution.py:39
  100.5 1.7 collective-permute-start.4
  102.3 0.9 constant_dynamic-update-slice_fusion.5
  103.2 0.9 constant_dynamic-update-slice_fusion.4
  104.0 0.9 constant_dynamic-update-slice_fusion.3
  104.9 0.7 collective-permute-start.5
  106.0 0.9 constant_dynamic-update-slice_fusion.12
  106.9 10.1 %collective-permute-done.4 = bf16[80,4096]{1,0:T(8,128)(2,1)S(1)} collective-permute-done((bf16[80,4096]{1,0:T(8,128)(2,1)S(1)}, bf16[80,4096]{1,0:T(8,128)(2,1)S(1)}, u32[]{:S(2)}, u32[]{:S(2)}) %collective-permute-start.4) | collective-permute-done | bytes 655392 | tf_op jit(solution)/shard_map/ppermute | solution.py:43
  116.9 0.9 constant_dynamic-update-slice_fusion.2
  117.8 4.7 %collective-permute-done.15 = bf16[80,4096]{1,0:T(8,128)(2,1)S(1)} collective-permute-done((bf16[80,4096]{1,0:T(8,128)(2,1)S(1)}, bf16[80,4096]{1,0:T(8,128)(2,1)S(1)}, u32[]{:S(2)}, u32[]{:S(2)}) %collective-permute-start.15) | collective-permute-done | bytes 655392 | tf_op jit(solution)/shard_map/ppermute | solution.py:39
  122.5 0.9 constant_dynamic-update-slice_fusion.11
  123.4 0.9 constant_dynamic-update-slice_fusion.10
  124.3 0.9 constant_dynamic-update-slice_fusion.1
  125.2 0.9 constant_dynamic-update-slice_fusion
  126.1 7.0 %convolution_convert_fusion = bf16[640,512]{1,0:T(8,128)(2,1)} fusion(bf16[640,4096]{1,0:T(8,128)(2,1)} %constant_dynamic-update-slice_fusion.10, bf16[256,4096]{1,0:T(8,128)(2,1)S(1)} %collective-permute-done.7, bf16[256,4096]{1,0:T(8,128)(2,1)S(1)} %copy-done.4, pred[]{:T(512)S(6)} %eq.3), kind=kOutput, calls=%fused_computation.10 | convolution fusion | flops 2703556608 | bytes 10092545 | tf_op jit(solution)/shard_map/dot_general | solution.py:91
  133.1 9.6 %all-to-all-start.1 = ((bf16[8,80,512]{2,1,0:T(8,128)(2,1)}), bf16[8,80,512]{2,1,0:T(8,128)(2,1)S(1)}, u32[]{:S(2)}, u32[]{:S(2)}) async-start(bf16[8,80,512]{2,1,0:T(8,128)(2,1)} %bitcast.1), calls=%async_computation.1 | async-start | bytes 1310720 | tf_op jit(solution)/shard_map/all_to_all | solution.py:62
  142.7 1.5 fusion.16
  144.3 5.6 %fusion.17 = f32[4096,512]{1,0:T(8,128)S(1)} fusion(bf16[640,4096]{1,0:T(8,128)(2,1)} %constant_dynamic-update-slice_fusion.10, bf16[640,512]{1,0:T(8,128)(2,1)S(1)} %bitcast.21), kind=kOutput, calls=%fused_computation.48 | convolution fusion | flops 2684354560 | bytes 14286848 | tf_op jit(solution)/shard_map/dot_general | solution.py:96
  149.9 3.5 %convolution_add_fusion = f32[4096,512]{1,0:T(8,128)S(1)} fusion(f32[4096,512]{1,0:T(8,128)S(1)} %fusion.17, bf16[640,4096]{1,0:T(8,128)(2,1)S(1)} %bitcast.18, bf16[640,512]{1,0:T(8,128)(2,1)S(1)} %bitcast.19), kind=kOutput, calls=%fused_computation | convolution fusion | flops 2686451712 | bytes 22675456 | tf_op jit(solution)/shard_map/dot_general | solution.py:96
  153.4 3.3 %copy-done = f32[4096,512]{1,0:T(8,128)} copy-done((f32[4096,512]{1,0:T(8,128)}, f32[4096,512]{1,0:T(8,128)S(1)}, u32[]{:S(2)}) %copy-start) | copy-done | bytes 8388632
  157.0 7.2 %convolution_convert_fusion.1 = bf16[640,512]{1,0:T(8,128)(2,1)} fusion(bf16[640,4096]{1,0:T(8,128)(2,1)S(1)} %bitcast.18, bf16[256,4096]{1,0:T(8,128)(2,1)} %copy-done.5, bf16[256,4096]{1,0:T(8,128)(2,1)} %copy-done.3, pred[]{:T(512)S(6)} %eq.3), kind=kOutput, calls=%fused_computation.11 | convolution fusion | flops 2703556608 | bytes 10092545 | tf_op jit(solution)/shard_map/dot_general | solution.py:91
  164.2 7.2 %all-to-all-start = ((bf16[8,80,512]{2,1,0:T(8,128)(2,1)}), bf16[8,80,512]{2,1,0:T(8,128)(2,1)S(1)}, u32[]{:S(2)}, u32[]{:S(2)}) async-start(bf16[8,80,512]{2,1,0:T(8,128)(2,1)} %bitcast.22), calls=%async_computation | async-start | bytes 1310720 | tf_op jit(solution)/shard_map/all_to_all | solution.py:62
  171.5 1.9 collective-permute-start.16
  173.5 9.8 %all-to-all-done = bf16[8,80,512]{2,1,0:T(8,128)(2,1)S(1)} async-done(((bf16[8,80,512]{2,1,0:T(8,128)(2,1)}), bf16[8,80,512]{2,1,0:T(8,128)(2,1)S(1)}, u32[]{:S(2)}, u32[]{:S(2)}) %all-to-all-start) | async-done | bytes 655392 | tf_op jit(solution)/shard_map/all_to_all | solution.py:62
  183.4 4.5 %collective-permute-start.8 = (bf16[80,512]{1,0:T(8,128)(2,1)S(1)}, bf16[80,512]{1,0:T(8,128)(2,1)S(1)}, u32[]{:S(2)}, u32[]{:S(2)}) collective-permute-start(bf16[80,512]{1,0:T(8,128)(2,1)S(1)} %reduce_sum.24), channel_id=1, source_target_pairs={{0,0},{1,16},{2,32},{3,48},{4,64},{5,80},{6,96},{7,112},{8,8},{9,2... | collective-permute-start | bytes 245768 | tf_op jit(solution)/shard_map/ppermute | solution.py:64
  187.9 4.0 %collective-permute-done.8 = bf16[80,512]{1,0:T(8,128)(2,1)S(1)} collective-permute-done((bf16[80,512]{1,0:T(8,128)(2,1)S(1)}, bf16[80,512]{1,0:T(8,128)(2,1)S(1)}, u32[]{:S(2)}, u32[]{:S(2)}) %collective-permute-start.8) | collective-permute-done | bytes 81952 | tf_op jit(solution)/shard_map/ppermute | solution.py:64
  192.5 3.3 %fusion = bf16[256,4096]{0,1:T(8,128)(2,1)S(1)} fusion(bf16[256,4096]{0,1:T(8,128)(2,1)} %collective-permute-done.18, f32[4096,512]{1,0:T(8,128)} %copy-done, s32[]{:T(128)S(6)} %select_n.16), kind=kLoop, calls=%fused_computation.3 | loop fusion | flops 3145728 | bytes 8388612 | tf_op jit(solution)/shard_map/convert_element_type | solution.py:105
  196.0 1.4 copy.9
  197.4 1.4 copy.10
  (45 shorter events, 2.0 us)
Async XLA Ops:
  7.2 13.2 %copy-start.1 = (bf16[256,2048]{1,0:T(8,128)(2,1)S(1)}, bf16[256,2048]{1,0:T(8,128)(2,1)}, u32[]{:S(2)}) copy-start(bf16[256,2048]{1,0:T(8,128)(2,1)} %param.10) | copy-start | bytes 3145732
  7.2 13.3 %copy-start.2 = (bf16[256,2048]{1,0:T(8,128)(2,1)S(1)}, bf16[256,2048]{1,0:T(8,128)(2,1)}, u32[]{:S(2)}) copy-start(bf16[256,2048]{1,0:T(8,128)(2,1)} %param.11) | copy-start | bytes 3145732
  7.2 135.5 %all-gather.3.cloned.1.call-start = ((), (), s32[]{:S(2)}) async-start(), calls=%async_computation.2 | async-start | bytes 1474560 | tf_op jit(solution)/shard_map/all_gather | solution.py:35
  11.2 38.2 %collective-permute-start.9 = (bf16[80,4096]{1,0:T(8,128)(2,1)}, bf16[80,4096]{1,0:T(8,128)(2,1)S(1)}, u32[]{:S(2)}, u32[]{:S(2)}) collective-permute-start(bf16[80,4096]{1,0:T(8,128)(2,1)} %get-tuple-element.15), channel_id=1, source_target_pairs={{0,48},{16,0},{32,16},{48,32},{1,49},{17,1},{33,17},{49,33},{2,50}... | collective-permute-start | bytes 1966088 | tf_op jit(solution)/shard_map/ppermute | solution.py:43
  13.9 52.4 %collective-permute-start.11 = (bf16[80,4096]{1,0:T(8,128)(2,1)}, bf16[80,4096]{1,0:T(8,128)(2,1)}, u32[]{:S(2)}, u32[]{:S(2)}) collective-permute-start(bf16[80,4096]{1,0:T(8,128)(2,1)} %get-tuple-element.15), channel_id=1, source_target_pairs={{0,16},{16,32},{32,48},{48,0},{1,17},{17,33},{33,49},{49,1},{2,18}... | collective-permute-start | bytes 1966088 | tf_op jit(solution)/shard_map/ppermute | solution.py:39
  13.9 53.7 %collective-permute-start.12 = (bf16[80,4096]{1,0:T(8,128)(2,1)}, bf16[80,4096]{1,0:T(8,128)(2,1)S(1)}, u32[]{:S(2)}, u32[]{:S(2)}) collective-permute-start(bf16[80,4096]{1,0:T(8,128)(2,1)} %get-tuple-element.15), channel_id=1, source_target_pairs={{0,64},{64,0},{1,65},{65,1},{2,66},{66,2},{3,67},{67,3},{4,68},{68... | collective-permute-start | bytes 1966088 | tf_op jit(solution)/shard_map/ppermute | solution.py:47
  15.2 38.3 %collective-permute-start = (bf16[80,4096]{1,0:T(8,128)(2,1)}, bf16[80,4096]{1,0:T(8,128)(2,1)}, u32[]{:S(2)}, u32[]{:S(2)}) collective-permute-start(bf16[80,4096]{1,0:T(8,128)(2,1)} %get-tuple-element.7), channel_id=1, source_target_pairs={{0,48},{16,0},{32,16},{48,32},{1,49},{17,1},{33,17},{49,33},{2,50}... | collective-permute-start | bytes 1966088 | tf_op jit(solution)/shard_map/ppermute | solution.py:43
  18.5 30.9 %collective-permute-start.17 = (bf16[160,512]{1,0:T(8,128)(2,1)}, bf16[160,512]{1,0:T(8,128)(2,1)}, u32[]{:S(2)}, u32[]{:S(2)}) collective-permute-start(bf16[160,512]{1,0:T(8,128)(2,1)} %param.6), channel_id=1, source_target_pairs={{0,0},{16,1},{32,2},{48,3},{64,4},{80,5},{96,6},{112,7},{8,8},{24,... | collective-permute-start | bytes 491528 | tf_op jit(solution)/shard_map/ppermute | solution.py:34
  20.6 1.4 copy-start.3
  49.3 18.4 %collective-permute-start.1 = (bf16[80,4096]{1,0:T(8,128)(2,1)}, bf16[80,4096]{1,0:T(8,128)(2,1)S(1)}, u32[]{:S(2)}, u32[]{:S(2)}) collective-permute-start(bf16[80,4096]{1,0:T(8,128)(2,1)} %get-tuple-element.7), channel_id=1, source_target_pairs={{0,16},{16,32},{32,48},{48,0},{1,17},{17,33},{33,49},{49,1},{2,18}... | collective-permute-start | bytes 1966088 | tf_op jit(solution)/shard_map/ppermute | solution.py:39
  49.4 16.1 %collective-permute-start.10 = (bf16[80,4096]{1,0:T(8,128)(2,1)S(1)}, bf16[80,4096]{1,0:T(8,128)(2,1)S(1)}, u32[]{:S(2)}, u32[]{:S(2)}) collective-permute-start(bf16[80,4096]{1,0:T(8,128)(2,1)S(1)} %collective-permute-done.9), channel_id=1, source_target_pairs={{0,48},{16,0},{32,16},{48,32},{1,49},{17,1},{33,17},{49,33},{2,50}... | collective-permute-start | bytes 1966088 | tf_op jit(solution)/shard_map/ppermute | solution.py:43
  53.5 19.3 %collective-permute-start.3 = (bf16[80,4096]{1,0:T(8,128)(2,1)}, bf16[80,4096]{1,0:T(8,128)(2,1)S(1)}, u32[]{:S(2)}, u32[]{:S(2)}) collective-permute-start(bf16[80,4096]{1,0:T(8,128)(2,1)} %get-tuple-element.7), channel_id=1, source_target_pairs={{0,64},{64,0},{1,65},{65,1},{2,66},{66,2},{3,67},{67,3},{4,68},{68... | collective-permute-start | bytes 1966088 | tf_op jit(solution)/shard_map/ppermute | solution.py:47
  65.5 60.6 %collective-permute-start.7 = (bf16[256,4096]{1,0:T(8,128)(2,1)}, bf16[256,4096]{1,0:T(8,128)(2,1)S(1)}, u32[]{:S(2)}, u32[]{:S(2)}) collective-permute-start(bf16[256,4096]{1,0:T(8,128)(2,1)} %copy-done.3), channel_id=1, source_target_pairs={{0,8},{8,0},{1,9},{9,1},{2,10},{10,2},{3,11},{11,3},{4,12},{12,4},... | collective-permute-start | bytes 6291464 | tf_op jit(solution)/shard_map/ppermute | solution.py:70
  66.4 38.6 %collective-permute-start.13 = (bf16[80,4096]{1,0:T(8,128)(2,1)S(1)}, bf16[80,4096]{1,0:T(8,128)(2,1)S(1)}, u32[]{:S(2)}, u32[]{:S(2)}) collective-permute-start(bf16[80,4096]{1,0:T(8,128)(2,1)S(1)} %collective-permute-done.9), channel_id=1, source_target_pairs={{0,64},{64,0},{1,65},{65,1},{2,66},{66,2},{3,67},{67,3},{4,68},{68... | collective-permute-start | bytes 1966088 | tf_op jit(solution)/shard_map/ppermute | solution.py:47
  67.7 38.0 %collective-permute-start.14 = (bf16[80,4096]{1,0:T(8,128)(2,1)S(1)}, bf16[80,4096]{1,0:T(8,128)(2,1)S(1)}, u32[]{:S(2)}, u32[]{:S(2)}) collective-permute-start(bf16[80,4096]{1,0:T(8,128)(2,1)S(1)} %collective-permute-done.12), channel_id=1, source_target_pairs={{0,16},{16,32},{32,48},{48,0},{1,17},{17,33},{33,49},{49,1},{2,18}... | collective-permute-start | bytes 1966088 | tf_op jit(solution)/shard_map/ppermute | solution.py:39
  67.7 32.8 %collective-permute-start.2 = (bf16[80,4096]{1,0:T(8,128)(2,1)S(1)}, bf16[80,4096]{1,0:T(8,128)(2,1)S(1)}, u32[]{:S(2)}, u32[]{:S(2)}) collective-permute-start(bf16[80,4096]{1,0:T(8,128)(2,1)S(1)} %collective-permute-done.1), channel_id=1, source_target_pairs={{0,16},{16,32},{32,48},{48,0},{1,17},{17,33},{33,49},{49,1},{2,18}... | collective-permute-start | bytes 1966088 | tf_op jit(solution)/shard_map/ppermute | solution.py:39
  72.8 52.4 %collective-permute-start.6 = (bf16[80,4096]{1,0:T(8,128)(2,1)S(1)}, bf16[80,4096]{1,0:T(8,128)(2,1)S(1)}, u32[]{:S(2)}, u32[]{:S(2)}) collective-permute-start(bf16[80,4096]{1,0:T(8,128)(2,1)S(1)} %collective-permute-done.1), channel_id=1, source_target_pairs={{0,64},{64,0},{1,65},{65,1},{2,66},{66,2},{3,67},{67,3},{4,68},{68... | collective-permute-start | bytes 1966088 | tf_op jit(solution)/shard_map/ppermute | solution.py:47
  100.5 16.4 %collective-permute-start.4 = (bf16[80,4096]{1,0:T(8,128)(2,1)S(1)}, bf16[80,4096]{1,0:T(8,128)(2,1)S(1)}, u32[]{:S(2)}, u32[]{:S(2)}) collective-permute-start(bf16[80,4096]{1,0:T(8,128)(2,1)S(1)} %collective-permute-done.3), channel_id=1, source_target_pairs={{0,48},{16,0},{32,16},{48,32},{1,49},{17,1},{33,17},{49,33},{2,50}... | collective-permute-start | bytes 1966088 | tf_op jit(solution)/shard_map/ppermute | solution.py:43
  103.1 23.0 %copy-start.4 = (bf16[256,4096]{1,0:T(8,128)(2,1)S(1)}, bf16[256,4096]{1,0:T(8,128)(2,1)}, u32[]{:S(2)}) copy-start(bf16[256,4096]{1,0:T(8,128)(2,1)} %copy-done.3) | copy-start | bytes 6291460
  104.9 19.4 %collective-permute-start.5 = (bf16[80,4096]{1,0:T(8,128)(2,1)S(1)}, bf16[80,4096]{1,0:T(8,128)(2,1)S(1)}, u32[]{:S(2)}, u32[]{:S(2)}) collective-permute-start(bf16[80,4096]{1,0:T(8,128)(2,1)S(1)} %collective-permute-done.2), channel_id=1, source_target_pairs={{0,64},{64,0},{1,65},{65,1},{2,66},{66,2},{3,67},{67,3},{4,68},{68... | collective-permute-start | bytes 1966088 | tf_op jit(solution)/shard_map/ppermute | solution.py:47
  105.7 16.8 %collective-permute-start.15 = (bf16[80,4096]{1,0:T(8,128)(2,1)S(1)}, bf16[80,4096]{1,0:T(8,128)(2,1)S(1)}, u32[]{:S(2)}, u32[]{:S(2)}) collective-permute-start(bf16[80,4096]{1,0:T(8,128)(2,1)S(1)} %collective-permute-done.14), channel_id=1, source_target_pairs={{0,16},{16,32},{32,48},{48,0},{1,17},{17,33},{33,49},{49,1},{2,18}... | collective-permute-start | bytes 1966088 | tf_op jit(solution)/shard_map/ppermute | solution.py:39
  126.1 7.0 %copy-start.5 = (bf16[256,4096]{1,0:T(8,128)(2,1)}, bf16[256,4096]{1,0:T(8,128)(2,1)S(1)}, u32[]{:S(2)}) copy-start(bf16[256,4096]{1,0:T(8,128)(2,1)S(1)} %collective-permute-done.7) | copy-start | bytes 6291460
  133.1 31.1 %all-to-all-start.1 = ((bf16[8,80,512]{2,1,0:T(8,128)(2,1)}), bf16[8,80,512]{2,1,0:T(8,128)(2,1)S(1)}, u32[]{:S(2)}, u32[]{:S(2)}) async-start(bf16[8,80,512]{2,1,0:T(8,128)(2,1)} %bitcast.1), calls=%async_computation.1 | async-start | bytes 1310720 | tf_op jit(solution)/shard_map/all_to_all | solution.py:62
  142.7 7.1 %slice-start = ((s8[5242880]{0:T(1024)(128)(4,1)}), s8[4194304]{0:T(1024)(128)(4,1)S(1)}, s32[]{:S(2)}) async-start(s8[5242880]{0:T(1024)(128)(4,1)} %bitcast.17), calls=%async_computation.3 | async-start | bytes 8388608
  144.3 5.6 %slice-start.1 = ((s8[5242880]{0:T(1024)(128)(4,1)}), s8[1048576]{0:T(1024)(128)(4,1)S(1)}, s32[]{:S(2)}) async-start(s8[5242880]{0:T(1024)(128)(4,1)} %bitcast.17), calls=%async_computation.4 | async-start | bytes 2097152
  153.4 3.3 %copy-start = (f32[4096,512]{1,0:T(8,128)}, f32[4096,512]{1,0:T(8,128)S(1)}, u32[]{:S(2)}) copy-start(f32[4096,512]{1,0:T(8,128)S(1)} %convolution_add_fusion) | copy-start | bytes 25165828
  156.9 35.6 %collective-permute-start.18 = (bf16[256,4096]{0,1:T(8,128)(2,1)S(1)}, bf16[256,4096]{0,1:T(8,128)(2,1)}, u32[]{:S(2)}, u32[]{:S(2)}) collective-permute-start(bf16[256,4096]{0,1:T(8,128)(2,1)S(1)} %fusion.1), channel_id=1, source_target_pairs={{0,8},{8,0},{1,9},{9,1},{2,10},{10,2},{3,11},{11,3},{4,12},{12,4},... | collective-permute-start | bytes 6291464 | tf_op jit(solution)/shard_map/ppermute | solution.py:104
  164.2 19.0 %all-to-all-start = ((bf16[8,80,512]{2,1,0:T(8,128)(2,1)}), bf16[8,80,512]{2,1,0:T(8,128)(2,1)S(1)}, u32[]{:S(2)}, u32[]{:S(2)}) async-start(bf16[8,80,512]{2,1,0:T(8,128)(2,1)} %bitcast.22), calls=%async_computation | async-start | bytes 1310720 | tf_op jit(solution)/shard_map/all_to_all | solution.py:62
  171.5 16.3 %collective-permute-start.16 = (bf16[80,512]{1,0:T(8,128)(2,1)S(1)}, bf16[80,512]{1,0:T(8,128)(2,1)S(1)}, u32[]{:S(2)}, u32[]{:S(2)}) collective-permute-start(bf16[80,512]{1,0:T(8,128)(2,1)S(1)} %reduce_sum.25), channel_id=1, source_target_pairs={{0,0},{1,16},{2,32},{3,48},{4,64},{5,80},{6,96},{7,112},{8,8},{9,2... | collective-permute-start | bytes 245768 | tf_op jit(solution)/shard_map/ppermute | solution.py:64
  183.4 8.4 %collective-permute-start.8 = (bf16[80,512]{1,0:T(8,128)(2,1)S(1)}, bf16[80,512]{1,0:T(8,128)(2,1)S(1)}, u32[]{:S(2)}, u32[]{:S(2)}) collective-permute-start(bf16[80,512]{1,0:T(8,128)(2,1)S(1)} %reduce_sum.24), channel_id=1, source_target_pairs={{0,0},{1,16},{2,32},{3,48},{4,64},{5,80},{6,96},{7,112},{8,8},{9,2... | collective-permute-start | bytes 245768 | tf_op jit(solution)/shard_map/ppermute | solution.py:64
Sparse Core Ops, SparseCore 0:
  49.5 56.6 all-gather.2

commit v2 on v1

v2 whole, which is shorter than its diff:
```python
import functools

import jax
import jax.numpy as jnp
from jax import lax
from jax.experimental import pallas as pl
from jax.experimental.pallas import tpu as pltpu
from jax.sharding import Mesh
from jax.sharding import PartitionSpec as P

ALL = ("yl", "x", "c", "z", "yh")
TENSOR = ("z", "yh")
BF16 = jnp.bfloat16
F32 = jnp.float32
AHEAD = [(i, (i + 1) % 4) for i in range(4)]
BACK = [(i, (i + 3) % 4) for i in range(4)]
SWAP = [(0, 1), (1, 0)]
BLOCK = 1024


def flat(q, c, t):
    return (q * 2 + c) * 8 + t


def group_at(q, place):
    return ((q >> 2) ^ (place >> 2)) * 4 + ((q & 3) + (place & 3)) % 4


TO_OWNER = [
    (flat(q, c, t), flat(group_at(q, t), c, q))
    for q in range(8)
    for c in range(2)
    for t in range(8)
]
TO_WORKER = [(b, a) for a, b in TO_OWNER]


def right(v):
    return lax.ppermute(v, "x", AHEAD)


def left(v):
    return lax.ppermute(v, "x", BACK)


def across(v):
    return lax.ppermute(v, "yl", SWAP)


def sibling(v):
    return lax.ppermute(v, "c", SWAP)


def along_z(v, step):
    return lax.ppermute(v, "z", [(i, (i + step) % 4) for i in range(4)])


def around_z(pair):
    behind, ahead = along_z(pair, 1), along_z(pair, 3)
    return pair, ahead, along_z(behind[:1], 1), along_z(ahead[1:], 3), behind


def in_order(ring, z):
    ring = jnp.concatenate(ring, axis=0)
    ring = jnp.where((z & 1) == 1, jnp.roll(ring, 2, axis=0), ring)
    return jnp.where((z & 2) == 2, jnp.roll(ring, 4, axis=0), ring)


def input_term(rows, weights):
    return lax.dot_general(
        rows, weights, (((1,), (1,)), ((), ())), preferred_element_type=F32
    ).astype(BF16)


def stacked_term(features_ref, pieces, rows_ref):
    tall = pieces[0].shape[0]
    for place, piece in enumerate(pieces):
        rows_ref[place * tall : (place + 1) * tall, :] = piece[...]
    return jnp.dot(features_ref[...], rows_ref[...], preferred_element_type=F32)


def store_halves(blocks, total, low_ref, high_ref):
    @pl.when(pl.program_id(0) < blocks // 2)
    def _():
        low_ref[...] = total.astype(BF16)

    @pl.when(pl.program_id(0) >= blocks // 2)
    def _():
        high_ref[...] = total.astype(BF16)


def send_kernel(blocks, features_ref, *refs):
    *pieces, gate_ref, up_ref, rows_ref = refs
    store_halves(blocks, stacked_term(features_ref, pieces, rows_ref), gate_ref, up_ref)


def keep_kernel(blocks, features_ref, *refs):
    *pieces, came_gate_ref, came_up_ref, gate_ref, up_ref, rows_ref = refs
    total = stacked_term(features_ref, pieces, rows_ref)
    low = pl.program_id(0) < blocks // 2
    came = jnp.where(low, came_gate_ref[...], came_up_ref[...])
    store_halves(blocks, total + came.astype(F32), gate_ref, up_ref)


def weight_sum(features, pieces, came=()):
    count, deep = features.shape
    tall, width = pieces[0].shape
    blocks = width // BLOCK
    half = blocks // 2
    halves = [
        pl.BlockSpec((count, BLOCK), lambda j: (0, jnp.minimum(j, half - 1))),
        pl.BlockSpec((count, BLOCK), lambda j: (0, jnp.maximum(j - half, 0))),
    ]
    return pl.pallas_call(
        functools.partial(keep_kernel if came else send_kernel, blocks),
        out_shape=[jax.ShapeDtypeStruct((count, width // 2), BF16)] * 2,
        grid=(blocks,),
        in_specs=[pl.BlockSpec((count, deep), lambda j: (0, 0))]
        + [pl.BlockSpec((tall, BLOCK), lambda j: (0, j))] * len(pieces)
        + (halves if came else []),
        out_specs=halves,
        scratch_shapes=[pltpu.VMEM((deep, BLOCK), BF16)],
        compiler_params=pltpu.CompilerParams(vmem_limit_bytes=60 * 2**20),
    )(features, *pieces, *came)


def local(tokens, gate_pre, up_pre, d_hidden, gate_weight, up_weight):
    tied = lax.optimization_barrier
    core, z, yh = lax.axis_index("c"), lax.axis_index("z"), lax.axis_index("yh")
    tall = gate_pre.shape[0]
    count = gate_weight.shape[0]

    other_gate, other_up = sibling(gate_weight), sibling(up_weight)
    gated, up, upstream = (v.astype(F32) for v in (gate_pre, up_pre, d_hidden))
    sigma = jax.nn.sigmoid(gated)
    d_up = (upstream * gated * sigma).astype(BF16)
    d_gate = (upstream * up * sigma * (1.0 + gated * (1.0 - sigma))).astype(BF16)
    own = jnp.concatenate([d_gate, d_up], axis=1)

    la, ra, ya = right(own), left(own), across(own)
    held = jnp.concatenate([gate_weight, up_weight], axis=1)
    other = jnp.concatenate([other_gate, other_up], axis=1)
    weights = jnp.where(
        core == 0,
        jnp.concatenate([held, other], axis=0),
        jnp.concatenate([other, held], axis=0),
    )
    la, ra, ya, weights, tokens = tied((la, ra, ya, weights, tokens))

    oa, yra, yla = right(la), left(ya), across(la)
    mine = lax.ppermute(tokens, ALL, TO_WORKER)
    partial = jnp.zeros((8,) + tokens.shape, BF16)
    for place, v in ((0, own), (1, ra), (3, la), (4, ya)):
        partial = lax.dynamic_update_index_in_dim(partial, input_term(v, weights), place, 0)
    oa, yra, yla, partial, mine = tied((oa, yra, yla, partial, mine))

    top = right(yla[: tall // 2])
    bottom = left(yra[tall // 2 :])
    pair = lax.ppermute(mine, "yh", SWAP)
    pair = jnp.where(yh == 0, jnp.stack([mine, pair]), jnp.stack([pair, mine]))
    for place, v in ((2, oa), (5, yra), (7, yla)):
        partial = lax.dynamic_update_index_in_dim(partial, input_term(v, weights), place, 0)
    ring = around_z(pair)
    yoa = jnp.concatenate([top, bottom], axis=0)
    partial = lax.dynamic_update_index_in_dim(partial, input_term(yoa, weights), 6, 0)
    yoa, partial, ring = tied((yoa, partial, ring))

    parts = lax.all_to_all(partial, TENSOR, split_axis=0, concat_axis=0, tiled=True)
    flipped = in_order(ring, z).reshape(8 * tall, -1).T
    send = jnp.where(core == 0, flipped[count:], flipped[:count])
    keep = jnp.where(core == 0, flipped[:count], flipped[count:])
    pieces = (own, ra, oa, la, ya, yra, yoa, yla)
    came = tuple(sibling(v) for v in weight_sum(send, pieces))
    grad_gate, grad_up = weight_sum(keep, pieces, came)
    total = jnp.sum(parts.astype(F32), axis=0).astype(BF16)
    return lax.ppermute(total, ALL, TO_OWNER), grad_gate, grad_up


def solution(mesh):
    split = Mesh(mesh.devices.reshape(2, 4, 2, 4, 2), ALL)
    placement = P(("yl", "x", "c"), TENSOR)
    return jax.shard_map(
        local,
        mesh=split,
        in_specs=(placement,) * 6,
        out_specs=(placement,) * 3,
        check_vma=False,
    )
```

time: 210 us -> 154 us (0.73)
  the two profiles are of different devices: /device:TPU:48 before, /device:TPU:30 now
where the time goes in v2:
time: 154 us; the launch traced here: 153 us
  waiting for transfers between devices  56.5 us (37%)
  starting transfers between devices  38.2 us (25%)
  matrix products  20.1 us (13%)
  Pallas kernels  16.4 us (11%)
  local copies, waits for them, and re-layouts  12.7 us (8%)
  other arithmetic  8.12 us (5%)
    ppermute x1, waiting for transfers between devices, local(): mine = lax.ppermute(tokens, ALL, TO_WORKER)  20.7 us
    dot_general x8, matrix products, input_term(): lax.dot_general(rows, weights, (((1,), (1,)), ((), ())), preferred_elemen...  20.1 us
    ppermute x3, waiting for transfers between devices, right(): return lax.ppermute(v, 'x', AHEAD)  19.1 us
    pallas_call x2, Pallas kernels, weight_sum(): pl.pallas_call(functools.partial(keep_kernel if came else send_kernel, bl...  16.4 us
    ppermute x4, waiting for transfers between devices, along_z(): return lax.ppermute(v, 'z', [(i, (i + step) % 4) for i in range(4)])  14.9 us
    all_to_all x1, starting transfers between devices, local(): lax.all_to_all(partial, TENSOR, split_axis=0, concat_axis=0, tiled=True)  7.9 us
    ppermute x1, starting transfers between devices, local(): mine = lax.ppermute(tokens, ALL, TO_WORKER)  7.41 us
    ppermute x1, starting transfers between devices, local(): return (lax.ppermute(total, ALL, TO_OWNER), grad_gate, grad_up)  6.62 us
  transfers between devices with their start and end apart: 20, of which 8 were waited for; matrix products, arithmetic and copies ran while one was open for 25% of the time, Pallas kernels for 11%

profile of v2, /device:TPU:30, one launch (start us, length us, event | category | flops | bytes accessed | tf_op | source)
XLA Modules:
  0.0 153.1 jit_solution(12078198912622884926)
XLA Ops:
  0.7 0.5 collective-permute-start.4
  1.2 2.2 %fusion.2 = (bf16[160,2048]{1,0:T(8,128)(2,1)S(1)}, bf16[160,2048]{1,0:T(8,128)(2,1)S(1)}) fusion(bf16[160,2048]{1,0:T(8,128)(2,1)} %param.9, bf16[160,2048]{1,0:T(8,128)(2,1)} %param.7, bf16[160,2048]{1,0:T(8,128)(2,1)} %param.8), kind=kLoop, calls=%fused_computation.7 | loop fusion | flops 5242880 | bytes 3276800 | tf_op jit(solution)/shard_map/convert_element_type | solution.py:137
  3.6 0.7 copy-done.8
  4.2 0.5 collective-permute-start
  4.7 1.5 %collective-permute-start.1 = (bf16[160,4096]{1,0:T(8,128)(2,1)S(1)}, bf16[160,4096]{1,0:T(8,128)(2,1)S(1)}, u32[]{:S(2)}, u32[]{:S(2)}) collective-permute-start(bf16[160,4096]{1,0:T(8,128)(2,1)S(1)} %pad_maximum_fusion.refs_0_), channel_id=1, source_target_pairs={{0,48},{16,0},{32,16},{48,32},{1,49},{17,1},{33,17},{49,33},{2,50}... | collective-permute-start | bytes 3932168 | tf_op jit(solution)/shard_map/ppermute | solution.py:43
  6.3 0.7 collective-permute-start.2
  7.0 1.2 constant_dynamic-update-slice_fusion.1
  8.2 2.5 %constant_dynamic-update-slice_fusion = bf16[256,4096]{1,0:T(8,128)(2,1)} fusion(bf16[256,4096]{1,0:T(8,128)(2,1)} %constant_dynamic-update-slice_fusion.1, bf16[256,2048]{1,0:T(8,128)(2,1)} %param.11), kind=kLoop, calls=%fused_computation.43 | loop fusion | bytes 2097152 | tf_op jit(solution)/shard_map/concatenate | solution.py:141
  10.6 1.3 constant_dynamic-update-slice_fusion.3
  12.0 1.5 constant_dynamic-update-slice_fusion.2
  13.5 0.4 copy-done.7
  13.9 2.2 %maximum_select_fusion = bf16[512,4096]{1,0:T(8,128)(2,1)S(1)} fusion(bf16[256,4096]{1,0:T(8,128)(2,1)S(1)} %constant_dynamic-update-slice_fusion.2, bf16[256,4096]{1,0:T(8,128)(2,1)S(1)} %copy-done.7, pred[]{:T(512)S(6)} %eq.14), kind=kLoop, calls=%fused_computation | loop fusion | flops 18874368 | bytes 8388609 | tf_op jit(solution)/shard_map/jit(_where)/select_n | solution.py:143
  16.1 19.1 %collective-permute-done.refs_3_ = bf16[160,4096]{1,0:T(8,128)(2,1)} collective-permute-done((bf16[160,4096]{1,0:T(8,128)(2,1)S(1)}, bf16[160,4096]{1,0:T(8,128)(2,1)}, u32[]{:S(2)}, u32[]{:S(2)}) %collective-permute-start) | collective-permute-done | bytes 1310752 | tf_op jit(solution)/shard_map/ppermute | solution.py:39
  35.1 1.3 collective-permute-done.1.refs_1_
  36.6 1.7 %collective-permute-start.5 = (bf16[160,4096]{1,0:T(8,128)(2,1)}, bf16[160,4096]{1,0:T(8,128)(2,1)S(1)}, u32[]{:S(2)}, u32[]{:S(2)}) collective-permute-start(bf16[160,4096]{1,0:T(8,128)(2,1)} %collective-permute-done.refs_3_), channel_id=1, source_target_pairs={{0,16},{16,32},{32,48},{48,0},{1,17},{17,33},{33,49},{49,1},{2,18}... | collective-permute-start | bytes 3932168 | tf_op jit(solution)/shard_map/ppermute | solution.py:39
  38.3 0.7 collective-permute-start.7
  39.0 0.3 collective-permute-start.6
  39.4 1.6 %fusion.9 = bf16[1,160,512]{2,1,0:T(8,128)(2,1)S(1)} fusion(bf16[512,4096]{1,0:T(8,128)(2,1)S(1)} %maximum_select_fusion, bf16[160,2048]{1,0:T(8,128)(2,1)S(1)} %copy-done.9, bf16[160,2048]{1,0:T(8,128)(2,1)S(1)} %get-tuple-element.49), kind=kOutput, calls=%fused_computation.25 | convolution fusion | flops 673792000 | bytes 5668864 | tf_op jit(solution)/shard_map/dot_general | solution.py:70
  41.0 7.4 %collective-permute-start.8 = (bf16[160,512]{1,0:T(8,128)(2,1)S(1)}, bf16[160,512]{1,0:T(8,128)(2,1)S(1)}, u32[]{:S(2)}, u32[]{:S(2)}) collective-permute-start(bf16[160,512]{1,0:T(8,128)(2,1)S(1)} %copy-done.13), channel_id=1, source_target_pairs={{0,0},{16,1},{32,2},{48,3},{64,4},{80,5},{96,6},{112,7},{8,8},{24,... | collective-permute-start | bytes 491528 | tf_op jit(solution)/shard_map/ppermute | solution.py:151
  48.4 1.2 dynamic_update_slice.25
  49.6 2.2 %fusion.11 = bf16[8,160,512]{2,1,0:T(8,128)(2,1)} fusion(bf16[8,160,512]{2,1,0:T(8,128)(2,1)} %dynamic_update_slice.25, bf16[160,4096]{1,0:T(8,128)(2,1)S(1)} %copy-done.5, bf16[512,4096]{1,0:T(8,128)(2,1)S(1)} %maximum_select_fusion), kind=kOutput, calls=%fused_computation.27 | convolution fusion | flops 671170560 | bytes 5668864 | tf_op jit(solution)/shard_map/dot_general | solution.py:70
  51.8 3.6 %fusion.13 = bf16[8,160,512]{2,1,0:T(8,128)(2,1)} fusion(bf16[8,160,512]{2,1,0:T(8,128)(2,1)} %fusion.11, bf16[160,4096]{1,0:T(8,128)(2,1)} %collective-permute-done.refs_3_, bf16[512,4096]{1,0:T(8,128)(2,1)S(1)} %maximum_select_fusion), kind=kOutput, calls=%fused_computation.29 | convolution fusion | flops 671170560 | bytes 5668864 | tf_op jit(solution)/shard_map/dot_general | solution.py:70
  55.4 3.6 %fusion.15 = bf16[8,160,512]{2,1,0:T(8,128)(2,1)} fusion(bf16[8,160,512]{2,1,0:T(8,128)(2,1)} %fusion.13, bf16[160,4096]{1,0:T(8,128)(2,1)} %collective-permute-done.2.refs_4_, bf16[512,4096]{1,0:T(8,128)(2,1)S(1)} %maximum_select_fusion), kind=kOutput, calls=%fused_computation.31 | convolution fusion | flops 671170560 | bytes 5668864 | tf_op jit(solution)/shard_map/dot_general | solution.py:70
  59.0 20.7 %collective-permute-done.8 = bf16[160,512]{1,0:T(8,128)(2,1)S(1)} collective-permute-done((bf16[160,512]{1,0:T(8,128)(2,1)S(1)}, bf16[160,512]{1,0:T(8,128)(2,1)S(1)}, u32[]{:S(2)}, u32[]{:S(2)}) %collective-permute-start.8) | collective-permute-done | bytes 163872 | tf_op jit(solution)/shard_map/ppermute | solution.py:151
  79.8 0.8 collective-permute-start.9
  80.7 1.3 collective-permute-start.10
  82.0 1.9 %collective-permute-start.11 = (bf16[160,512]{1,0:T(8,128)(2,1)S(1)}, bf16[160,512]{1,0:T(8,128)(2,1)S(1)}, u32[]{:S(2)}, u32[]{:S(2)}) collective-permute-start(bf16[160,512]{1,0:T(8,128)(2,1)S(1)} %collective-permute-done.8), channel_id=1, source_target_pairs={{0,1},{1,0},{2,3},{3,2},{4,5},{5,4},{6,7},{7,6},{8,9},{9,8},{10,11... | collective-permute-start | bytes 491528 | tf_op jit(solution)/shard_map/ppermute | solution.py:159
  83.9 2.3 %fusion.17 = bf16[8,160,512]{2,1,0:T(8,128)(2,1)} fusion(bf16[8,160,512]{2,1,0:T(8,128)(2,1)} %fusion.15, bf16[160,4096]{1,0:T(8,128)(2,1)S(1)} %collective-permute-done.5.refs_2_, bf16[512,4096]{1,0:T(8,128)(2,1)S(1)} %maximum_select_fusion), kind=kOutput, calls=%fused_computation.33 | convolution fusion | flops 671170560 | bytes 5668864 | tf_op jit(solution)/shard_map/dot_general | solution.py:70
  86.1 2.3 %fusion.19 = bf16[8,160,512]{2,1,0:T(8,128)(2,1)} fusion(bf16[8,160,512]{2,1,0:T(8,128)(2,1)} %fusion.17, bf16[160,4096]{1,0:T(8,128)(2,1)S(1)} %collective-permute-done.6.refs_5_, bf16[512,4096]{1,0:T(8,128)(2,1)S(1)} %maximum_select_fusion), kind=kOutput, calls=%fused_computation.35 | convolution fusion | flops 671170560 | bytes 5668864 | tf_op jit(solution)/shard_map/dot_general | solution.py:70
  88.4 0.4 collective-permute-done.11
  88.9 2.2 %collective-permute-start.12 = (bf16[2,160,512]{2,1,0:T(8,128)(2,1)S(1)}, bf16[2,160,512]{2,1,0:T(8,128)(2,1)S(1)}, u32[]{:S(2)}, u32[]{:S(2)}) collective-permute-start(bf16[2,160,512]{2,1,0:T(8,128)(2,1)S(1)} %maximum_select_fusion.2), channel_id=1, source_target_pairs={{0,6},{2,0},{4,2},{6,4},{1,7},{3,1},{5,3},{7,5},{8,14},{10,8},{12,... | collective-permute-start | bytes 983048 | tf_op jit(solution)/shard_map/ppermute | solution.py:55
  91.1 2.3 %fusion.21 = bf16[8,160,512]{2,1,0:T(8,128)(2,1)} fusion(bf16[8,160,512]{2,1,0:T(8,128)(2,1)} %fusion.19, bf16[160,4096]{1,0:T(8,128)(2,1)S(1)} %collective-permute-done.7.refs_7_, bf16[512,4096]{1,0:T(8,128)(2,1)S(1)} %maximum_select_fusion), kind=kOutput, calls=%fused_computation.37 | convolution fusion | flops 671170560 | bytes 5668864 | tf_op jit(solution)/shard_map/dot_general | solution.py:70
  93.4 7.7 %collective-permute-done.13 = bf16[2,160,512]{2,1,0:T(8,128)(2,1)S(1)} collective-permute-done((bf16[2,160,512]{2,1,0:T(8,128)(2,1)S(1)}, bf16[2,160,512]{2,1,0:T(8,128)(2,1)S(1)}, u32[]{:S(2)}, u32[]{:S(2)}) %collective-permute-start.13) | collective-permute-done | bytes 327712 | tf_op jit(solution)/shard_map/ppermute | solution.py:55
  101.2 3.3 %collective-permute-start.15 = (bf16[1,160,512]{2,1,0:T(8,128)(2,1)S(1)}, bf16[1,160,512]{2,1,0:T(8,128)(2,1)S(1)}, u32[]{:S(2)}, u32[]{:S(2)}) collective-permute-start(bf16[1,160,512]{2,1,0:T(8,128)(2,1)S(1)} %slice.42), channel_id=1, source_target_pairs={{0,6},{2,0},{4,2},{6,4},{1,7},{3,1},{5,3},{7,5},{8,14},{10,8},{12,... | collective-permute-start | bytes 491528 | tf_op jit(solution)/shard_map/ppermute | solution.py:55
  104.6 2.3 %fusion.23 = bf16[8,160,512]{2,1,0:T(8,128)(2,1)} fusion(bf16[8,160,512]{2,1,0:T(8,128)(2,1)} %fusion.21, bf16[160,4096]{1,0:T(8,128)(2,1)S(1)} %constant_dynamic-update-slice_fusion.4.refs_6_, bf16[512,4096]{1,0:T(8,128)(2,1)S(1)} %maximum_select_fusion), kind=kOutput, calls=%fused_computation.39 | convolution fusion | flops 671170560 | bytes 5668864 | tf_op jit(solution)/shard_map/dot_general | solution.py:70
  106.9 0.8 collective-permute-done.14
  107.7 6.4 %collective-permute-done.15 = bf16[1,160,512]{2,1,0:T(8,128)(2,1)S(1)} collective-permute-done((bf16[1,160,512]{2,1,0:T(8,128)(2,1)S(1)}, bf16[1,160,512]{2,1,0:T(8,128)(2,1)S(1)}, u32[]{:S(2)}, u32[]{:S(2)}) %collective-permute-start.15) | collective-permute-done | bytes 163872 | tf_op jit(solution)/shard_map/ppermute | solution.py:55
  114.1 7.9 %all-to-all-start = ((bf16[8,160,512]{2,1,0:T(8,128)(2,1)}), bf16[8,160,512]{2,1,0:T(8,128)(2,1)S(1)}, u32[]{:S(2)}, u32[]{:S(2)}) async-start(bf16[8,160,512]{2,1,0:T(8,128)(2,1)} %fusion.23), calls=%async_computation | async-start | bytes 2621440 | tf_op jit(solution)/shard_map/all_to_all | solution.py:168
  122.7 1.5 copy.10
  124.2 2.4 %broadcast_select_fusion.1 = (bf16[256,1280]{1,0:T(8,128)(2,1)}, bf16[256,1280]{1,0:T(8,128)(2,1)}) fusion(pred[]{:T(512)S(6)} %eq.14, bf16[512,1280]{1,0:T(8,128)(2,1)} %bitcast.50), kind=kLoop, calls=%fused_computation.40 | loop fusion | flops 655360 | bytes 2621441 | tf_op jit(solution)/shard_map/jit(_where)/select_n | solution.py:170
  126.6 7.9 %shard_map.85 = (bf16[256,2048]{1,0:T(8,128)(2,1)}, bf16[256,2048]{1,0:T(8,128)(2,1)}) custom-call(bf16[256,1280]{1,0:T(8,128)(2,1)} %get-tuple-element.45.features_ref, bf16[160,4096]{1,0:T(8,128)(2,1)} %copy-done.3, bf16[160,4096]{1,0:T(8,128)(2,1)} %copy-done.4, bf16[160,4096]{1,0:T(8,128)(2,1)} %copy-done.6, ...), custom_call_target="tpu_custom_call" | custom-call | tf_op jit(solution)/shard_map/pallas_call | solution.py:114
  134.5 0.5 collective-permute-start.18
  135.0 0.9 reduce_sum.12
  135.9 6.6 %collective-permute-start.16 = (bf16[160,512]{1,0:T(8,128)(2,1)}, bf16[160,512]{1,0:T(8,128)(2,1)S(1)}, u32[]{:S(2)}, u32[]{:S(2)}) collective-permute-start(bf16[160,512]{1,0:T(8,128)(2,1)} %reduce_sum.12), channel_id=1, source_target_pairs={{0,0},{1,16},{2,32},{3,48},{4,64},{5,80},{6,96},{7,112},{8,8},{9,2... | collective-permute-start | bytes 491528 | tf_op jit(solution)/shard_map/ppermute | solution.py:176
  142.5 1.0 copy-done.10
  143.5 0.4 copy-done.11
  143.9 8.5 %shard_map.86 = (bf16[256,2048]{1,0:T(8,128)(2,1)}, bf16[256,2048]{1,0:T(8,128)(2,1)}) custom-call(bf16[256,1280]{1,0:T(8,128)(2,1)} %get-tuple-element.46.features_ref, bf16[160,4096]{1,0:T(8,128)(2,1)} %copy-done.3, bf16[160,4096]{1,0:T(8,128)(2,1)} %copy-done.4, bf16[160,4096]{1,0:T(8,128)(2,1)} %copy-done.6, ...), custom_call_target="tpu_custom_call" | custom-call | tf_op jit(solution)/shard_map/pallas_call | solution.py:114
  152.4 0.7 copy.30
  (61 shorter events, 1.5 us)
Async XLA Ops:
  0.6 10.0 %collective-permute-start.3 = (bf16[256,2048]{1,0:T(8,128)(2,1)}, bf16[256,2048]{1,0:T(8,128)(2,1)}, u32[]{:S(2)}, u32[]{:S(2)}) collective-permute-start(bf16[256,2048]{1,0:T(8,128)(2,1)} %param.10), channel_id=1, source_target_pairs={{0,8},{8,0},{1,9},{9,1},{2,10},{10,2},{3,11},{11,3},{4,12},{12,4},... | collective-permute-start | bytes 3145736 | tf_op jit(solution)/shard_map/ppermute | solution.py:51
  0.7 11.3 %collective-permute-start.4 = (bf16[256,2048]{1,0:T(8,128)(2,1)}, bf16[256,2048]{1,0:T(8,128)(2,1)}, u32[]{:S(2)}, u32[]{:S(2)}) collective-permute-start(bf16[256,2048]{1,0:T(8,128)(2,1)} %param.11), channel_id=1, source_target_pairs={{0,8},{8,0},{1,9},{9,1},{2,10},{10,2},{3,11},{11,3},{4,12},{12,4},... | collective-permute-start | bytes 3145736 | tf_op jit(solution)/shard_map/ppermute | solution.py:51
  3.4 0.8 copy-start.8
  3.4 3.6 %copy-start.12 = (bf16[256,2048]{1,0:T(8,128)(2,1)S(1)}, bf16[256,2048]{1,0:T(8,128)(2,1)}, u32[]{:S(2)}) copy-start(bf16[256,2048]{1,0:T(8,128)(2,1)} %param.10) | copy-start | bytes 3145732
  4.2 6.4 %copy-start.3 = (bf16[160,4096]{1,0:T(8,128)(2,1)}, bf16[160,4096]{1,0:T(8,128)(2,1)S(1)}, u32[]{:S(2)}) copy-start(bf16[160,4096]{1,0:T(8,128)(2,1)S(1)} %pad_maximum_fusion.refs_0_) | copy-start | bytes 3932164
  4.2 30.9 %collective-permute-start = (bf16[160,4096]{1,0:T(8,128)(2,1)S(1)}, bf16[160,4096]{1,0:T(8,128)(2,1)}, u32[]{:S(2)}, u32[]{:S(2)}) collective-permute-start(bf16[160,4096]{1,0:T(8,128)(2,1)S(1)} %pad_maximum_fusion.refs_0_), channel_id=1, source_target_pairs={{0,16},{16,32},{32,48},{48,0},{1,17},{17,33},{33,49},{49,1},{2,18}... | collective-permute-start | bytes 3932168 | tf_op jit(solution)/shard_map/ppermute | solution.py:39
  4.7 31.7 %collective-permute-start.1 = (bf16[160,4096]{1,0:T(8,128)(2,1)S(1)}, bf16[160,4096]{1,0:T(8,128)(2,1)S(1)}, u32[]{:S(2)}, u32[]{:S(2)}) collective-permute-start(bf16[160,4096]{1,0:T(8,128)(2,1)S(1)} %pad_maximum_fusion.refs_0_), channel_id=1, source_target_pairs={{0,48},{16,0},{32,16},{48,32},{1,49},{17,1},{33,17},{49,33},{2,50}... | collective-permute-start | bytes 3932168 | tf_op jit(solution)/shard_map/ppermute | solution.py:43
  6.3 30.3 %collective-permute-start.2 = (bf16[160,4096]{1,0:T(8,128)(2,1)S(1)}, bf16[160,4096]{1,0:T(8,128)(2,1)}, u32[]{:S(2)}, u32[]{:S(2)}) collective-permute-start(bf16[160,4096]{1,0:T(8,128)(2,1)S(1)} %pad_maximum_fusion.refs_0_), channel_id=1, source_target_pairs={{0,64},{64,0},{1,65},{65,1},{2,66},{66,2},{3,67},{67,3},{4,68},{68... | collective-permute-start | bytes 3932168 | tf_op jit(solution)/shard_map/ppermute | solution.py:47
  12.0 1.9 %copy-start.7 = (bf16[256,4096]{1,0:T(8,128)(2,1)S(1)}, bf16[256,4096]{1,0:T(8,128)(2,1)}, u32[]{:S(2)}) copy-start(bf16[256,4096]{1,0:T(8,128)(2,1)} %constant_dynamic-update-slice_fusion) | copy-start | bytes 6291460
  13.9 25.5 %copy-start.9 = (bf16[160,2048]{1,0:T(8,128)(2,1)S(1)}, bf16[160,2048]{1,0:T(8,128)(2,1)}, u32[]{:S(2)}) copy-start(bf16[160,2048]{1,0:T(8,128)(2,1)} %copy-done.8) | copy-start | bytes 1966084
  16.0 24.9 %copy-start.13 = (bf16[160,512]{1,0:T(8,128)(2,1)S(1)}, bf16[160,512]{1,0:T(8,128)(2,1)}, u32[]{:S(2)}) copy-start(bf16[160,512]{1,0:T(8,128)(2,1)} %param.6) | copy-start | bytes 491524
  36.4 1.9 %copy-start.4 = (bf16[160,4096]{1,0:T(8,128)(2,1)}, bf16[160,4096]{1,0:T(8,128)(2,1)S(1)}, u32[]{:S(2)}) copy-start(bf16[160,4096]{1,0:T(8,128)(2,1)S(1)} %collective-permute-done.1.refs_1_) | copy-start | bytes 3932164
  36.6 43.1 %collective-permute-start.5 = (bf16[160,4096]{1,0:T(8,128)(2,1)}, bf16[160,4096]{1,0:T(8,128)(2,1)S(1)}, u32[]{:S(2)}, u32[]{:S(2)}) collective-permute-start(bf16[160,4096]{1,0:T(8,128)(2,1)} %collective-permute-done.refs_3_), channel_id=1, source_target_pairs={{0,16},{16,32},{32,48},{48,0},{1,17},{17,33},{33,49},{49,1},{2,18}... | collective-permute-start | bytes 3932168 | tf_op jit(solution)/shard_map/ppermute | solution.py:39
  38.3 41.4 %collective-permute-start.7 = (bf16[160,4096]{1,0:T(8,128)(2,1)}, bf16[160,4096]{1,0:T(8,128)(2,1)S(1)}, u32[]{:S(2)}, u32[]{:S(2)}) collective-permute-start(bf16[160,4096]{1,0:T(8,128)(2,1)} %collective-permute-done.refs_3_), channel_id=1, source_target_pairs={{0,64},{64,0},{1,65},{65,1},{2,66},{66,2},{3,67},{67,3},{4,68},{68... | collective-permute-start | bytes 3932168 | tf_op jit(solution)/shard_map/ppermute | solution.py:47
  39.0 40.7 %collective-permute-start.6 = (bf16[160,4096]{1,0:T(8,128)(2,1)}, bf16[160,4096]{1,0:T(8,128)(2,1)S(1)}, u32[]{:S(2)}, u32[]{:S(2)}) collective-permute-start(bf16[160,4096]{1,0:T(8,128)(2,1)} %collective-permute-done.2.refs_4_), channel_id=1, source_target_pairs={{0,48},{16,0},{32,16},{48,32},{1,49},{17,1},{33,17},{49,33},{2,50}... | collective-permute-start | bytes 3932168 | tf_op jit(solution)/shard_map/ppermute | solution.py:43
  41.0 8.6 %copy-start.5 = (bf16[160,4096]{1,0:T(8,128)(2,1)S(1)}, bf16[160,4096]{1,0:T(8,128)(2,1)}, u32[]{:S(2)}) copy-start(bf16[160,4096]{1,0:T(8,128)(2,1)} %copy-done.4) | copy-start | bytes 3932164
  41.0 38.7 %collective-permute-start.8 = (bf16[160,512]{1,0:T(8,128)(2,1)S(1)}, bf16[160,512]{1,0:T(8,128)(2,1)S(1)}, u32[]{:S(2)}, u32[]{:S(2)}) collective-permute-start(bf16[160,512]{1,0:T(8,128)(2,1)S(1)} %copy-done.13), channel_id=1, source_target_pairs={{0,0},{16,1},{32,2},{48,3},{64,4},{80,5},{96,6},{112,7},{8,8},{24,... | collective-permute-start | bytes 491528 | tf_op jit(solution)/shard_map/ppermute | solution.py:151
  79.7 4.2 %copy-start.6 = (bf16[160,4096]{1,0:T(8,128)(2,1)}, bf16[160,4096]{1,0:T(8,128)(2,1)S(1)}, u32[]{:S(2)}) copy-start(bf16[160,4096]{1,0:T(8,128)(2,1)S(1)} %collective-permute-done.5.refs_2_) | copy-start | bytes 3932164
  79.7 6.4 %copy-start.1 = (bf16[160,4096]{1,0:T(8,128)(2,1)}, bf16[160,4096]{1,0:T(8,128)(2,1)S(1)}, u32[]{:S(2)}) copy-start(bf16[160,4096]{1,0:T(8,128)(2,1)S(1)} %collective-permute-done.6.refs_5_) | copy-start | bytes 3932164
  79.7 11.4 %copy-start = (bf16[160,4096]{1,0:T(8,128)(2,1)}, bf16[160,4096]{1,0:T(8,128)(2,1)S(1)}, u32[]{:S(2)}) copy-start(bf16[160,4096]{1,0:T(8,128)(2,1)S(1)} %collective-permute-done.7.refs_7_) | copy-start | bytes 3932164
  79.8 24.7 %collective-permute-start.9 = (bf16[80,4096]{1,0:T(8,128)(2,1)S(1)}, bf16[80,4096]{1,0:T(8,128)(2,1)S(1)}, u32[]{:S(2)}, u32[]{:S(2)}) collective-permute-start(bf16[80,4096]{1,0:T(8,128)(2,1)S(1)} %slice.33), channel_id=1, source_target_pairs={{0,16},{16,32},{32,48},{48,0},{1,17},{17,33},{33,49},{49,1},{2,18}... | collective-permute-start | bytes 1966088 | tf_op jit(solution)/shard_map/ppermute | solution.py:39
  80.7 23.9 %collective-permute-start.10 = (bf16[80,4096]{1,0:T(8,128)(2,1)S(1)}, bf16[80,4096]{1,0:T(8,128)(2,1)S(1)}, u32[]{:S(2)}, u32[]{:S(2)}) collective-permute-start(bf16[80,4096]{1,0:T(8,128)(2,1)S(1)} %slice.34), channel_id=1, source_target_pairs={{0,48},{16,0},{32,16},{48,32},{1,49},{17,1},{33,17},{49,33},{2,50}... | collective-permute-start | bytes 1966088 | tf_op jit(solution)/shard_map/ppermute | solution.py:43
  82.0 6.8 %collective-permute-start.11 = (bf16[160,512]{1,0:T(8,128)(2,1)S(1)}, bf16[160,512]{1,0:T(8,128)(2,1)S(1)}, u32[]{:S(2)}, u32[]{:S(2)}) collective-permute-start(bf16[160,512]{1,0:T(8,128)(2,1)S(1)} %collective-permute-done.8), channel_id=1, source_target_pairs={{0,1},{1,0},{2,3},{3,2},{4,5},{5,4},{6,7},{7,6},{8,9},{9,8},{10,11... | collective-permute-start | bytes 491528 | tf_op jit(solution)/shard_map/ppermute | solution.py:159
  88.9 12.3 %collective-permute-start.12 = (bf16[2,160,512]{2,1,0:T(8,128)(2,1)S(1)}, bf16[2,160,512]{2,1,0:T(8,128)(2,1)S(1)}, u32[]{:S(2)}, u32[]{:S(2)}) collective-permute-start(bf16[2,160,512]{2,1,0:T(8,128)(2,1)S(1)} %maximum_select_fusion.2), channel_id=1, source_target_pairs={{0,6},{2,0},{4,2},{6,4},{1,7},{3,1},{5,3},{7,5},{8,14},{10,8},{12,... | collective-permute-start | bytes 983048 | tf_op jit(solution)/shard_map/ppermute | solution.py:55
  91.1 10.0 %collective-permute-start.13 = (bf16[2,160,512]{2,1,0:T(8,128)(2,1)S(1)}, bf16[2,160,512]{2,1,0:T(8,128)(2,1)S(1)}, u32[]{:S(2)}, u32[]{:S(2)}) collective-permute-start(bf16[2,160,512]{2,1,0:T(8,128)(2,1)S(1)} %maximum_select_fusion.2), channel_id=1, source_target_pairs={{0,2},{2,4},{4,6},{6,0},{1,3},{3,5},{5,7},{7,1},{8,10},{10,12},{12... | collective-permute-start | bytes 983048 | tf_op jit(solution)/shard_map/ppermute | solution.py:55
  101.1 6.6 %collective-permute-start.14 = (bf16[1,160,512]{2,1,0:T(8,128)(2,1)S(1)}, bf16[1,160,512]{2,1,0:T(8,128)(2,1)S(1)}, u32[]{:S(2)}, u32[]{:S(2)}) collective-permute-start(bf16[1,160,512]{2,1,0:T(8,128)(2,1)S(1)} %slice.41), channel_id=1, source_target_pairs={{0,2},{2,4},{4,6},{6,0},{1,3},{3,5},{5,7},{7,1},{8,10},{10,12},{12... | collective-permute-start | bytes 491528 | tf_op jit(solution)/shard_map/ppermute | solution.py:55
  101.2 12.9 %collective-permute-start.15 = (bf16[1,160,512]{2,1,0:T(8,128)(2,1)S(1)}, bf16[1,160,512]{2,1,0:T(8,128)(2,1)S(1)}, u32[]{:S(2)}, u32[]{:S(2)}) collective-permute-start(bf16[1,160,512]{2,1,0:T(8,128)(2,1)S(1)} %slice.42), channel_id=1, source_target_pairs={{0,6},{2,0},{4,2},{6,4},{1,7},{3,1},{5,3},{7,5},{8,14},{10,8},{12,... | collective-permute-start | bytes 491528 | tf_op jit(solution)/shard_map/ppermute | solution.py:55
  104.6 2.3 %copy-start.2 = (bf16[160,4096]{1,0:T(8,128)(2,1)}, bf16[160,4096]{1,0:T(8,128)(2,1)S(1)}, u32[]{:S(2)}) copy-start(bf16[160,4096]{1,0:T(8,128)(2,1)S(1)} %constant_dynamic-update-slice_fusion.4.refs_6_) | copy-start | bytes 3932164
  114.1 20.9 %all-to-all-start = ((bf16[8,160,512]{2,1,0:T(8,128)(2,1)}), bf16[8,160,512]{2,1,0:T(8,128)(2,1)S(1)}, u32[]{:S(2)}, u32[]{:S(2)}) async-start(bf16[8,160,512]{2,1,0:T(8,128)(2,1)} %fusion.23), calls=%async_computation | async-start | bytes 2621440 | tf_op jit(solution)/shard_map/all_to_all | solution.py:168
  134.5 8.0 %collective-permute-start.17 = (bf16[256,2048]{1,0:T(8,128)(2,1)}, bf16[256,2048]{1,0:T(8,128)(2,1)S(1)}, u32[]{:S(2)}, u32[]{:S(2)}) collective-permute-start(bf16[256,2048]{1,0:T(8,128)(2,1)} %get-tuple-element.41), channel_id=1, source_target_pairs={{0,8},{8,0},{1,9},{9,1},{2,10},{10,2},{3,11},{11,3},{4,12},{12,4},... | collective-permute-start | bytes 3145736 | tf_op jit(solution)/shard_map/ppermute | solution.py:51
  134.5 8.0 %collective-permute-start.18 = (bf16[256,2048]{1,0:T(8,128)(2,1)}, bf16[256,2048]{1,0:T(8,128)(2,1)S(1)}, u32[]{:S(2)}, u32[]{:S(2)}) collective-permute-start(bf16[256,2048]{1,0:T(8,128)(2,1)} %get-tuple-element.42), channel_id=1, source_target_pairs={{0,8},{8,0},{1,9},{9,1},{2,10},{10,2},{3,11},{11,3},{4,12},{12,4},... | collective-permute-start | bytes 3145736 | tf_op jit(solution)/shard_map/ppermute | solution.py:51
  135.9 16.5 %collective-permute-start.16 = (bf16[160,512]{1,0:T(8,128)(2,1)}, bf16[160,512]{1,0:T(8,128)(2,1)S(1)}, u32[]{:S(2)}, u32[]{:S(2)}) collective-permute-start(bf16[160,512]{1,0:T(8,128)(2,1)} %reduce_sum.12), channel_id=1, source_target_pairs={{0,0},{1,16},{2,32},{3,48},{4,64},{5,80},{6,96},{7,112},{8,8},{9,2... | collective-permute-start | bytes 491528 | tf_op jit(solution)/shard_map/ppermute | solution.py:176
  142.5 1.0 copy-start.10
  142.5 1.3 copy-start.11

commit v3 on v2

--- a/solution.py
+++ b/solution.py
@@ -26,13 +26,16 @@
     return ((q >> 2) ^ (place >> 2)) * 4 + ((q & 3) + (place & 3)) % 4
 
 
-TO_OWNER = [
-    (flat(q, c, t), flat(group_at(q, t), c, q))
-    for q in range(8)
-    for c in range(2)
-    for t in range(8)
-]
-TO_WORKER = [(b, a) for a, b in TO_OWNER]
+def to_owner(flip):
+    return [
+        (flat(q, c, t), flat(group_at(q, t ^ flip), c, q))
+        for q in range(8)
+        for c in range(2)
+        for t in range(8)
+    ]
+
+
+TO_WORKER = [(b, a) for a, b in to_owner(0)]
 
 
 def right(v):
@@ -82,46 +85,41 @@
 def store_halves(blocks, total, low_ref, high_ref):
     @pl.when(pl.program_id(0) < blocks // 2)
     def _():
-        low_ref[...] = total.astype(BF16)
+        low_ref[...] = total.astype(low_ref.dtype)
 
     @pl.when(pl.program_id(0) >= blocks // 2)
     def _():
-        high_ref[...] = total.astype(BF16)
+        high_ref[...] = total.astype(high_ref.dtype)
 
 
-def send_kernel(blocks, features_ref, *refs):
+def sum_kernel(blocks, features_ref, *refs):
     *pieces, gate_ref, up_ref, rows_ref = refs
     store_halves(blocks, stacked_term(features_ref, pieces, rows_ref), gate_ref, up_ref)
 
 
-def keep_kernel(blocks, features_ref, *refs):
-    *pieces, came_gate_ref, came_up_ref, gate_ref, up_ref, rows_ref = refs
-    total = stacked_term(features_ref, pieces, rows_ref)
-    low = pl.program_id(0) < blocks // 2
-    came = jnp.where(low, came_gate_ref[...], came_up_ref[...])
-    store_halves(blocks, total + came.astype(F32), gate_ref, up_ref)
-
-
-def weight_sum(features, pieces, came=()):
+def weight_sum(features, pieces, dtype):
     count, deep = features.shape
     tall, width = pieces[0].shape
     blocks = width // BLOCK
     half = blocks // 2
-    halves = [
-        pl.BlockSpec((count, BLOCK), lambda j: (0, jnp.minimum(j, half - 1))),
-        pl.BlockSpec((count, BLOCK), lambda j: (0, jnp.maximum(j - half, 0))),
-    ]
     return pl.pallas_call(
-        functools.partial(keep_kernel if came else send_kernel, blocks),
-        out_shape=[jax.ShapeDtypeStruct((count, width // 2), BF16)] * 2,
+        functools.partial(sum_kernel, blocks),
+        out_shape=[jax.ShapeDtypeStruct((count, width // 2), dtype)] * 2,
         grid=(blocks,),
         in_specs=[pl.BlockSpec((count, deep), lambda j: (0, 0))]
-        + [pl.BlockSpec((tall, BLOCK), lambda j: (0, j))] * len(pieces)
-        + (halves if came else []),
-        out_specs=halves,
+        + [pl.BlockSpec((tall, BLOCK), lambda j: (0, j))] * len(pieces),
+        out_specs=[
+            pl.BlockSpec((count, BLOCK), lambda j: (0, jnp.minimum(j, half - 1))),
+            pl.BlockSpec((count, BLOCK), lambda j: (0, jnp.maximum(j - half, 0))),
+        ],
         scratch_shapes=[pltpu.VMEM((deep, BLOCK), BF16)],
         compiler_params=pltpu.CompilerParams(vmem_limit_bytes=60 * 2**20),
-    )(features, *pieces, *came)
+        cost_estimate=pl.CostEstimate(
+            flops=2 * count * deep * width,
+            bytes_accessed=2 * (deep * width + count * (deep + width)),
+            transcendentals=0,
+        ),
+    )(features, *pieces)
 
 
 def local(tokens, gate_pre, up_pre, d_hidden, gate_weight, up_weight):
@@ -152,7 +150,8 @@
     partial = jnp.zeros((8,) + tokens.shape, BF16)
     for place, v in ((0, own), (1, ra), (3, la), (4, ya)):
         partial = lax.dynamic_update_index_in_dim(partial, input_term(v, weights), place, 0)
-    oa, yra, yla, partial, mine = tied((oa, yra, yla, partial, mine))
+    oa, yra, yla, partial = tied((oa, yra, yla, partial))
+    _, mine = tied((yla, mine))
 
     top = right(yla[: tall // 2])
     bottom = left(yra[tall // 2 :])
@@ -163,17 +162,28 @@
     ring = around_z(pair)
     yoa = jnp.concatenate([top, bottom], axis=0)
     partial = lax.dynamic_update_index_in_dim(partial, input_term(yoa, weights), 6, 0)
-    yoa, partial, ring = tied((yoa, partial, ring))
+    yoa, partial, pair = tied((yoa, partial, pair))
 
-    parts = lax.all_to_all(partial, TENSOR, split_axis=0, concat_axis=0, tiled=True)
+    by_z = partial.reshape((4, 2) + partial.shape[1:])
+    block = [lax.dynamic_index_in_dim(by_z, (z + s) % 4, 0, keepdims=False) for s in range(4)]
+    came_z = [along_z(block[s], s) for s in (1, 3, 2)]
     flipped = in_order(ring, z).reshape(8 * tall, -1).T
     send = jnp.where(core == 0, flipped[count:], flipped[:count])
     keep = jnp.where(core == 0, flipped[:count], flipped[count:])
     pieces = (own, ra, oa, la, ya, yra, yoa, yla)
-    came = tuple(sibling(v) for v in weight_sum(send, pieces))
-    grad_gate, grad_up = weight_sum(keep, pieces, came)
-    total = jnp.sum(parts.astype(F32), axis=0).astype(BF16)
-    return lax.ppermute(total, ALL, TO_OWNER), grad_gate, grad_up
+    sent = weight_sum(send, pieces, BF16)
+    sums = block[0].astype(F32)
+    for v in came_z:
+        sums = sums + v.astype(F32)
+    same, cross = jnp.where(yh == 0, sums, sums[::-1]).astype(BF16)
+    same, cross, sent, keep = tied((same, cross, sent, keep))
+    came = tuple(sibling(v) for v in sent)
+    same = lax.ppermute(same, ALL, to_owner(0))
+    cross = lax.ppermute(cross, ALL, to_owner(1))
+    kept = weight_sum(keep, pieces, F32)
+    grad_gate, grad_up = ((k + v.astype(F32)).astype(BF16) for k, v in zip(kept, came))
+    d_tokens = (same.astype(F32) + cross.astype(F32)).astype(BF16)
+    return d_tokens, grad_gate, grad_up
 
 
 def solution(mesh):

time: 154 us -> 147 us (0.955)
  the two profiles are of different devices: /device:TPU:30 before, /device:TPU:48 now
where the time goes in v3:
time: 147 us; the launch traced here: 144 us
  waiting for transfers between devices  51.8 us (35%)
  starting transfers between devices  38 us (26%)
  Pallas kernels  16.3 us (11%)
  matrix products  15.4 us (10%)
  other arithmetic  12.4 us (8%)
  local copies, waits for them, and re-layouts  9.54 us (6%)
    ppermute x3, waiting for transfers between devices, right(): return lax.ppermute(v, 'x', AHEAD)  33.7 us
    pallas_call x2, Pallas kernels, weight_sum(): pl.pallas_call(functools.partial(sum_kernel, blocks), out_shape=[jax.Shap...  16.3 us
    dot_general x8, matrix products, input_term(): lax.dot_general(rows, weights, (((1,), (1,)), ((), ())), preferred_elemen...  15.4 us
    ppermute x7, starting transfers between devices, along_z(): return lax.ppermute(v, 'z', [(i, (i + step) % 4) for i in range(4)])  11.6 us
    ppermute x3, starting transfers between devices, left(): return lax.ppermute(v, 'x', BACK)  8.36 us
    ppermute x1, starting transfers between devices, local(): same = lax.ppermute(same, ALL, to_owner(0))  7.89 us
    ppermute x3, waiting for transfers between devices, left(): return lax.ppermute(v, 'x', BACK)  6.86 us
    ppermute x7, waiting for transfers between devices, along_z(): return lax.ppermute(v, 'z', [(i, (i + step) % 4) for i in range(4)])  6.15 us
  transfers between devices with their start and end apart: 23, of which 6 were waited for; matrix products, arithmetic and copies ran while one was open for 23% of the time, Pallas kernels for 11%

profile of v3, /device:TPU:48, one launch (start us, length us, event | category | flops | bytes accessed | tf_op | source)
XLA Modules:
  0.0 144.4 jit_solution(8968791519940730575)
XLA Ops:
  0.7 0.5 collective-permute-start.4
  1.2 2.2 %fusion.2 = (bf16[160,2048]{1,0:T(8,128)(2,1)S(1)}, bf16[160,2048]{1,0:T(8,128)(2,1)S(1)}) fusion(bf16[160,2048]{1,0:T(8,128)(2,1)} %param.9, bf16[160,2048]{1,0:T(8,128)(2,1)} %param.7, bf16[160,2048]{1,0:T(8,128)(2,1)} %param.8), kind=kLoop, calls=%fused_computation.9 | loop fusion | flops 5242880 | bytes 3276800 | tf_op jit(solution)/shard_map/convert_element_type | solution.py:135
  3.6 0.7 copy-done.9
  4.2 1.5 %collective-permute-start = (bf16[160,4096]{1,0:T(8,128)(2,1)S(1)}, bf16[160,4096]{1,0:T(8,128)(2,1)}, u32[]{:S(2)}, u32[]{:S(2)}) collective-permute-start(bf16[160,4096]{1,0:T(8,128)(2,1)S(1)} %pad_maximum_fusion.refs_0_), channel_id=1, source_target_pairs={{0,16},{16,32},{32,48},{48,0},{1,17},{17,33},{33,49},{49,1},{2,18}... | collective-permute-start | bytes 3932168 | tf_op jit(solution)/shard_map/ppermute | solution.py:42
  5.7 1.7 %collective-permute-start.1 = (bf16[160,4096]{1,0:T(8,128)(2,1)S(1)}, bf16[160,4096]{1,0:T(8,128)(2,1)S(1)}, u32[]{:S(2)}, u32[]{:S(2)}) collective-permute-start(bf16[160,4096]{1,0:T(8,128)(2,1)S(1)} %pad_maximum_fusion.refs_0_), channel_id=1, source_target_pairs={{0,48},{16,0},{32,16},{48,32},{1,49},{17,1},{33,17},{49,33},{2,50}... | collective-permute-start | bytes 3932168 | tf_op jit(solution)/shard_map/ppermute | solution.py:46
  7.5 1.3 collective-permute-start.2
  8.8 1.1 constant_dynamic-update-slice_fusion.1
  9.9 2.3 %constant_dynamic-update-slice_fusion = bf16[256,4096]{1,0:T(8,128)(2,1)} fusion(bf16[256,4096]{1,0:T(8,128)(2,1)} %constant_dynamic-update-slice_fusion.1, bf16[256,2048]{1,0:T(8,128)(2,1)} %param.11), kind=kLoop, calls=%fused_computation.56 | loop fusion | bytes 2097152 | tf_op jit(solution)/shard_map/concatenate | solution.py:139
  12.2 1.3 constant_dynamic-update-slice_fusion.3
  13.5 1.5 %constant_dynamic-update-slice_fusion.2 = bf16[256,4096]{1,0:T(8,128)(2,1)S(1)} fusion(bf16[256,4096]{1,0:T(8,128)(2,1)S(1)} %constant_dynamic-update-slice_fusion.3, bf16[256,2048]{1,0:T(8,128)(2,1)} %collective-permute-done.4), kind=kLoop, calls=%fused_computation.58 | loop fusion | bytes 2097152 | tf_op jit(solution)/shard_map/concatenate | solution.py:140
  15.0 0.4 copy-done.8
  15.4 2.2 %maximum_select_fusion = bf16[512,4096]{1,0:T(8,128)(2,1)S(1)} fusion(bf16[256,4096]{1,0:T(8,128)(2,1)S(1)} %constant_dynamic-update-slice_fusion.2, bf16[256,4096]{1,0:T(8,128)(2,1)S(1)} %copy-done.8, pred[]{:T(512)S(6)} %eq.21), kind=kLoop, calls=%fused_computation | loop fusion | flops 18874368 | bytes 8388609 | tf_op jit(solution)/shard_map/jit(_where)/select_n | solution.py:141
  17.6 18.7 %collective-permute-done.refs_3_ = bf16[160,4096]{1,0:T(8,128)(2,1)} collective-permute-done((bf16[160,4096]{1,0:T(8,128)(2,1)S(1)}, bf16[160,4096]{1,0:T(8,128)(2,1)}, u32[]{:S(2)}, u32[]{:S(2)}) %collective-permute-start) | collective-permute-done | bytes 1310752 | tf_op jit(solution)/shard_map/ppermute | solution.py:42
  36.3 1.5 %collective-permute-done.2.refs_4_ = bf16[160,4096]{1,0:T(8,128)(2,1)} collective-permute-done((bf16[160,4096]{1,0:T(8,128)(2,1)S(1)}, bf16[160,4096]{1,0:T(8,128)(2,1)}, u32[]{:S(2)}, u32[]{:S(2)}) %collective-permute-start.2) | collective-permute-done | bytes 1310752 | tf_op jit(solution)/shard_map/ppermute | solution.py:50
  37.8 0.3 collective-permute-start.5
  38.1 1.3 collective-permute-start.7
  39.4 3.0 %collective-permute-start.6 = (bf16[160,4096]{1,0:T(8,128)(2,1)}, bf16[160,4096]{1,0:T(8,128)(2,1)S(1)}, u32[]{:S(2)}, u32[]{:S(2)}) collective-permute-start(bf16[160,4096]{1,0:T(8,128)(2,1)} %collective-permute-done.2.refs_4_), channel_id=1, source_target_pairs={{0,48},{16,0},{32,16},{48,32},{1,49},{17,1},{33,17},{49,33},{2,50}... | collective-permute-start | bytes 3932168 | tf_op jit(solution)/shard_map/ppermute | solution.py:46
  42.3 1.6 %fusion.9 = bf16[1,160,512]{2,1,0:T(8,128)(2,1)S(1)} fusion(bf16[512,4096]{1,0:T(8,128)(2,1)S(1)} %maximum_select_fusion, bf16[160,2048]{1,0:T(8,128)(2,1)S(1)} %copy-done.10, bf16[160,2048]{1,0:T(8,128)(2,1)S(1)} %get-tuple-element.54), kind=kOutput, calls=%fused_computation.27 | convolution fusion | flops 673792000 | bytes 5668864 | tf_op jit(solution)/shard_map/dot_general | solution.py:73
  43.9 2.1 %collective-permute-start.10 = (bf16[160,512]{1,0:T(8,128)(2,1)S(1)}, bf16[160,512]{1,0:T(8,128)(2,1)S(1)}, u32[]{:S(2)}, u32[]{:S(2)}) collective-permute-start(bf16[160,512]{1,0:T(8,128)(2,1)S(1)} %copy-done.13), channel_id=1, source_target_pairs={{0,0},{16,1},{32,2},{48,3},{64,4},{80,5},{96,6},{112,7},{8,8},{24,... | collective-permute-start | bytes 491528 | tf_op jit(solution)/shard_map/ppermute | solution.py:149
  46.1 1.6 %fusion.11 = bf16[8,160,512]{2,1,0:T(8,128)(2,1)S(1)} fusion(bf16[8,160,512]{2,1,0:T(8,128)(2,1)S(1)} %dynamic_update_slice.25, bf16[160,4096]{1,0:T(8,128)(2,1)S(1)} %copy-done.5, bf16[512,4096]{1,0:T(8,128)(2,1)S(1)} %maximum_select_fusion), kind=kOutput, calls=%fused_computation.29 | convolution fusion | flops 671170560 | bytes 5668864 | tf_op jit(solution)/shard_map/dot_general | solution.py:73
  47.7 2.9 %fusion.13 = bf16[8,160,512]{2,1,0:T(8,128)(2,1)S(1)} fusion(bf16[8,160,512]{2,1,0:T(8,128)(2,1)S(1)} %fusion.11, bf16[160,4096]{1,0:T(8,128)(2,1)} %collective-permute-done.refs_3_, bf16[512,4096]{1,0:T(8,128)(2,1)S(1)} %maximum_select_fusion), kind=kOutput, calls=%fused_computation.31 | convolution fusion | flops 671170560 | bytes 5668864 | tf_op jit(solution)/shard_map/dot_general | solution.py:73
  50.6 2.9 %fusion.15 = bf16[8,160,512]{2,1,0:T(8,128)(2,1)S(1)} fusion(bf16[8,160,512]{2,1,0:T(8,128)(2,1)S(1)} %fusion.13, bf16[160,4096]{1,0:T(8,128)(2,1)} %collective-permute-done.2.refs_4_, bf16[512,4096]{1,0:T(8,128)(2,1)S(1)} %maximum_select_fusion), kind=kOutput, calls=%fused_computation.33 | convolution fusion | flops 671170560 | bytes 5668864 | tf_op jit(solution)/shard_map/dot_general | solution.py:73
  53.6 15.0 %collective-permute-done.5.refs_2_ = bf16[160,4096]{1,0:T(8,128)(2,1)S(1)} collective-permute-done((bf16[160,4096]{1,0:T(8,128)(2,1)}, bf16[160,4096]{1,0:T(8,128)(2,1)S(1)}, u32[]{:S(2)}, u32[]{:S(2)}) %collective-permute-start.5) | collective-permute-done | bytes 1310752 | tf_op jit(solution)/shard_map/ppermute | solution.py:42
  68.5 6.9 %collective-permute-done.6.refs_5_ = bf16[160,4096]{1,0:T(8,128)(2,1)S(1)} collective-permute-done((bf16[160,4096]{1,0:T(8,128)(2,1)}, bf16[160,4096]{1,0:T(8,128)(2,1)S(1)}, u32[]{:S(2)}, u32[]{:S(2)}) %collective-permute-start.6) | collective-permute-done | bytes 1310752 | tf_op jit(solution)/shard_map/ppermute | solution.py:46
  75.6 3.7 %collective-permute-start.9 = (bf16[80,4096]{1,0:T(8,128)(2,1)S(1)}, bf16[80,4096]{1,0:T(8,128)(2,1)S(1)}, u32[]{:S(2)}, u32[]{:S(2)}) collective-permute-start(bf16[80,4096]{1,0:T(8,128)(2,1)S(1)} %slice.34), channel_id=1, source_target_pairs={{0,48},{16,0},{32,16},{48,32},{1,49},{17,1},{33,17},{49,33},{2,50}... | collective-permute-start | bytes 1966088 | tf_op jit(solution)/shard_map/ppermute | solution.py:46
  79.2 1.6 %fusion.17 = bf16[8,160,512]{2,1,0:T(8,128)(2,1)S(1)} fusion(bf16[8,160,512]{2,1,0:T(8,128)(2,1)S(1)} %fusion.15, bf16[160,4096]{1,0:T(8,128)(2,1)S(1)} %collective-permute-done.5.refs_2_, bf16[512,4096]{1,0:T(8,128)(2,1)S(1)} %maximum_select_fusion), kind=kOutput, calls=%fused_computation.35 | convolution fusion | flops 671170560 | bytes 5668864 | tf_op jit(solution)/shard_map/dot_general | solution.py:73
  80.9 1.6 %fusion.19 = bf16[8,160,512]{2,1,0:T(8,128)(2,1)S(1)} fusion(bf16[8,160,512]{2,1,0:T(8,128)(2,1)S(1)} %fusion.17, bf16[160,4096]{1,0:T(8,128)(2,1)S(1)} %collective-permute-done.6.refs_5_, bf16[512,4096]{1,0:T(8,128)(2,1)S(1)} %maximum_select_fusion), kind=kOutput, calls=%fused_computation.37 | convolution fusion | flops 671170560 | bytes 5668864 | tf_op jit(solution)/shard_map/dot_general | solution.py:73
  82.5 3.6 %collective-permute-done.11 = bf16[160,512]{1,0:T(8,128)(2,1)S(1)} collective-permute-done((bf16[160,512]{1,0:T(8,128)(2,1)S(1)}, bf16[160,512]{1,0:T(8,128)(2,1)S(1)}, u32[]{:S(2)}, u32[]{:S(2)}) %collective-permute-start.11) | collective-permute-done | bytes 163872 | tf_op jit(solution)/shard_map/ppermute | solution.py:158
  86.2 2.0 %collective-permute-start.15 = (bf16[2,160,512]{2,1,0:T(8,128)(2,1)S(1)}, bf16[2,160,512]{2,1,0:T(8,128)(2,1)S(1)}, u32[]{:S(2)}, u32[]{:S(2)}) collective-permute-start(bf16[2,160,512]{2,1,0:T(8,128)(2,1)S(1)} %get-tuple-element.46), channel_id=1, source_target_pairs={{0,2},{2,4},{4,6},{6,0},{1,3},{3,5},{5,7},{7,1},{8,10},{10,12},{12... | collective-permute-start | bytes 983048 | tf_op jit(solution)/shard_map/ppermute | solution.py:58
  88.2 1.6 %fusion.21 = bf16[8,160,512]{2,1,0:T(8,128)(2,1)S(1)} fusion(bf16[8,160,512]{2,1,0:T(8,128)(2,1)S(1)} %fusion.19, bf16[160,4096]{1,0:T(8,128)(2,1)S(1)} %collective-permute-done.7.refs_7_, bf16[512,4096]{1,0:T(8,128)(2,1)S(1)} %maximum_select_fusion), kind=kOutput, calls=%fused_computation.39 | convolution fusion | flops 671170560 | bytes 5668864 | tf_op jit(solution)/shard_map/dot_general | solution.py:73
  89.8 6.1 %collective-permute-done.15 = bf16[2,160,512]{2,1,0:T(8,128)(2,1)S(1)} collective-permute-done((bf16[2,160,512]{2,1,0:T(8,128)(2,1)S(1)}, bf16[2,160,512]{2,1,0:T(8,128)(2,1)S(1)}, u32[]{:S(2)}, u32[]{:S(2)}) %collective-permute-start.15) | collective-permute-done | bytes 327712 | tf_op jit(solution)/shard_map/ppermute | solution.py:58
  96.1 4.2 %collective-permute-start.18 = (bf16[1,160,512]{2,1,0:T(8,128)(2,1)S(1)}, bf16[1,160,512]{2,1,0:T(8,128)(2,1)S(1)}, u32[]{:S(2)}, u32[]{:S(2)}) collective-permute-start(bf16[1,160,512]{2,1,0:T(8,128)(2,1)S(1)} %slice.42), channel_id=1, source_target_pairs={{0,6},{2,0},{4,2},{6,4},{1,7},{3,1},{5,3},{7,5},{8,14},{10,8},{12,... | collective-permute-start | bytes 491528 | tf_op jit(solution)/shard_map/ppermute | solution.py:58
  100.4 1.5 %fusion.23 = bf16[8,160,512]{2,1,0:T(8,128)(2,1)S(1)} fusion(bf16[8,160,512]{2,1,0:T(8,128)(2,1)S(1)} %fusion.21, bf16[160,4096]{1,0:T(8,128)(2,1)S(1)} %constant_dynamic-update-slice_fusion.4.refs_6_, bf16[512,4096]{1,0:T(8,128)(2,1)S(1)} %maximum_select_fusion), kind=kOutput, calls=%fused_computation.41 | convolution fusion | flops 671170560 | bytes 5668864 | tf_op jit(solution)/shard_map/dot_general | solution.py:73
  102.0 1.0 dynamic-slice_bitcast_fusion.2
  103.0 2.7 %collective-permute-start.14 = (bf16[2,160,512]{2,1,0:T(8,128)(2,1)}, bf16[2,160,512]{2,1,0:T(8,128)(2,1)S(1)}, u32[]{:S(2)}, u32[]{:S(2)}) collective-permute-start(bf16[2,160,512]{2,1,0:T(8,128)(2,1)} %get-tuple-element.52), channel_id=1, source_target_pairs={{0,4},{2,6},{4,0},{6,2},{1,5},{3,7},{5,1},{7,3},{8,12},{10,14},{12... | collective-permute-start | bytes 983048 | tf_op jit(solution)/shard_map/ppermute | solution.py:58
  105.7 1.2 collective-permute-start.13
  106.8 1.5 %collective-permute-start.12 = (bf16[2,160,512]{2,1,0:T(8,128)(2,1)S(1)}, bf16[2,160,512]{2,1,0:T(8,128)(2,1)}, u32[]{:S(2)}, u32[]{:S(2)}) collective-permute-start(bf16[2,160,512]{2,1,0:T(8,128)(2,1)S(1)} %get-tuple-element.51), channel_id=1, source_target_pairs={{0,2},{2,4},{4,6},{6,0},{1,3},{3,5},{5,7},{7,1},{8,10},{10,12},{12... | collective-permute-start | bytes 983048 | tf_op jit(solution)/shard_map/ppermute | solution.py:58
  108.9 0.6 copy.10
  109.6 1.1 broadcast_select_fusion.1
  110.7 7.9 %shard_map.85 = (bf16[256,2048]{1,0:T(8,128)(2,1)}, bf16[256,2048]{1,0:T(8,128)(2,1)}) custom-call(bf16[256,1280]{1,0:T(8,128)(2,1)} %get-tuple-element.48.features_ref, bf16[160,4096]{1,0:T(8,128)(2,1)} %copy-done.3, bf16[160,4096]{1,0:T(8,128)(2,1)} %copy-done.4, bf16[160,4096]{1,0:T(8,128)(2,1)} %copy-done.6, ...), custom_call_target="tpu_custom_call" | custom-call | flops 2684354560 | bytes 13238272 | tf_op jit(solution)/shard_map/pallas_call | solution.py:105
  118.6 1.3 fusion.26
  120.1 0.5 collective-permute-start.22
  120.6 2.5 %collective-permute-start.20 = (bf16[160,512]{1,0:T(8,128)(2,1)S(1)}, bf16[160,512]{1,0:T(8,128)(2,1)S(1)}, u32[]{:S(2)}, u32[]{:S(2)}) collective-permute-start(bf16[160,512]{1,0:T(8,128)(2,1)S(1)} %get-tuple-element.39), channel_id=1, source_target_pairs={{0,16},{1,0},{2,48},{3,32},{4,80},{5,64},{6,112},{7,96},{8,24},{9,... | collective-permute-start | bytes 491528 | tf_op jit(solution)/shard_map/ppermute | solution.py:182
  123.1 7.9 %collective-permute-start.19 = (bf16[160,512]{1,0:T(8,128)(2,1)S(1)}, bf16[160,512]{1,0:T(8,128)(2,1)S(1)}, u32[]{:S(2)}, u32[]{:S(2)}) collective-permute-start(bf16[160,512]{1,0:T(8,128)(2,1)S(1)} %get-tuple-element.38), channel_id=1, source_target_pairs={{0,0},{1,16},{2,32},{3,48},{4,64},{5,80},{6,96},{7,112},{8,8},{9,2... | collective-permute-start | bytes 491528 | tf_op jit(solution)/shard_map/ppermute | solution.py:181
  131.0 8.4 %shard_map.86 = (f32[256,2048]{1,0:T(8,128)}, f32[256,2048]{1,0:T(8,128)}) custom-call(bf16[256,1280]{1,0:T(8,128)(2,1)} %get-tuple-element.40.features_ref, bf16[160,4096]{1,0:T(8,128)(2,1)} %copy-done.3, bf16[160,4096]{1,0:T(8,128)(2,1)} %copy-done.4, bf16[160,4096]{1,0:T(8,128)(2,1)} %copy-done.6, bf16[160,4096]{1,0:T(8,128)(2,1)} %collective-permute-done.refs_3_, ...), custom_call_target="tpu_custom_call" | custom-call | flops 2684354560 | bytes 13238272 | tf_op jit(solution)/shard_map/pallas_call | solution.py:105
  139.4 0.7 add_convert_fusion.2
  140.1 3.0 %add_convert_fusion.1 = bf16[256,2048]{1,0:T(8,128)(2,1)} fusion(f32[256,2048]{1,0:T(8,128)} %get-tuple-element.41, bf16[256,2048]{1,0:T(8,128)(2,1)S(1)} %collective-permute-done.21), kind=kLoop, calls=%fused_computation.2 | loop fusion | flops 1572864 | bytes 4194304 | tf_op jit(solution)/shard_map/convert_element_type | solution.py:184
  143.1 1.3 add_convert_fusion
  (71 shorter events, 1.7 us)
Async XLA Ops:
  0.6 11.5 %collective-permute-start.3 = (bf16[256,2048]{1,0:T(8,128)(2,1)}, bf16[256,2048]{1,0:T(8,128)(2,1)}, u32[]{:S(2)}, u32[]{:S(2)}) collective-permute-start(bf16[256,2048]{1,0:T(8,128)(2,1)} %param.10), channel_id=1, source_target_pairs={{0,8},{8,0},{1,9},{9,1},{2,10},{10,2},{3,11},{11,3},{4,12},{12,4},... | collective-permute-start | bytes 3145736 | tf_op jit(solution)/shard_map/ppermute | solution.py:54
  0.7 12.8 %collective-permute-start.4 = (bf16[256,2048]{1,0:T(8,128)(2,1)}, bf16[256,2048]{1,0:T(8,128)(2,1)}, u32[]{:S(2)}, u32[]{:S(2)}) collective-permute-start(bf16[256,2048]{1,0:T(8,128)(2,1)} %param.11), channel_id=1, source_target_pairs={{0,8},{8,0},{1,9},{9,1},{2,10},{10,2},{3,11},{11,3},{4,12},{12,4},... | collective-permute-start | bytes 3145736 | tf_op jit(solution)/shard_map/ppermute | solution.py:54
  3.4 0.8 copy-start.9
  3.4 5.4 %copy-start.12 = (bf16[256,2048]{1,0:T(8,128)(2,1)S(1)}, bf16[256,2048]{1,0:T(8,128)(2,1)}, u32[]{:S(2)}) copy-start(bf16[256,2048]{1,0:T(8,128)(2,1)} %param.10) | copy-start | bytes 3145732
  4.2 7.9 %copy-start.3 = (bf16[160,4096]{1,0:T(8,128)(2,1)}, bf16[160,4096]{1,0:T(8,128)(2,1)S(1)}, u32[]{:S(2)}) copy-start(bf16[160,4096]{1,0:T(8,128)(2,1)S(1)} %pad_maximum_fusion.refs_0_) | copy-start | bytes 3932164
  4.2 32.1 %collective-permute-start = (bf16[160,4096]{1,0:T(8,128)(2,1)S(1)}, bf16[160,4096]{1,0:T(8,128)(2,1)}, u32[]{:S(2)}, u32[]{:S(2)}) collective-permute-start(bf16[160,4096]{1,0:T(8,128)(2,1)S(1)} %pad_maximum_fusion.refs_0_), channel_id=1, source_target_pairs={{0,16},{16,32},{32,48},{48,0},{1,17},{17,33},{33,49},{49,1},{2,18}... | collective-permute-start | bytes 3932168 | tf_op jit(solution)/shard_map/ppermute | solution.py:42
  5.7 30.6 %collective-permute-start.1 = (bf16[160,4096]{1,0:T(8,128)(2,1)S(1)}, bf16[160,4096]{1,0:T(8,128)(2,1)S(1)}, u32[]{:S(2)}, u32[]{:S(2)}) collective-permute-start(bf16[160,4096]{1,0:T(8,128)(2,1)S(1)} %pad_maximum_fusion.refs_0_), channel_id=1, source_target_pairs={{0,48},{16,0},{32,16},{48,32},{1,49},{17,1},{33,17},{49,33},{2,50}... | collective-permute-start | bytes 3932168 | tf_op jit(solution)/shard_map/ppermute | solution.py:46
  7.5 30.3 %collective-permute-start.2 = (bf16[160,4096]{1,0:T(8,128)(2,1)S(1)}, bf16[160,4096]{1,0:T(8,128)(2,1)}, u32[]{:S(2)}, u32[]{:S(2)}) collective-permute-start(bf16[160,4096]{1,0:T(8,128)(2,1)S(1)} %pad_maximum_fusion.refs_0_), channel_id=1, source_target_pairs={{0,64},{64,0},{1,65},{65,1},{2,66},{66,2},{3,67},{67,3},{4,68},{68... | collective-permute-start | bytes 3932168 | tf_op jit(solution)/shard_map/ppermute | solution.py:50
  13.5 1.9 %copy-start.8 = (bf16[256,4096]{1,0:T(8,128)(2,1)S(1)}, bf16[256,4096]{1,0:T(8,128)(2,1)}, u32[]{:S(2)}) copy-start(bf16[256,4096]{1,0:T(8,128)(2,1)} %constant_dynamic-update-slice_fusion) | copy-start | bytes 6291460
  15.4 26.9 %copy-start.10 = (bf16[160,2048]{1,0:T(8,128)(2,1)S(1)}, bf16[160,2048]{1,0:T(8,128)(2,1)}, u32[]{:S(2)}) copy-start(bf16[160,2048]{1,0:T(8,128)(2,1)} %copy-done.9) | copy-start | bytes 1966084
  17.6 26.3 %copy-start.13 = (bf16[160,512]{1,0:T(8,128)(2,1)S(1)}, bf16[160,512]{1,0:T(8,128)(2,1)}, u32[]{:S(2)}) copy-start(bf16[160,512]{1,0:T(8,128)(2,1)} %param.6) | copy-start | bytes 491524
  36.3 1.7 %copy-start.4 = (bf16[160,4096]{1,0:T(8,128)(2,1)}, bf16[160,4096]{1,0:T(8,128)(2,1)S(1)}, u32[]{:S(2)}) copy-start(bf16[160,4096]{1,0:T(8,128)(2,1)S(1)} %collective-permute-done.1.refs_1_) | copy-start | bytes 3932164
  37.8 30.7 %collective-permute-start.5 = (bf16[160,4096]{1,0:T(8,128)(2,1)}, bf16[160,4096]{1,0:T(8,128)(2,1)S(1)}, u32[]{:S(2)}, u32[]{:S(2)}) collective-permute-start(bf16[160,4096]{1,0:T(8,128)(2,1)} %collective-permute-done.refs_3_), channel_id=1, source_target_pairs={{0,16},{16,32},{32,48},{48,0},{1,17},{17,33},{33,49},{49,1},{2,18}... | collective-permute-start | bytes 3932168 | tf_op jit(solution)/shard_map/ppermute | solution.py:42
  38.1 37.3 %collective-permute-start.7 = (bf16[160,4096]{1,0:T(8,128)(2,1)}, bf16[160,4096]{1,0:T(8,128)(2,1)S(1)}, u32[]{:S(2)}, u32[]{:S(2)}) collective-permute-start(bf16[160,4096]{1,0:T(8,128)(2,1)} %collective-permute-done.refs_3_), channel_id=1, source_target_pairs={{0,64},{64,0},{1,65},{65,1},{2,66},{66,2},{3,67},{67,3},{4,68},{68... | collective-permute-start | bytes 3932168 | tf_op jit(solution)/shard_map/ppermute | solution.py:50
  39.4 36.0 %collective-permute-start.6 = (bf16[160,4096]{1,0:T(8,128)(2,1)}, bf16[160,4096]{1,0:T(8,128)(2,1)S(1)}, u32[]{:S(2)}, u32[]{:S(2)}) collective-permute-start(bf16[160,4096]{1,0:T(8,128)(2,1)} %collective-permute-done.2.refs_4_), channel_id=1, source_target_pairs={{0,48},{16,0},{32,16},{48,32},{1,49},{17,1},{33,17},{49,33},{2,50}... | collective-permute-start | bytes 3932168 | tf_op jit(solution)/shard_map/ppermute | solution.py:46
  43.9 2.2 %copy-start.5 = (bf16[160,4096]{1,0:T(8,128)(2,1)S(1)}, bf16[160,4096]{1,0:T(8,128)(2,1)}, u32[]{:S(2)}) copy-start(bf16[160,4096]{1,0:T(8,128)(2,1)} %copy-done.4) | copy-start | bytes 3932164
  43.9 35.3 %collective-permute-start.10 = (bf16[160,512]{1,0:T(8,128)(2,1)S(1)}, bf16[160,512]{1,0:T(8,128)(2,1)S(1)}, u32[]{:S(2)}, u32[]{:S(2)}) collective-permute-start(bf16[160,512]{1,0:T(8,128)(2,1)S(1)} %copy-done.13), channel_id=1, source_target_pairs={{0,0},{16,1},{32,2},{48,3},{64,4},{80,5},{96,6},{112,7},{8,8},{24,... | collective-permute-start | bytes 491528 | tf_op jit(solution)/shard_map/ppermute | solution.py:149
  68.5 10.7 %copy-start.6 = (bf16[160,4096]{1,0:T(8,128)(2,1)}, bf16[160,4096]{1,0:T(8,128)(2,1)S(1)}, u32[]{:S(2)}) copy-start(bf16[160,4096]{1,0:T(8,128)(2,1)S(1)} %collective-permute-done.5.refs_2_) | copy-start | bytes 3932164
  75.4 5.5 %copy-start.1 = (bf16[160,4096]{1,0:T(8,128)(2,1)}, bf16[160,4096]{1,0:T(8,128)(2,1)S(1)}, u32[]{:S(2)}) copy-start(bf16[160,4096]{1,0:T(8,128)(2,1)S(1)} %collective-permute-done.6.refs_5_) | copy-start | bytes 3932164
  75.4 12.8 %copy-start = (bf16[160,4096]{1,0:T(8,128)(2,1)}, bf16[160,4096]{1,0:T(8,128)(2,1)S(1)}, u32[]{:S(2)}) copy-start(bf16[160,4096]{1,0:T(8,128)(2,1)S(1)} %collective-permute-done.7.refs_7_) | copy-start | bytes 3932164
  75.4 24.9 %collective-permute-start.8 = (bf16[80,4096]{1,0:T(8,128)(2,1)S(1)}, bf16[80,4096]{1,0:T(8,128)(2,1)S(1)}, u32[]{:S(2)}, u32[]{:S(2)}) collective-permute-start(bf16[80,4096]{1,0:T(8,128)(2,1)S(1)} %slice.33), channel_id=1, source_target_pairs={{0,16},{16,32},{32,48},{48,0},{1,17},{17,33},{33,49},{49,1},{2,18}... | collective-permute-start | bytes 1966088 | tf_op jit(solution)/shard_map/ppermute | solution.py:42
  75.6 24.8 %collective-permute-start.9 = (bf16[80,4096]{1,0:T(8,128)(2,1)S(1)}, bf16[80,4096]{1,0:T(8,128)(2,1)S(1)}, u32[]{:S(2)}, u32[]{:S(2)}) collective-permute-start(bf16[80,4096]{1,0:T(8,128)(2,1)S(1)} %slice.34), channel_id=1, source_target_pairs={{0,48},{16,0},{32,16},{48,32},{1,49},{17,1},{33,17},{49,33},{2,50}... | collective-permute-start | bytes 1966088 | tf_op jit(solution)/shard_map/ppermute | solution.py:46
  79.2 6.8 %collective-permute-start.11 = (bf16[160,512]{1,0:T(8,128)(2,1)S(1)}, bf16[160,512]{1,0:T(8,128)(2,1)S(1)}, u32[]{:S(2)}, u32[]{:S(2)}) collective-permute-start(bf16[160,512]{1,0:T(8,128)(2,1)S(1)} %collective-permute-done.10), channel_id=1, source_target_pairs={{0,1},{1,0},{2,3},{3,2},{4,5},{5,4},{6,7},{7,6},{8,9},{9,8},{10,11... | collective-permute-start | bytes 491528 | tf_op jit(solution)/shard_map/ppermute | solution.py:158
  86.1 9.9 %collective-permute-start.16 = (bf16[2,160,512]{2,1,0:T(8,128)(2,1)S(1)}, bf16[2,160,512]{2,1,0:T(8,128)(2,1)S(1)}, u32[]{:S(2)}, u32[]{:S(2)}) collective-permute-start(bf16[2,160,512]{2,1,0:T(8,128)(2,1)S(1)} %get-tuple-element.46), channel_id=1, source_target_pairs={{0,6},{2,0},{4,2},{6,4},{1,7},{3,1},{5,3},{7,5},{8,14},{10,8},{12,... | collective-permute-start | bytes 983048 | tf_op jit(solution)/shard_map/ppermute | solution.py:58
  86.2 9.8 %collective-permute-start.15 = (bf16[2,160,512]{2,1,0:T(8,128)(2,1)S(1)}, bf16[2,160,512]{2,1,0:T(8,128)(2,1)S(1)}, u32[]{:S(2)}, u32[]{:S(2)}) collective-permute-start(bf16[2,160,512]{2,1,0:T(8,128)(2,1)S(1)} %get-tuple-element.46), channel_id=1, source_target_pairs={{0,2},{2,4},{4,6},{6,0},{1,3},{3,5},{5,7},{7,1},{8,10},{10,12},{12... | collective-permute-start | bytes 983048 | tf_op jit(solution)/shard_map/ppermute | solution.py:58
  96.0 12.3 %collective-permute-start.17 = (bf16[1,160,512]{2,1,0:T(8,128)(2,1)S(1)}, bf16[1,160,512]{2,1,0:T(8,128)(2,1)S(1)}, u32[]{:S(2)}, u32[]{:S(2)}) collective-permute-start(bf16[1,160,512]{2,1,0:T(8,128)(2,1)S(1)} %slice.41), channel_id=1, source_target_pairs={{0,2},{2,4},{4,6},{6,0},{1,3},{3,5},{5,7},{7,1},{8,10},{10,12},{12... | collective-permute-start | bytes 491528 | tf_op jit(solution)/shard_map/ppermute | solution.py:58
  96.1 12.2 %collective-permute-start.18 = (bf16[1,160,512]{2,1,0:T(8,128)(2,1)S(1)}, bf16[1,160,512]{2,1,0:T(8,128)(2,1)S(1)}, u32[]{:S(2)}, u32[]{:S(2)}) collective-permute-start(bf16[1,160,512]{2,1,0:T(8,128)(2,1)S(1)} %slice.42), channel_id=1, source_target_pairs={{0,6},{2,0},{4,2},{6,4},{1,7},{3,1},{5,3},{7,5},{8,14},{10,8},{12,... | collective-permute-start | bytes 491528 | tf_op jit(solution)/shard_map/ppermute | solution.py:58
  100.4 1.6 %copy-start.2 = (bf16[160,4096]{1,0:T(8,128)(2,1)}, bf16[160,4096]{1,0:T(8,128)(2,1)S(1)}, u32[]{:S(2)}) copy-start(bf16[160,4096]{1,0:T(8,128)(2,1)S(1)} %constant_dynamic-update-slice_fusion.4.refs_6_) | copy-start | bytes 3932164
  102.0 6.3 %copy-start.7 = (bf16[8,160,512]{2,1,0:T(8,128)(2,1)}, bf16[8,160,512]{2,1,0:T(8,128)(2,1)S(1)}, u32[]{:S(2)}) copy-start(bf16[8,160,512]{2,1,0:T(8,128)(2,1)S(1)} %fusion.23) | copy-start | bytes 3932164
  103.0 15.6 %collective-permute-start.14 = (bf16[2,160,512]{2,1,0:T(8,128)(2,1)}, bf16[2,160,512]{2,1,0:T(8,128)(2,1)S(1)}, u32[]{:S(2)}, u32[]{:S(2)}) collective-permute-start(bf16[2,160,512]{2,1,0:T(8,128)(2,1)} %get-tuple-element.52), channel_id=1, source_target_pairs={{0,4},{2,6},{4,0},{6,2},{1,5},{3,7},{5,1},{7,3},{8,12},{10,14},{12... | collective-permute-start | bytes 983048 | tf_op jit(solution)/shard_map/ppermute | solution.py:58
  105.7 12.9 %collective-permute-start.13 = (bf16[2,160,512]{2,1,0:T(8,128)(2,1)}, bf16[2,160,512]{2,1,0:T(8,128)(2,1)}, u32[]{:S(2)}, u32[]{:S(2)}) collective-permute-start(bf16[2,160,512]{2,1,0:T(8,128)(2,1)} %get-tuple-element.53), channel_id=1, source_target_pairs={{0,6},{2,0},{4,2},{6,4},{1,7},{3,1},{5,3},{7,5},{8,14},{10,8},{12,... | collective-permute-start | bytes 983048 | tf_op jit(solution)/shard_map/ppermute | solution.py:58
  106.8 11.8 %collective-permute-start.12 = (bf16[2,160,512]{2,1,0:T(8,128)(2,1)S(1)}, bf16[2,160,512]{2,1,0:T(8,128)(2,1)}, u32[]{:S(2)}, u32[]{:S(2)}) collective-permute-start(bf16[2,160,512]{2,1,0:T(8,128)(2,1)S(1)} %get-tuple-element.51), channel_id=1, source_target_pairs={{0,2},{2,4},{4,6},{6,0},{1,3},{3,5},{5,7},{7,1},{8,10},{10,12},{12... | collective-permute-start | bytes 983048 | tf_op jit(solution)/shard_map/ppermute | solution.py:58
  120.0 20.1 %collective-permute-start.21 = (bf16[256,2048]{1,0:T(8,128)(2,1)}, bf16[256,2048]{1,0:T(8,128)(2,1)S(1)}, u32[]{:S(2)}, u32[]{:S(2)}) collective-permute-start(bf16[256,2048]{1,0:T(8,128)(2,1)} %get-tuple-element.42), channel_id=1, source_target_pairs={{0,8},{8,0},{1,9},{9,1},{2,10},{10,2},{3,11},{11,3},{4,12},{12,4},... | collective-permute-start | bytes 3145736 | tf_op jit(solution)/shard_map/ppermute | solution.py:54
  120.1 23.0 %collective-permute-start.22 = (bf16[256,2048]{1,0:T(8,128)(2,1)}, bf16[256,2048]{1,0:T(8,128)(2,1)S(1)}, u32[]{:S(2)}, u32[]{:S(2)}) collective-permute-start(bf16[256,2048]{1,0:T(8,128)(2,1)} %get-tuple-element.44), channel_id=1, source_target_pairs={{0,8},{8,0},{1,9},{9,1},{2,10},{10,2},{3,11},{11,3},{4,12},{12,4},... | collective-permute-start | bytes 3145736 | tf_op jit(solution)/shard_map/ppermute | solution.py:54
  120.6 18.8 %collective-permute-start.20 = (bf16[160,512]{1,0:T(8,128)(2,1)S(1)}, bf16[160,512]{1,0:T(8,128)(2,1)S(1)}, u32[]{:S(2)}, u32[]{:S(2)}) collective-permute-start(bf16[160,512]{1,0:T(8,128)(2,1)S(1)} %get-tuple-element.39), channel_id=1, source_target_pairs={{0,16},{1,0},{2,48},{3,32},{4,80},{5,64},{6,112},{7,96},{8,24},{9,... | collective-permute-start | bytes 491528 | tf_op jit(solution)/shard_map/ppermute | solution.py:182
  123.1 16.3 %collective-permute-start.19 = (bf16[160,512]{1,0:T(8,128)(2,1)S(1)}, bf16[160,512]{1,0:T(8,128)(2,1)S(1)}, u32[]{:S(2)}, u32[]{:S(2)}) collective-permute-start(bf16[160,512]{1,0:T(8,128)(2,1)S(1)} %get-tuple-element.38), channel_id=1, source_target_pairs={{0,0},{1,16},{2,32},{3,48},{4,64},{5,80},{6,96},{7,112},{8,8},{9,2... | collective-permute-start | bytes 491528 | tf_op jit(solution)/shard_map/ppermute | solution.py:181
  140.1 3.0 %copy-start.11 = (f32[256,2048]{1,0:T(8,128)S(1)}, f32[256,2048]{1,0:T(8,128)}, u32[]{:S(2)}) copy-start(f32[256,2048]{1,0:T(8,128)} %get-tuple-element.43) | copy-start | bytes 6291460

commit v4 on v3

--- a/solution.py
+++ b/solution.py
@@ -82,41 +82,45 @@
     return jnp.dot(features_ref[...], rows_ref[...], preferred_element_type=F32)
 
 
-def store_halves(blocks, total, low_ref, high_ref):
+def sum_kernel(blocks, features_ref, *refs):
+    *pieces, sent_gate_ref, sent_up_ref, kept_gate_ref, kept_up_ref, rows_ref = refs
+    total = stacked_term(features_ref, pieces, rows_ref)
+    count = total.shape[0] // 2
+
     @pl.when(pl.program_id(0) < blocks // 2)
     def _():
-        low_ref[...] = total.astype(low_ref.dtype)
+        sent_gate_ref[...] = total[:count].astype(BF16)
+        kept_gate_ref[...] = total[count:]
 
     @pl.when(pl.program_id(0) >= blocks // 2)
     def _():
-        high_ref[...] = total.astype(high_ref.dtype)
-
-
-def sum_kernel(blocks, features_ref, *refs):
-    *pieces, gate_ref, up_ref, rows_ref = refs
-    store_halves(blocks, stacked_term(features_ref, pieces, rows_ref), gate_ref, up_ref)
-
-
-def weight_sum(features, pieces, dtype):
-    count, deep = features.shape
+        sent_up_ref[...] = total[:count].astype(BF16)
+        kept_up_ref[...] = total[count:]
+
+
+def weight_sums(features, pieces):
+    double, deep = features.shape
+    count = double // 2
     tall, width = pieces[0].shape
     blocks = width // BLOCK
     half = blocks // 2
+    halves = [
+        pl.BlockSpec((count, BLOCK), lambda j: (0, jnp.minimum(j, half - 1))),
+        pl.BlockSpec((count, BLOCK), lambda j: (0, jnp.maximum(j - half, 0))),
+    ]
     return pl.pallas_call(
         functools.partial(sum_kernel, blocks),
-        out_shape=[jax.ShapeDtypeStruct((count, width // 2), dtype)] * 2,
+        out_shape=[jax.ShapeDtypeStruct((count, width // 2), BF16)] * 2
+        + [jax.ShapeDtypeStruct((count, width // 2), F32)] * 2,
         grid=(blocks,),
-        in_specs=[pl.BlockSpec((count, deep), lambda j: (0, 0))]
+        in_specs=[pl.BlockSpec((double, deep), lambda j: (0, 0))]
         + [pl.BlockSpec((tall, BLOCK), lambda j: (0, j))] * len(pieces),
-        out_specs=[
-            pl.BlockSpec((count, BLOCK), lambda j: (0, jnp.minimum(j, half - 1))),
-            pl.BlockSpec((count, BLOCK), lambda j: (0, jnp.maximum(j - half, 0))),
-        ],
+        out_specs=halves + halves,
         scratch_shapes=[pltpu.VMEM((deep, BLOCK), BF16)],
         compiler_params=pltpu.CompilerParams(vmem_limit_bytes=60 * 2**20),
         cost_estimate=pl.CostEstimate(
-            flops=2 * count * deep * width,
-            bytes_accessed=2 * (deep * width + count * (deep + width)),
+            flops=2 * double * deep * width,
+            bytes_accessed=2 * deep * (width + double) + 6 * count * width,
             transcendentals=0,
         ),
     )(features, *pieces)
@@ -135,6 +139,7 @@
     d_gate = (upstream * up * sigma * (1.0 + gated * (1.0 - sigma))).astype(BF16)
     own = jnp.concatenate([d_gate, d_up], axis=1)
 
+    own, tokens = tied((own, tokens))
     la, ra, ya = right(own), left(own), across(own)
     held = jnp.concatenate([gate_weight, up_weight], axis=1)
     other = jnp.concatenate([other_gate, other_up], axis=1)
@@ -143,10 +148,11 @@
         jnp.concatenate([held, other], axis=0),
         jnp.concatenate([other, held], axis=0),
     )
-    la, ra, ya, weights, tokens = tied((la, ra, ya, weights, tokens))
+    mine = lax.ppermute(tokens, ALL, TO_WORKER)
+    la, ra, ya, weights = tied((la, ra, ya, weights))
 
     oa, yra, yla = right(la), left(ya), across(la)
-    mine = lax.ppermute(tokens, ALL, TO_WORKER)
+    _, mine = tied((la, mine))
     partial = jnp.zeros((8,) + tokens.shape, BF16)
     for place, v in ((0, own), (1, ra), (3, la), (4, ya)):
         partial = lax.dynamic_update_index_in_dim(partial, input_term(v, weights), place, 0)
@@ -168,20 +174,21 @@
     block = [lax.dynamic_index_in_dim(by_z, (z + s) % 4, 0, keepdims=False) for s in range(4)]
     came_z = [along_z(block[s], s) for s in (1, 3, 2)]
     flipped = in_order(ring, z).reshape(8 * tall, -1).T
-    send = jnp.where(core == 0, flipped[count:], flipped[:count])
-    keep = jnp.where(core == 0, flipped[:count], flipped[count:])
+    turned = jnp.where(
+        core == 0, jnp.concatenate([flipped[count:], flipped[:count]], axis=0), flipped
+    )
     pieces = (own, ra, oa, la, ya, yra, yoa, yla)
-    sent = weight_sum(send, pieces, BF16)
+    *sent, kept_gate, kept_up = weight_sums(turned, pieces)
     sums = block[0].astype(F32)
     for v in came_z:
         sums = sums + v.astype(F32)
     same, cross = jnp.where(yh == 0, sums, sums[::-1]).astype(BF16)
-    same, cross, sent, keep = tied((same, cross, sent, keep))
+    same, cross, sent = tied((same, cross, sent))
     came = tuple(sibling(v) for v in sent)
     same = lax.ppermute(same, ALL, to_owner(0))
     cross = lax.ppermute(cross, ALL, to_owner(1))
-    kept = weight_sum(keep, pieces, F32)
-    grad_gate, grad_up = ((k + v.astype(F32)).astype(BF16) for k, v in zip(kept, came))
+    grad_gate = (kept_gate + came[0].astype(F32)).astype(BF16)
+    grad_up = (kept_up + came[1].astype(F32)).astype(BF16)
     d_tokens = (same.astype(F32) + cross.astype(F32)).astype(BF16)
     return d_tokens, grad_gate, grad_up
 

time: 147 us -> 141 us (0.959); the launches traced: 144 us -> 141 us
  Pallas kernels: 16.3 us -> 11.5 us
  starting transfers between devices: 38 us -> 42 us
  local copies, waits for them, and re-layouts: 9.54 us -> 7.13 us
  other arithmetic: 12.4 us -> 10.7 us
    ppermute x3, waiting for transfers between devices: 33.7 us -> 0.35 us  [right(): return lax.ppermute(v, 'x', AHEAD)]
    ppermute x2, waiting for transfers between devices: 1.46 us -> 16.1 us  [across(): return lax.ppermute(v, 'yl', SWAP)]
    ppermute x3, waiting for transfers between devices: 6.86 us -> 20.9 us  [left(): return lax.ppermute(v, 'x', BACK)]
    ppermute x1, waiting for transfers between devices: 0.01 us -> 5.09 us  [local(): cross = lax.ppermute(cross, ALL, to_owner(1))]
    pallas_call x2 -> x1, Pallas kernels: 16.3 us -> 11.5 us  [weight_sums(): pl.pallas_call(functools.partial(sum_kernel, blocks), out_shape=[jax.Shap...]
    ppermute x1, waiting for transfers between devices: 0.01 us -> 3.65 us  [local(): same = lax.ppermute(same, ALL, to_owner(0))]
    ppermute x1, waiting for transfers between devices: 3.6 us -> 0.01 us  [local(): pair = lax.ppermute(mine, 'yh', SWAP)]
    ppermute x1, starting transfers between devices: 2.05 us -> 4.69 us  [local(): mine = lax.ppermute(tokens, ALL, TO_WORKER)]
  transfers between devices with their start and end apart: 23 -> 23, of which waited for: 6 -> 9; matrix products, arithmetic and copies ran while one was open for 23% -> 22% of each run, Pallas kernels for 11% -> 8%
where the time goes in v4:
time: 141 us
  waiting for transfers between devices  51.9 us (37%)
  starting transfers between devices  42 us (30%)
  matrix products  16.5 us (12%)
  Pallas kernels  11.5 us (8%)
  other arithmetic  10.7 us (8%)
  local copies, waits for them, and re-layouts  7.13 us (5%)
    ppermute x3, waiting for transfers between devices, left(): return lax.ppermute(v, 'x', BACK)  20.9 us
    dot_general x8, matrix products, input_term(): lax.dot_general(rows, weights, (((1,), (1,)), ((), ())), preferred_elemen...  16.5 us
    ppermute x2, waiting for transfers between devices, across(): return lax.ppermute(v, 'yl', SWAP)  16.1 us
    ppermute x7, starting transfers between devices, along_z(): return lax.ppermute(v, 'z', [(i, (i + step) % 4) for i in range(4)])  13.5 us
    pallas_call x1, Pallas kernels, weight_sums(): pl.pallas_call(functools.partial(sum_kernel, blocks), out_shape=[jax.Shap...  11.5 us
    ppermute x3, starting transfers between devices, left(): return lax.ppermute(v, 'x', BACK)  7.46 us
    ppermute x1, starting transfers between devices, local(): same = lax.ppermute(same, ALL, to_owner(0))  6.53 us
    ppermute x7, waiting for transfers between devices, along_z(): return lax.ppermute(v, 'z', [(i, (i + step) % 4) for i in range(4)])  5.09 us
  transfers between devices with their start and end apart: 23, of which 9 were waited for; matrix products, arithmetic and copies ran while one was open for 22% of the time, Pallas kernels for 8%

profile of v4, /device:TPU:48, one launch (start us, length us, event | category | flops | bytes accessed | tf_op | source)
XLA Modules:
  0.0 141.0 jit_solution(14860667673848416917)
XLA Ops:
  0.7 0.5 collective-permute-start.4
  1.2 2.2 %fusion.2 = (bf16[160,2048]{1,0:T(8,128)(2,1)S(1)}, bf16[160,2048]{1,0:T(8,128)(2,1)S(1)}) fusion(bf16[160,2048]{1,0:T(8,128)(2,1)} %param.9, bf16[160,2048]{1,0:T(8,128)(2,1)} %param.7, bf16[160,2048]{1,0:T(8,128)(2,1)} %param.8), kind=kLoop, calls=%fused_computation.9 | loop fusion | flops 5242880 | bytes 3276800 | tf_op jit(solution)/shard_map/convert_element_type | solution.py:139
  3.6 1.4 collective-permute-start.2
  4.9 2.8 %collective-permute-start.1 = (bf16[160,4096]{1,0:T(8,128)(2,1)S(1)}, bf16[160,4096]{1,0:T(8,128)(2,1)}, u32[]{:S(2)}, u32[]{:S(2)}) collective-permute-start(bf16[160,4096]{1,0:T(8,128)(2,1)S(1)} %pad_maximum_fusion.refs_0_), channel_id=1, source_target_pairs={{0,48},{16,0},{32,16},{48,32},{1,49},{17,1},{33,17},{49,33},{2,50}... | collective-permute-start | bytes 3932168 | tf_op jit(solution)/shard_map/ppermute | solution.py:46
  7.9 1.3 constant_dynamic-update-slice_fusion
  9.2 4.7 %collective-permute-start.10 = (bf16[160,512]{1,0:T(8,128)(2,1)S(1)}, bf16[160,512]{1,0:T(8,128)(2,1)S(1)}, u32[]{:S(2)}, u32[]{:S(2)}) collective-permute-start(bf16[160,512]{1,0:T(8,128)(2,1)S(1)} %copy-done.10), channel_id=1, source_target_pairs={{0,0},{16,1},{32,2},{48,3},{64,4},{80,5},{96,6},{112,7},{8,8},{24,... | collective-permute-start | bytes 491528 | tf_op jit(solution)/shard_map/ppermute | solution.py:151
  13.9 1.3 constant_dynamic-update-slice_fusion.3
  15.3 1.3 constant_dynamic-update-slice_fusion.2
  16.6 1.8 %maximum_select_fusion = bf16[512,4096]{1,0:T(8,128)(2,1)S(1)} fusion(bf16[256,4096]{1,0:T(8,128)(2,1)S(1)} %constant_dynamic-update-slice_fusion.2, bf16[256,4096]{1,0:T(8,128)(2,1)S(1)} %constant_dynamic-update-slice_fusion, pred[]{:T(512)S(6)} %eq.20), kind=kLoop, calls=%fused_computation | loop fusion | flops 18874368 | bytes 8388609 | tf_op jit(solution)/shard_map/jit(_where)/select_n | solution.py:146
  18.4 16.1 %collective-permute-done.2.refs_4_ = bf16[160,4096]{1,0:T(8,128)(2,1)} collective-permute-done((bf16[160,4096]{1,0:T(8,128)(2,1)S(1)}, bf16[160,4096]{1,0:T(8,128)(2,1)}, u32[]{:S(2)}, u32[]{:S(2)}) %collective-permute-start.2) | collective-permute-done | bytes 1310752 | tf_op jit(solution)/shard_map/ppermute | solution.py:50
  34.5 5.9 %collective-permute-done.1.refs_1_ = bf16[160,4096]{1,0:T(8,128)(2,1)} collective-permute-done((bf16[160,4096]{1,0:T(8,128)(2,1)S(1)}, bf16[160,4096]{1,0:T(8,128)(2,1)}, u32[]{:S(2)}, u32[]{:S(2)}) %collective-permute-start.1) | collective-permute-done | bytes 1310752 | tf_op jit(solution)/shard_map/ppermute | solution.py:46
  40.4 0.7 collective-permute-start.7
  41.1 3.8 %collective-permute-start.6 = (bf16[160,4096]{1,0:T(8,128)(2,1)}, bf16[160,4096]{1,0:T(8,128)(2,1)S(1)}, u32[]{:S(2)}, u32[]{:S(2)}) collective-permute-start(bf16[160,4096]{1,0:T(8,128)(2,1)} %collective-permute-done.2.refs_4_), channel_id=1, source_target_pairs={{0,48},{16,0},{32,16},{48,32},{1,49},{17,1},{33,17},{49,33},{2,50}... | collective-permute-start | bytes 3932168 | tf_op jit(solution)/shard_map/ppermute | solution.py:46
  44.9 1.6 %fusion.9 = bf16[1,160,512]{2,1,0:T(8,128)(2,1)S(1)} fusion(bf16[160,4096]{1,0:T(8,128)(2,1)S(1)} %pad_maximum_fusion.refs_0_, bf16[512,4096]{1,0:T(8,128)(2,1)S(1)} %maximum_select_fusion), kind=kOutput, calls=%fused_computation.28 | convolution fusion | flops 671170560 | bytes 5668864 | tf_op jit(solution)/shard_map/dot_general | solution.py:73
  46.5 0.8 collective-permute-done.10
  47.5 2.9 %fusion.11 = bf16[8,160,512]{2,1,0:T(8,128)(2,1)S(1)} fusion(bf16[8,160,512]{2,1,0:T(8,128)(2,1)S(1)} %dynamic_update_slice.25, bf16[160,4096]{1,0:T(8,128)(2,1)} %collective-permute-done.1.refs_1_, bf16[512,4096]{1,0:T(8,128)(2,1)S(1)} %maximum_select_fusion), kind=kOutput, calls=%fused_computation.30 | convolution fusion | flops 671170560 | bytes 5668864 | tf_op jit(solution)/shard_map/dot_general | solution.py:73
  50.4 2.9 %fusion.13 = bf16[8,160,512]{2,1,0:T(8,128)(2,1)S(1)} fusion(bf16[8,160,512]{2,1,0:T(8,128)(2,1)S(1)} %fusion.11, bf16[160,4096]{1,0:T(8,128)(2,1)} %collective-permute-done.refs_3_, bf16[512,4096]{1,0:T(8,128)(2,1)S(1)} %maximum_select_fusion), kind=kOutput, calls=%fused_computation.32 | convolution fusion | flops 671170560 | bytes 5668864 | tf_op jit(solution)/shard_map/dot_general | solution.py:73
  53.3 2.9 %fusion.15 = bf16[8,160,512]{2,1,0:T(8,128)(2,1)S(1)} fusion(bf16[8,160,512]{2,1,0:T(8,128)(2,1)S(1)} %fusion.13, bf16[160,4096]{1,0:T(8,128)(2,1)} %collective-permute-done.2.refs_4_, bf16[512,4096]{1,0:T(8,128)(2,1)S(1)} %maximum_select_fusion), kind=kOutput, calls=%fused_computation.34 | convolution fusion | flops 671170560 | bytes 5668864 | tf_op jit(solution)/shard_map/dot_general | solution.py:73
  56.2 14.7 %collective-permute-done.6.refs_5_ = bf16[160,4096]{1,0:T(8,128)(2,1)S(1)} collective-permute-done((bf16[160,4096]{1,0:T(8,128)(2,1)}, bf16[160,4096]{1,0:T(8,128)(2,1)S(1)}, u32[]{:S(2)}, u32[]{:S(2)}) %collective-permute-start.6) | collective-permute-done | bytes 1310752 | tf_op jit(solution)/shard_map/ppermute | solution.py:46
  70.9 0.3 collective-permute-done.5.refs_2_
  71.4 2.9 %collective-permute-start.8 = (bf16[80,4096]{1,0:T(8,128)(2,1)S(1)}, bf16[80,4096]{1,0:T(8,128)(2,1)S(1)}, u32[]{:S(2)}, u32[]{:S(2)}) collective-permute-start(bf16[80,4096]{1,0:T(8,128)(2,1)S(1)} %slice.31), channel_id=1, source_target_pairs={{0,16},{16,32},{32,48},{48,0},{1,17},{17,33},{33,49},{49,1},{2,18}... | collective-permute-start | bytes 1966088 | tf_op jit(solution)/shard_map/ppermute | solution.py:42
  74.3 1.5 %fusion.17 = bf16[8,160,512]{2,1,0:T(8,128)(2,1)S(1)} fusion(bf16[8,160,512]{2,1,0:T(8,128)(2,1)S(1)} %fusion.15, bf16[160,4096]{1,0:T(8,128)(2,1)S(1)} %collective-permute-done.5.refs_2_, bf16[512,4096]{1,0:T(8,128)(2,1)S(1)} %maximum_select_fusion), kind=kOutput, calls=%fused_computation.36 | convolution fusion | flops 671170560 | bytes 5668864 | tf_op jit(solution)/shard_map/dot_general | solution.py:73
  75.8 1.5 %fusion.19 = bf16[8,160,512]{2,1,0:T(8,128)(2,1)S(1)} fusion(bf16[8,160,512]{2,1,0:T(8,128)(2,1)S(1)} %fusion.17, bf16[160,4096]{1,0:T(8,128)(2,1)S(1)} %collective-permute-done.6.refs_5_, bf16[512,4096]{1,0:T(8,128)(2,1)S(1)} %maximum_select_fusion), kind=kOutput, calls=%fused_computation.38 | convolution fusion | flops 671170560 | bytes 5668864 | tf_op jit(solution)/shard_map/dot_general | solution.py:73
  77.4 0.9 collective-permute-start.9
  78.4 3.3 %collective-permute-start.16 = (bf16[2,160,512]{2,1,0:T(8,128)(2,1)S(1)}, bf16[2,160,512]{2,1,0:T(8,128)(2,1)S(1)}, u32[]{:S(2)}, u32[]{:S(2)}) collective-permute-start(bf16[2,160,512]{2,1,0:T(8,128)(2,1)S(1)} %get-tuple-element.48), channel_id=1, source_target_pairs={{0,6},{2,0},{4,2},{6,4},{1,7},{3,1},{5,3},{7,5},{8,14},{10,8},{12,... | collective-permute-start | bytes 983048 | tf_op jit(solution)/shard_map/ppermute | solution.py:58
  81.7 1.9 %collective-permute-start.15 = (bf16[2,160,512]{2,1,0:T(8,128)(2,1)S(1)}, bf16[2,160,512]{2,1,0:T(8,128)(2,1)S(1)}, u32[]{:S(2)}, u32[]{:S(2)}) collective-permute-start(bf16[2,160,512]{2,1,0:T(8,128)(2,1)S(1)} %get-tuple-element.48), channel_id=1, source_target_pairs={{0,2},{2,4},{4,6},{6,0},{1,3},{3,5},{5,7},{7,1},{8,10},{10,12},{12... | collective-permute-start | bytes 983048 | tf_op jit(solution)/shard_map/ppermute | solution.py:58
  83.6 1.5 %fusion.21 = bf16[8,160,512]{2,1,0:T(8,128)(2,1)S(1)} fusion(bf16[8,160,512]{2,1,0:T(8,128)(2,1)S(1)} %fusion.19, bf16[160,4096]{1,0:T(8,128)(2,1)S(1)} %collective-permute-done.7.refs_7_, bf16[512,4096]{1,0:T(8,128)(2,1)S(1)} %maximum_select_fusion), kind=kOutput, calls=%fused_computation.40 | convolution fusion | flops 671170560 | bytes 5668864 | tf_op jit(solution)/shard_map/dot_general | solution.py:73
  85.1 5.1 %collective-permute-done.16 = bf16[2,160,512]{2,1,0:T(8,128)(2,1)S(1)} collective-permute-done((bf16[2,160,512]{2,1,0:T(8,128)(2,1)S(1)}, bf16[2,160,512]{2,1,0:T(8,128)(2,1)S(1)}, u32[]{:S(2)}, u32[]{:S(2)}) %collective-permute-start.16) | collective-permute-done | bytes 327712 | tf_op jit(solution)/shard_map/ppermute | solution.py:58
  90.4 2.1 %collective-permute-start.17 = (bf16[1,160,512]{2,1,0:T(8,128)(2,1)S(1)}, bf16[1,160,512]{2,1,0:T(8,128)(2,1)S(1)}, u32[]{:S(2)}, u32[]{:S(2)}) collective-permute-start(bf16[1,160,512]{2,1,0:T(8,128)(2,1)S(1)} %slice.39), channel_id=1, source_target_pairs={{0,2},{2,4},{4,6},{6,0},{1,3},{3,5},{5,7},{7,1},{8,10},{10,12},{12... | collective-permute-start | bytes 491528 | tf_op jit(solution)/shard_map/ppermute | solution.py:58
  92.5 0.3 collective-permute-done.9
  92.9 1.5 %fusion.23 = bf16[8,160,512]{2,1,0:T(8,128)(2,1)S(1)} fusion(bf16[8,160,512]{2,1,0:T(8,128)(2,1)S(1)} %fusion.21, bf16[160,4096]{1,0:T(8,128)(2,1)S(1)} %constant_dynamic-update-slice_fusion.4.refs_6_, bf16[512,4096]{1,0:T(8,128)(2,1)S(1)} %maximum_select_fusion), kind=kOutput, calls=%fused_computation.42 | convolution fusion | flops 671170560 | bytes 5668864 | tf_op jit(solution)/shard_map/dot_general | solution.py:73
  94.4 1.0 dynamic-slice_bitcast_fusion.2
  95.5 2.8 %collective-permute-start.12 = (bf16[2,160,512]{2,1,0:T(8,128)(2,1)}, bf16[2,160,512]{2,1,0:T(8,128)(2,1)S(1)}, u32[]{:S(2)}, u32[]{:S(2)}) collective-permute-start(bf16[2,160,512]{2,1,0:T(8,128)(2,1)} %get-tuple-element.53), channel_id=1, source_target_pairs={{0,2},{2,4},{4,6},{6,0},{1,3},{3,5},{5,7},{7,1},{8,10},{10,12},{12... | collective-permute-start | bytes 983048 | tf_op jit(solution)/shard_map/ppermute | solution.py:58
  98.2 0.8 collective-permute-start.14
  99.0 2.6 %collective-permute-start.13 = (bf16[2,160,512]{2,1,0:T(8,128)(2,1)S(1)}, bf16[2,160,512]{2,1,0:T(8,128)(2,1)}, u32[]{:S(2)}, u32[]{:S(2)}) collective-permute-start(bf16[2,160,512]{2,1,0:T(8,128)(2,1)S(1)} %get-tuple-element.55), channel_id=1, source_target_pairs={{0,6},{2,0},{4,2},{6,4},{1,7},{3,1},{5,3},{7,5},{8,14},{10,8},{12,... | collective-permute-start | bytes 983048 | tf_op jit(solution)/shard_map/ppermute | solution.py:58
  102.3 0.6 copy.10
  103.0 1.4 maximum_select_fusion.2.features_ref
  104.4 11.5 %shard_map.85 = (bf16[256,2048]{1,0:T(8,128)(2,1)}, bf16[256,2048]{1,0:T(8,128)(2,1)}, f32[256,2048]{1,0:T(8,128)}, f32[256,2048]{1,0:T(8,128)}) custom-call(bf16[512,1280]{1,0:T(8,128)(2,1)} %maximum_select_fusion.2.features_ref, bf16[160,4096]{1,0:T(8,128)(2,1)} %copy-done.1, bf16[160,4096]{1,0:T(8,128)(2,1)} %collective-permute-done.1.refs_1_, ...), custom_call_target="tpu_custom_call" | custom-call | flops 5368709120 | bytes 18087936 | tf_op jit(solution)/shard_map/pallas_call | solution.py:111
  116.0 1.5 %fusion.26 = bf16[2,160,512]{2,1,0:T(8,128)(2,1)S(1)} fusion(bf16[2,160,512]{2,1,0:T(8,128)(2,1)} %collective-permute-done.14, bf16[2,160,512]{2,1,0:T(8,128)(2,1)} %collective-permute-done.13, bf16[2,160,512]{2,1,0:T(8,128)(2,1)S(1)} %collective-permute-done.12, bf16[4,2,160,512]{3,2,1,0:T(8,128)(2,1)} %bitcast.68, s32[]{:T(128)S(6)} %select_n.96), kind=kLoop, calls=%fused_computation.47 | loop fusion | flops 1310720 | bytes 1638404 | tf_op jit(solution)/shard_map/add | solution.py:184
  117.7 0.5 collective-permute-start.22
  118.2 6.5 %collective-permute-start.19 = (bf16[160,512]{1,0:T(8,128)(2,1)S(1)}, bf16[160,512]{1,0:T(8,128)(2,1)S(1)}, u32[]{:S(2)}, u32[]{:S(2)}) collective-permute-start(bf16[160,512]{1,0:T(8,128)(2,1)S(1)} %get-tuple-element.41), channel_id=1, source_target_pairs={{0,0},{1,16},{2,32},{3,48},{4,64},{5,80},{6,96},{7,112},{8,8},{9,2... | collective-permute-start | bytes 491528 | tf_op jit(solution)/shard_map/ppermute | solution.py:188
  124.7 3.6 %collective-permute-start.20 = (bf16[160,512]{1,0:T(8,128)(2,1)S(1)}, bf16[160,512]{1,0:T(8,128)(2,1)S(1)}, u32[]{:S(2)}, u32[]{:S(2)}) collective-permute-start(bf16[160,512]{1,0:T(8,128)(2,1)S(1)} %get-tuple-element.42), channel_id=1, source_target_pairs={{0,16},{1,0},{2,48},{3,32},{4,80},{5,64},{6,112},{7,96},{8,24},{9,... | collective-permute-start | bytes 491528 | tf_op jit(solution)/shard_map/ppermute | solution.py:189
  128.3 3.6 %collective-permute-done.19 = bf16[160,512]{1,0:T(8,128)(2,1)S(1)} collective-permute-done((bf16[160,512]{1,0:T(8,128)(2,1)S(1)}, bf16[160,512]{1,0:T(8,128)(2,1)S(1)}, u32[]{:S(2)}, u32[]{:S(2)}) %collective-permute-start.19) | collective-permute-done | bytes 163872 | tf_op jit(solution)/shard_map/ppermute | solution.py:188
  132.0 5.1 %collective-permute-done.20 = bf16[160,512]{1,0:T(8,128)(2,1)S(1)} collective-permute-done((bf16[160,512]{1,0:T(8,128)(2,1)S(1)}, bf16[160,512]{1,0:T(8,128)(2,1)S(1)}, u32[]{:S(2)}, u32[]{:S(2)}) %collective-permute-start.20) | collective-permute-done | bytes 163872 | tf_op jit(solution)/shard_map/ppermute | solution.py:189
  137.0 0.7 add_convert_fusion.2
  137.8 1.3 add_convert_fusion.1
  139.0 0.7 copy-done.5
  139.7 1.3 add_convert_fusion
  (65 shorter events, 1.8 us)
Async XLA Ops:
  0.6 8.6 %collective-permute-start.3 = (bf16[256,2048]{1,0:T(8,128)(2,1)}, bf16[256,2048]{1,0:T(8,128)(2,1)}, u32[]{:S(2)}, u32[]{:S(2)}) collective-permute-start(bf16[256,2048]{1,0:T(8,128)(2,1)} %param.10), channel_id=1, source_target_pairs={{0,8},{8,0},{1,9},{9,1},{2,10},{10,2},{3,11},{11,3},{4,12},{12,4},... | collective-permute-start | bytes 3145736 | tf_op jit(solution)/shard_map/ppermute | solution.py:54
  0.7 14.5 %collective-permute-start.4 = (bf16[256,2048]{1,0:T(8,128)(2,1)}, bf16[256,2048]{1,0:T(8,128)(2,1)}, u32[]{:S(2)}, u32[]{:S(2)}) collective-permute-start(bf16[256,2048]{1,0:T(8,128)(2,1)} %param.11), channel_id=1, source_target_pairs={{0,8},{8,0},{1,9},{9,1},{2,10},{10,2},{3,11},{11,3},{4,12},{12,4},... | collective-permute-start | bytes 3145736 | tf_op jit(solution)/shard_map/ppermute | solution.py:54
  3.4 4.3 %copy-start.8 = (bf16[256,2048]{1,0:T(8,128)(2,1)S(1)}, bf16[256,2048]{1,0:T(8,128)(2,1)}, u32[]{:S(2)}) copy-start(bf16[256,2048]{1,0:T(8,128)(2,1)} %param.10) | copy-start | bytes 3145732
  3.5 41.4 %copy-start.1 = (bf16[160,4096]{1,0:T(8,128)(2,1)}, bf16[160,4096]{1,0:T(8,128)(2,1)S(1)}, u32[]{:S(2)}) copy-start(bf16[160,4096]{1,0:T(8,128)(2,1)S(1)} %pad_maximum_fusion.refs_0_) | copy-start | bytes 3932164
  3.6 31.0 %collective-permute-start.2 = (bf16[160,4096]{1,0:T(8,128)(2,1)S(1)}, bf16[160,4096]{1,0:T(8,128)(2,1)}, u32[]{:S(2)}, u32[]{:S(2)}) collective-permute-start(bf16[160,4096]{1,0:T(8,128)(2,1)S(1)} %pad_maximum_fusion.refs_0_), channel_id=1, source_target_pairs={{0,64},{64,0},{1,65},{65,1},{2,66},{66,2},{3,67},{67,3},{4,68},{68... | collective-permute-start | bytes 3932168 | tf_op jit(solution)/shard_map/ppermute | solution.py:50
  4.9 35.5 %collective-permute-start.1 = (bf16[160,4096]{1,0:T(8,128)(2,1)S(1)}, bf16[160,4096]{1,0:T(8,128)(2,1)}, u32[]{:S(2)}, u32[]{:S(2)}) collective-permute-start(bf16[160,4096]{1,0:T(8,128)(2,1)S(1)} %pad_maximum_fusion.refs_0_), channel_id=1, source_target_pairs={{0,48},{16,0},{32,16},{48,32},{1,49},{17,1},{33,17},{49,33},{2,50}... | collective-permute-start | bytes 3932168 | tf_op jit(solution)/shard_map/ppermute | solution.py:46
  7.7 32.7 %collective-permute-start = (bf16[160,4096]{1,0:T(8,128)(2,1)S(1)}, bf16[160,4096]{1,0:T(8,128)(2,1)}, u32[]{:S(2)}, u32[]{:S(2)}) collective-permute-start(bf16[160,4096]{1,0:T(8,128)(2,1)S(1)} %pad_maximum_fusion.refs_0_), channel_id=1, source_target_pairs={{0,16},{16,32},{32,48},{48,0},{1,17},{17,33},{33,49},{49,1},{2,18}... | collective-permute-start | bytes 3932168 | tf_op jit(solution)/shard_map/ppermute | solution.py:42
  7.9 1.4 copy-start.10
  9.2 38.1 %collective-permute-start.10 = (bf16[160,512]{1,0:T(8,128)(2,1)S(1)}, bf16[160,512]{1,0:T(8,128)(2,1)S(1)}, u32[]{:S(2)}, u32[]{:S(2)}) collective-permute-start(bf16[160,512]{1,0:T(8,128)(2,1)S(1)} %copy-done.10), channel_id=1, source_target_pairs={{0,0},{16,1},{32,2},{48,3},{64,4},{80,5},{96,6},{112,7},{8,8},{24,... | collective-permute-start | bytes 491528 | tf_op jit(solution)/shard_map/ppermute | solution.py:151
  40.4 30.5 %collective-permute-start.7 = (bf16[160,4096]{1,0:T(8,128)(2,1)}, bf16[160,4096]{1,0:T(8,128)(2,1)S(1)}, u32[]{:S(2)}, u32[]{:S(2)}) collective-permute-start(bf16[160,4096]{1,0:T(8,128)(2,1)} %collective-permute-done.refs_3_), channel_id=1, source_target_pairs={{0,64},{64,0},{1,65},{65,1},{2,66},{66,2},{3,67},{67,3},{4,68},{68... | collective-permute-start | bytes 3932168 | tf_op jit(solution)/shard_map/ppermute | solution.py:50
  41.1 30.1 %collective-permute-start.5 = (bf16[160,4096]{1,0:T(8,128)(2,1)}, bf16[160,4096]{1,0:T(8,128)(2,1)S(1)}, u32[]{:S(2)}, u32[]{:S(2)}) collective-permute-start(bf16[160,4096]{1,0:T(8,128)(2,1)} %collective-permute-done.refs_3_), channel_id=1, source_target_pairs={{0,16},{16,32},{32,48},{48,0},{1,17},{17,33},{33,49},{49,1},{2,18}... | collective-permute-start | bytes 3932168 | tf_op jit(solution)/shard_map/ppermute | solution.py:42
  41.1 29.8 %collective-permute-start.6 = (bf16[160,4096]{1,0:T(8,128)(2,1)}, bf16[160,4096]{1,0:T(8,128)(2,1)S(1)}, u32[]{:S(2)}, u32[]{:S(2)}) collective-permute-start(bf16[160,4096]{1,0:T(8,128)(2,1)} %collective-permute-done.2.refs_4_), channel_id=1, source_target_pairs={{0,48},{16,0},{32,16},{48,32},{1,49},{17,1},{33,17},{49,33},{2,50}... | collective-permute-start | bytes 3932168 | tf_op jit(solution)/shard_map/ppermute | solution.py:46
  70.9 6.5 %copy-start.3 = (bf16[160,4096]{1,0:T(8,128)(2,1)}, bf16[160,4096]{1,0:T(8,128)(2,1)S(1)}, u32[]{:S(2)}) copy-start(bf16[160,4096]{1,0:T(8,128)(2,1)S(1)} %collective-permute-done.6.refs_5_) | copy-start | bytes 3932164
  70.9 12.7 %copy-start.2 = (bf16[160,4096]{1,0:T(8,128)(2,1)}, bf16[160,4096]{1,0:T(8,128)(2,1)S(1)}, u32[]{:S(2)}) copy-start(bf16[160,4096]{1,0:T(8,128)(2,1)S(1)} %collective-permute-done.7.refs_7_) | copy-start | bytes 3932164
  71.3 4.5 %copy-start.7 = (bf16[160,4096]{1,0:T(8,128)(2,1)}, bf16[160,4096]{1,0:T(8,128)(2,1)S(1)}, u32[]{:S(2)}) copy-start(bf16[160,4096]{1,0:T(8,128)(2,1)S(1)} %collective-permute-done.5.refs_2_) | copy-start | bytes 3932164
  71.3 7.0 %collective-permute-start.11 = (bf16[160,512]{1,0:T(8,128)(2,1)S(1)}, bf16[160,512]{1,0:T(8,128)(2,1)S(1)}, u32[]{:S(2)}, u32[]{:S(2)}) collective-permute-start(bf16[160,512]{1,0:T(8,128)(2,1)S(1)} %collective-permute-done.10), channel_id=1, source_target_pairs={{0,1},{1,0},{2,3},{3,2},{4,5},{5,4},{6,7},{7,6},{8,9},{9,8},{10,11... | collective-permute-start | bytes 491528 | tf_op jit(solution)/shard_map/ppermute | solution.py:164
  71.4 21.0 %collective-permute-start.8 = (bf16[80,4096]{1,0:T(8,128)(2,1)S(1)}, bf16[80,4096]{1,0:T(8,128)(2,1)S(1)}, u32[]{:S(2)}, u32[]{:S(2)}) collective-permute-start(bf16[80,4096]{1,0:T(8,128)(2,1)S(1)} %slice.31), channel_id=1, source_target_pairs={{0,16},{16,32},{32,48},{48,0},{1,17},{17,33},{33,49},{49,1},{2,18}... | collective-permute-start | bytes 1966088 | tf_op jit(solution)/shard_map/ppermute | solution.py:42
  77.4 15.4 %collective-permute-start.9 = (bf16[80,4096]{1,0:T(8,128)(2,1)S(1)}, bf16[80,4096]{1,0:T(8,128)(2,1)S(1)}, u32[]{:S(2)}, u32[]{:S(2)}) collective-permute-start(bf16[80,4096]{1,0:T(8,128)(2,1)S(1)} %slice.32), channel_id=1, source_target_pairs={{0,48},{16,0},{32,16},{48,32},{1,49},{17,1},{33,17},{49,33},{2,50}... | collective-permute-start | bytes 1966088 | tf_op jit(solution)/shard_map/ppermute | solution.py:46
  78.4 11.8 %collective-permute-start.16 = (bf16[2,160,512]{2,1,0:T(8,128)(2,1)S(1)}, bf16[2,160,512]{2,1,0:T(8,128)(2,1)S(1)}, u32[]{:S(2)}, u32[]{:S(2)}) collective-permute-start(bf16[2,160,512]{2,1,0:T(8,128)(2,1)S(1)} %get-tuple-element.48), channel_id=1, source_target_pairs={{0,6},{2,0},{4,2},{6,4},{1,7},{3,1},{5,3},{7,5},{8,14},{10,8},{12,... | collective-permute-start | bytes 983048 | tf_op jit(solution)/shard_map/ppermute | solution.py:58
  81.7 8.6 %collective-permute-start.15 = (bf16[2,160,512]{2,1,0:T(8,128)(2,1)S(1)}, bf16[2,160,512]{2,1,0:T(8,128)(2,1)S(1)}, u32[]{:S(2)}, u32[]{:S(2)}) collective-permute-start(bf16[2,160,512]{2,1,0:T(8,128)(2,1)S(1)} %get-tuple-element.48), channel_id=1, source_target_pairs={{0,2},{2,4},{4,6},{6,0},{1,3},{3,5},{5,7},{7,1},{8,10},{10,12},{12... | collective-permute-start | bytes 983048 | tf_op jit(solution)/shard_map/ppermute | solution.py:58
  90.2 11.4 %collective-permute-start.18 = (bf16[1,160,512]{2,1,0:T(8,128)(2,1)S(1)}, bf16[1,160,512]{2,1,0:T(8,128)(2,1)S(1)}, u32[]{:S(2)}, u32[]{:S(2)}) collective-permute-start(bf16[1,160,512]{2,1,0:T(8,128)(2,1)S(1)} %slice.40), channel_id=1, source_target_pairs={{0,6},{2,0},{4,2},{6,4},{1,7},{3,1},{5,3},{7,5},{8,14},{10,8},{12,... | collective-permute-start | bytes 491528 | tf_op jit(solution)/shard_map/ppermute | solution.py:58
  90.4 11.3 %collective-permute-start.17 = (bf16[1,160,512]{2,1,0:T(8,128)(2,1)S(1)}, bf16[1,160,512]{2,1,0:T(8,128)(2,1)S(1)}, u32[]{:S(2)}, u32[]{:S(2)}) collective-permute-start(bf16[1,160,512]{2,1,0:T(8,128)(2,1)S(1)} %slice.39), channel_id=1, source_target_pairs={{0,2},{2,4},{4,6},{6,0},{1,3},{3,5},{5,7},{7,1},{8,10},{10,12},{12... | collective-permute-start | bytes 491528 | tf_op jit(solution)/shard_map/ppermute | solution.py:58
  92.9 1.6 %copy-start.4 = (bf16[160,4096]{1,0:T(8,128)(2,1)}, bf16[160,4096]{1,0:T(8,128)(2,1)S(1)}, u32[]{:S(2)}) copy-start(bf16[160,4096]{1,0:T(8,128)(2,1)S(1)} %constant_dynamic-update-slice_fusion.4.refs_6_) | copy-start | bytes 3932164
  94.4 7.3 %copy-start = (bf16[8,160,512]{2,1,0:T(8,128)(2,1)}, bf16[8,160,512]{2,1,0:T(8,128)(2,1)S(1)}, u32[]{:S(2)}) copy-start(bf16[8,160,512]{2,1,0:T(8,128)(2,1)S(1)} %fusion.23) | copy-start | bytes 3932164
  95.5 20.5 %collective-permute-start.12 = (bf16[2,160,512]{2,1,0:T(8,128)(2,1)}, bf16[2,160,512]{2,1,0:T(8,128)(2,1)S(1)}, u32[]{:S(2)}, u32[]{:S(2)}) collective-permute-start(bf16[2,160,512]{2,1,0:T(8,128)(2,1)} %get-tuple-element.53), channel_id=1, source_target_pairs={{0,2},{2,4},{4,6},{6,0},{1,3},{3,5},{5,7},{7,1},{8,10},{10,12},{12... | collective-permute-start | bytes 983048 | tf_op jit(solution)/shard_map/ppermute | solution.py:58
  98.2 17.7 %collective-permute-start.14 = (bf16[2,160,512]{2,1,0:T(8,128)(2,1)}, bf16[2,160,512]{2,1,0:T(8,128)(2,1)}, u32[]{:S(2)}, u32[]{:S(2)}) collective-permute-start(bf16[2,160,512]{2,1,0:T(8,128)(2,1)} %get-tuple-element.54), channel_id=1, source_target_pairs={{0,4},{2,6},{4,0},{6,2},{1,5},{3,7},{5,1},{7,3},{8,12},{10,14},{12... | collective-permute-start | bytes 983048 | tf_op jit(solution)/shard_map/ppermute | solution.py:58
  99.0 17.0 %collective-permute-start.13 = (bf16[2,160,512]{2,1,0:T(8,128)(2,1)S(1)}, bf16[2,160,512]{2,1,0:T(8,128)(2,1)}, u32[]{:S(2)}, u32[]{:S(2)}) collective-permute-start(bf16[2,160,512]{2,1,0:T(8,128)(2,1)S(1)} %get-tuple-element.55), channel_id=1, source_target_pairs={{0,6},{2,0},{4,2},{6,4},{1,7},{3,1},{5,3},{7,5},{8,14},{10,8},{12,... | collective-permute-start | bytes 983048 | tf_op jit(solution)/shard_map/ppermute | solution.py:58
  115.9 1.7 %copy-start.9 = (bf16[256,2048]{1,0:T(8,128)(2,1)S(1)}, bf16[256,2048]{1,0:T(8,128)(2,1)}, u32[]{:S(2)}) copy-start(bf16[256,2048]{1,0:T(8,128)(2,1)} %get-tuple-element.46) | copy-start | bytes 3145732
  116.0 21.8 %copy-start.6 = (f32[256,2048]{1,0:T(8,128)S(1)}, f32[256,2048]{1,0:T(8,128)}, u32[]{:S(2)}) copy-start(f32[256,2048]{1,0:T(8,128)} %get-tuple-element.43) | copy-start | bytes 6291460
  117.6 20.2 %collective-permute-start.21 = (bf16[256,2048]{1,0:T(8,128)(2,1)}, bf16[256,2048]{1,0:T(8,128)(2,1)S(1)}, u32[]{:S(2)}, u32[]{:S(2)}) collective-permute-start(bf16[256,2048]{1,0:T(8,128)(2,1)} %get-tuple-element.44), channel_id=1, source_target_pairs={{0,8},{8,0},{1,9},{9,1},{2,10},{10,2},{3,11},{11,3},{4,12},{12,4},... | collective-permute-start | bytes 3145736 | tf_op jit(solution)/shard_map/ppermute | solution.py:54
  117.7 21.3 %collective-permute-start.22 = (bf16[256,2048]{1,0:T(8,128)(2,1)S(1)}, bf16[256,2048]{1,0:T(8,128)(2,1)S(1)}, u32[]{:S(2)}, u32[]{:S(2)}) collective-permute-start(bf16[256,2048]{1,0:T(8,128)(2,1)S(1)} %copy-done.9), channel_id=1, source_target_pairs={{0,8},{8,0},{1,9},{9,1},{2,10},{10,2},{3,11},{11,3},{4,12},{12,4},... | collective-permute-start | bytes 3145736 | tf_op jit(solution)/shard_map/ppermute | solution.py:54
  118.2 13.8 %collective-permute-start.19 = (bf16[160,512]{1,0:T(8,128)(2,1)S(1)}, bf16[160,512]{1,0:T(8,128)(2,1)S(1)}, u32[]{:S(2)}, u32[]{:S(2)}) collective-permute-start(bf16[160,512]{1,0:T(8,128)(2,1)S(1)} %get-tuple-element.41), channel_id=1, source_target_pairs={{0,0},{1,16},{2,32},{3,48},{4,64},{5,80},{6,96},{7,112},{8,8},{9,2... | collective-permute-start | bytes 491528 | tf_op jit(solution)/shard_map/ppermute | solution.py:188
  124.7 12.3 %collective-permute-start.20 = (bf16[160,512]{1,0:T(8,128)(2,1)S(1)}, bf16[160,512]{1,0:T(8,128)(2,1)S(1)}, u32[]{:S(2)}, u32[]{:S(2)}) collective-permute-start(bf16[160,512]{1,0:T(8,128)(2,1)S(1)} %get-tuple-element.42), channel_id=1, source_target_pairs={{0,16},{1,0},{2,48},{3,32},{4,80},{5,64},{6,112},{7,96},{8,24},{9,... | collective-permute-start | bytes 491528 | tf_op jit(solution)/shard_map/ppermute | solution.py:189
  137.8 2.0 %copy-start.5 = (f32[256,2048]{1,0:T(8,128)S(1)}, f32[256,2048]{1,0:T(8,128)}, u32[]{:S(2)}) copy-start(f32[256,2048]{1,0:T(8,128)} %get-tuple-element.45) | copy-start | bytes 6291460

commit v5 on v4

--- a/solution.py
+++ b/solution.py
@@ -189,6 +189,7 @@
     cross = lax.ppermute(cross, ALL, to_owner(1))
     grad_gate = (kept_gate + came[0].astype(F32)).astype(BF16)
     grad_up = (kept_up + came[1].astype(F32)).astype(BF16)
+    same, cross, grad_gate, grad_up = tied((same, cross, grad_gate, grad_up))
     d_tokens = (same.astype(F32) + cross.astype(F32)).astype(BF16)
     return d_tokens, grad_gate, grad_up
 

time: 141 us -> 138 us (0.979)
  waiting for transfers between devices: 51.9 us -> 48.7 us
    ppermute x1, waiting for transfers between devices: 3.65 us -> 0.39 us  [local(): same = lax.ppermute(same, ALL, to_owner(0))]
  transfers between devices with their start and end apart: 23 -> 23, of which waited for: 9 -> 9; matrix products, arithmetic and copies ran while one was open for 22% -> 23% of each run, Pallas kernels for 8% -> 8%
where the time goes in v5:
time: 138 us
  waiting for transfers between devices  48.7 us (35%)
  starting transfers between devices  42 us (30%)
  matrix products  16.5 us (12%)
  Pallas kernels  11.6 us (8%)
  other arithmetic  10.7 us (8%)
  local copies, waits for them, and re-layouts  7.16 us (5%)
    ppermute x3, waiting for transfers between devices, left(): return lax.ppermute(v, 'x', BACK)  20.9 us
    dot_general x8, matrix products, input_term(): lax.dot_general(rows, weights, (((1,), (1,)), ((), ())), preferred_elemen...  16.5 us
    ppermute x2, waiting for transfers between devices, across(): return lax.ppermute(v, 'yl', SWAP)  16.1 us
    ppermute x7, starting transfers between devices, along_z(): return lax.ppermute(v, 'z', [(i, (i + step) % 4) for i in range(4)])  13.5 us
    pallas_call x1, Pallas kernels, weight_sums(): pl.pallas_call(functools.partial(sum_kernel, blocks), out_shape=[jax.Shap...  11.6 us
    ppermute x3, starting transfers between devices, left(): return lax.ppermute(v, 'x', BACK)  7.46 us
    ppermute x1, starting transfers between devices, local(): same = lax.ppermute(same, ALL, to_owner(0))  6.53 us
    ppermute x7, waiting for transfers between devices, along_z(): return lax.ppermute(v, 'z', [(i, (i + step) % 4) for i in range(4)])  5.09 us
  transfers between devices with their start and end apart: 23, of which 9 were waited for; matrix products, arithmetic and copies ran while one was open for 23% of the time, Pallas kernels for 8%

profile of v5, /device:TPU:48, one launch (start us, length us, event | category | flops | bytes accessed | tf_op | source)
XLA Modules:
  0.0 137.8 jit_solution(9009749783430863861)
XLA Ops:
  0.7 0.5 collective-permute-start.4
  1.2 2.2 %fusion.2 = (bf16[160,2048]{1,0:T(8,128)(2,1)S(1)}, bf16[160,2048]{1,0:T(8,128)(2,1)S(1)}) fusion(bf16[160,2048]{1,0:T(8,128)(2,1)} %param.9, bf16[160,2048]{1,0:T(8,128)(2,1)} %param.7, bf16[160,2048]{1,0:T(8,128)(2,1)} %param.8), kind=kLoop, calls=%fused_computation.9 | loop fusion | flops 5242880 | bytes 3276800 | tf_op jit(solution)/shard_map/convert_element_type | solution.py:139
  3.6 1.4 collective-permute-start.2
  4.9 2.8 %collective-permute-start.1 = (bf16[160,4096]{1,0:T(8,128)(2,1)S(1)}, bf16[160,4096]{1,0:T(8,128)(2,1)}, u32[]{:S(2)}, u32[]{:S(2)}) collective-permute-start(bf16[160,4096]{1,0:T(8,128)(2,1)S(1)} %pad_maximum_fusion.refs_0_), channel_id=1, source_target_pairs={{0,48},{16,0},{32,16},{48,32},{1,49},{17,1},{33,17},{49,33},{2,50}... | collective-permute-start | bytes 3932168 | tf_op jit(solution)/shard_map/ppermute | solution.py:46
  7.9 1.3 constant_dynamic-update-slice_fusion
  9.2 4.7 %collective-permute-start.10 = (bf16[160,512]{1,0:T(8,128)(2,1)S(1)}, bf16[160,512]{1,0:T(8,128)(2,1)S(1)}, u32[]{:S(2)}, u32[]{:S(2)}) collective-permute-start(bf16[160,512]{1,0:T(8,128)(2,1)S(1)} %copy-done.9), channel_id=1, source_target_pairs={{0,0},{16,1},{32,2},{48,3},{64,4},{80,5},{96,6},{112,7},{8,8},{24,... | collective-permute-start | bytes 491528 | tf_op jit(solution)/shard_map/ppermute | solution.py:151
  13.9 1.3 constant_dynamic-update-slice_fusion.3
  15.3 1.3 constant_dynamic-update-slice_fusion.2
  16.6 1.8 %maximum_select_fusion = bf16[512,4096]{1,0:T(8,128)(2,1)S(1)} fusion(bf16[256,4096]{1,0:T(8,128)(2,1)S(1)} %constant_dynamic-update-slice_fusion.2, bf16[256,4096]{1,0:T(8,128)(2,1)S(1)} %constant_dynamic-update-slice_fusion, pred[]{:T(512)S(6)} %eq.20), kind=kLoop, calls=%fused_computation | loop fusion | flops 18874368 | bytes 8388609 | tf_op jit(solution)/shard_map/jit(_where)/select_n | solution.py:146
  18.4 16.1 %collective-permute-done.2.refs_4_ = bf16[160,4096]{1,0:T(8,128)(2,1)} collective-permute-done((bf16[160,4096]{1,0:T(8,128)(2,1)S(1)}, bf16[160,4096]{1,0:T(8,128)(2,1)}, u32[]{:S(2)}, u32[]{:S(2)}) %collective-permute-start.2) | collective-permute-done | bytes 1310752 | tf_op jit(solution)/shard_map/ppermute | solution.py:50
  34.5 5.9 %collective-permute-done.1.refs_1_ = bf16[160,4096]{1,0:T(8,128)(2,1)} collective-permute-done((bf16[160,4096]{1,0:T(8,128)(2,1)S(1)}, bf16[160,4096]{1,0:T(8,128)(2,1)}, u32[]{:S(2)}, u32[]{:S(2)}) %collective-permute-start.1) | collective-permute-done | bytes 1310752 | tf_op jit(solution)/shard_map/ppermute | solution.py:46
  40.4 0.7 collective-permute-start.7
  41.1 3.8 %collective-permute-start.6 = (bf16[160,4096]{1,0:T(8,128)(2,1)}, bf16[160,4096]{1,0:T(8,128)(2,1)S(1)}, u32[]{:S(2)}, u32[]{:S(2)}) collective-permute-start(bf16[160,4096]{1,0:T(8,128)(2,1)} %collective-permute-done.2.refs_4_), channel_id=1, source_target_pairs={{0,48},{16,0},{32,16},{48,32},{1,49},{17,1},{33,17},{49,33},{2,50}... | collective-permute-start | bytes 3932168 | tf_op jit(solution)/shard_map/ppermute | solution.py:46
  44.9 1.6 %fusion.9 = bf16[1,160,512]{2,1,0:T(8,128)(2,1)S(1)} fusion(bf16[160,4096]{1,0:T(8,128)(2,1)S(1)} %pad_maximum_fusion.refs_0_, bf16[512,4096]{1,0:T(8,128)(2,1)S(1)} %maximum_select_fusion), kind=kOutput, calls=%fused_computation.28 | convolution fusion | flops 671170560 | bytes 5668864 | tf_op jit(solution)/shard_map/dot_general | solution.py:73
  46.5 0.8 collective-permute-done.10
  47.5 2.9 %fusion.11 = bf16[8,160,512]{2,1,0:T(8,128)(2,1)S(1)} fusion(bf16[8,160,512]{2,1,0:T(8,128)(2,1)S(1)} %dynamic_update_slice.25, bf16[160,4096]{1,0:T(8,128)(2,1)} %collective-permute-done.1.refs_1_, bf16[512,4096]{1,0:T(8,128)(2,1)S(1)} %maximum_select_fusion), kind=kOutput, calls=%fused_computation.30 | convolution fusion | flops 671170560 | bytes 5668864 | tf_op jit(solution)/shard_map/dot_general | solution.py:73
  50.4 2.9 %fusion.13 = bf16[8,160,512]{2,1,0:T(8,128)(2,1)S(1)} fusion(bf16[8,160,512]{2,1,0:T(8,128)(2,1)S(1)} %fusion.11, bf16[160,4096]{1,0:T(8,128)(2,1)} %collective-permute-done.refs_3_, bf16[512,4096]{1,0:T(8,128)(2,1)S(1)} %maximum_select_fusion), kind=kOutput, calls=%fused_computation.32 | convolution fusion | flops 671170560 | bytes 5668864 | tf_op jit(solution)/shard_map/dot_general | solution.py:73
  53.3 2.9 %fusion.15 = bf16[8,160,512]{2,1,0:T(8,128)(2,1)S(1)} fusion(bf16[8,160,512]{2,1,0:T(8,128)(2,1)S(1)} %fusion.13, bf16[160,4096]{1,0:T(8,128)(2,1)} %collective-permute-done.2.refs_4_, bf16[512,4096]{1,0:T(8,128)(2,1)S(1)} %maximum_select_fusion), kind=kOutput, calls=%fused_computation.34 | convolution fusion | flops 671170560 | bytes 5668864 | tf_op jit(solution)/shard_map/dot_general | solution.py:73
  56.2 14.7 %collective-permute-done.6.refs_5_ = bf16[160,4096]{1,0:T(8,128)(2,1)S(1)} collective-permute-done((bf16[160,4096]{1,0:T(8,128)(2,1)}, bf16[160,4096]{1,0:T(8,128)(2,1)S(1)}, u32[]{:S(2)}, u32[]{:S(2)}) %collective-permute-start.6) | collective-permute-done | bytes 1310752 | tf_op jit(solution)/shard_map/ppermute | solution.py:46
  70.9 0.3 collective-permute-done.5.refs_2_
  71.4 2.9 %collective-permute-start.8 = (bf16[80,4096]{1,0:T(8,128)(2,1)S(1)}, bf16[80,4096]{1,0:T(8,128)(2,1)S(1)}, u32[]{:S(2)}, u32[]{:S(2)}) collective-permute-start(bf16[80,4096]{1,0:T(8,128)(2,1)S(1)} %slice.31), channel_id=1, source_target_pairs={{0,16},{16,32},{32,48},{48,0},{1,17},{17,33},{33,49},{49,1},{2,18}... | collective-permute-start | bytes 1966088 | tf_op jit(solution)/shard_map/ppermute | solution.py:42
  74.3 1.5 %fusion.17 = bf16[8,160,512]{2,1,0:T(8,128)(2,1)S(1)} fusion(bf16[8,160,512]{2,1,0:T(8,128)(2,1)S(1)} %fusion.15, bf16[160,4096]{1,0:T(8,128)(2,1)S(1)} %collective-permute-done.5.refs_2_, bf16[512,4096]{1,0:T(8,128)(2,1)S(1)} %maximum_select_fusion), kind=kOutput, calls=%fused_computation.36 | convolution fusion | flops 671170560 | bytes 5668864 | tf_op jit(solution)/shard_map/dot_general | solution.py:73
  75.8 1.5 %fusion.19 = bf16[8,160,512]{2,1,0:T(8,128)(2,1)S(1)} fusion(bf16[8,160,512]{2,1,0:T(8,128)(2,1)S(1)} %fusion.17, bf16[160,4096]{1,0:T(8,128)(2,1)S(1)} %collective-permute-done.6.refs_5_, bf16[512,4096]{1,0:T(8,128)(2,1)S(1)} %maximum_select_fusion), kind=kOutput, calls=%fused_computation.38 | convolution fusion | flops 671170560 | bytes 5668864 | tf_op jit(solution)/shard_map/dot_general | solution.py:73
  77.4 0.9 collective-permute-start.9
  78.4 3.3 %collective-permute-start.16 = (bf16[2,160,512]{2,1,0:T(8,128)(2,1)S(1)}, bf16[2,160,512]{2,1,0:T(8,128)(2,1)S(1)}, u32[]{:S(2)}, u32[]{:S(2)}) collective-permute-start(bf16[2,160,512]{2,1,0:T(8,128)(2,1)S(1)} %get-tuple-element.56), channel_id=1, source_target_pairs={{0,6},{2,0},{4,2},{6,4},{1,7},{3,1},{5,3},{7,5},{8,14},{10,8},{12,... | collective-permute-start | bytes 983048 | tf_op jit(solution)/shard_map/ppermute | solution.py:58
  81.7 1.9 %collective-permute-start.15 = (bf16[2,160,512]{2,1,0:T(8,128)(2,1)S(1)}, bf16[2,160,512]{2,1,0:T(8,128)(2,1)S(1)}, u32[]{:S(2)}, u32[]{:S(2)}) collective-permute-start(bf16[2,160,512]{2,1,0:T(8,128)(2,1)S(1)} %get-tuple-element.56), channel_id=1, source_target_pairs={{0,2},{2,4},{4,6},{6,0},{1,3},{3,5},{5,7},{7,1},{8,10},{10,12},{12... | collective-permute-start | bytes 983048 | tf_op jit(solution)/shard_map/ppermute | solution.py:58
  83.6 1.5 %fusion.21 = bf16[8,160,512]{2,1,0:T(8,128)(2,1)S(1)} fusion(bf16[8,160,512]{2,1,0:T(8,128)(2,1)S(1)} %fusion.19, bf16[160,4096]{1,0:T(8,128)(2,1)S(1)} %collective-permute-done.7.refs_7_, bf16[512,4096]{1,0:T(8,128)(2,1)S(1)} %maximum_select_fusion), kind=kOutput, calls=%fused_computation.40 | convolution fusion | flops 671170560 | bytes 5668864 | tf_op jit(solution)/shard_map/dot_general | solution.py:73
  85.1 5.1 %collective-permute-done.16 = bf16[2,160,512]{2,1,0:T(8,128)(2,1)S(1)} collective-permute-done((bf16[2,160,512]{2,1,0:T(8,128)(2,1)S(1)}, bf16[2,160,512]{2,1,0:T(8,128)(2,1)S(1)}, u32[]{:S(2)}, u32[]{:S(2)}) %collective-permute-start.16) | collective-permute-done | bytes 327712 | tf_op jit(solution)/shard_map/ppermute | solution.py:58
  90.4 2.1 %collective-permute-start.17 = (bf16[1,160,512]{2,1,0:T(8,128)(2,1)S(1)}, bf16[1,160,512]{2,1,0:T(8,128)(2,1)S(1)}, u32[]{:S(2)}, u32[]{:S(2)}) collective-permute-start(bf16[1,160,512]{2,1,0:T(8,128)(2,1)S(1)} %slice.39), channel_id=1, source_target_pairs={{0,2},{2,4},{4,6},{6,0},{1,3},{3,5},{5,7},{7,1},{8,10},{10,12},{12... | collective-permute-start | bytes 491528 | tf_op jit(solution)/shard_map/ppermute | solution.py:58
  92.5 0.3 collective-permute-done.9
  92.9 1.5 %fusion.23 = bf16[8,160,512]{2,1,0:T(8,128)(2,1)S(1)} fusion(bf16[8,160,512]{2,1,0:T(8,128)(2,1)S(1)} %fusion.21, bf16[160,4096]{1,0:T(8,128)(2,1)S(1)} %constant_dynamic-update-slice_fusion.4.refs_6_, bf16[512,4096]{1,0:T(8,128)(2,1)S(1)} %maximum_select_fusion), kind=kOutput, calls=%fused_computation.42 | convolution fusion | flops 671170560 | bytes 5668864 | tf_op jit(solution)/shard_map/dot_general | solution.py:73
  94.4 1.1 dynamic-slice_bitcast_fusion.2
  95.5 2.8 %collective-permute-start.12 = (bf16[2,160,512]{2,1,0:T(8,128)(2,1)}, bf16[2,160,512]{2,1,0:T(8,128)(2,1)S(1)}, u32[]{:S(2)}, u32[]{:S(2)}) collective-permute-start(bf16[2,160,512]{2,1,0:T(8,128)(2,1)} %get-tuple-element.61), channel_id=1, source_target_pairs={{0,2},{2,4},{4,6},{6,0},{1,3},{3,5},{5,7},{7,1},{8,10},{10,12},{12... | collective-permute-start | bytes 983048 | tf_op jit(solution)/shard_map/ppermute | solution.py:58
  98.3 0.8 collective-permute-start.14
  99.1 2.6 %collective-permute-start.13 = (bf16[2,160,512]{2,1,0:T(8,128)(2,1)S(1)}, bf16[2,160,512]{2,1,0:T(8,128)(2,1)}, u32[]{:S(2)}, u32[]{:S(2)}) collective-permute-start(bf16[2,160,512]{2,1,0:T(8,128)(2,1)S(1)} %get-tuple-element.63), channel_id=1, source_target_pairs={{0,6},{2,0},{4,2},{6,4},{1,7},{3,1},{5,3},{7,5},{8,14},{10,8},{12,... | collective-permute-start | bytes 983048 | tf_op jit(solution)/shard_map/ppermute | solution.py:58
  102.3 0.6 copy.10
  103.1 1.4 %maximum_select_fusion.2.features_ref = bf16[512,1280]{1,0:T(8,128)(2,1)} fusion(bf16[256,1280]{1,0:T(8,128)(2,1)S(1)} %get-tuple-element.58, bf16[256,1280]{1,0:T(8,128)(2,1)S(1)} %get-tuple-element.57, pred[]{:T(512)S(6)} %eq.20, bf16[1280,512]{0,1:T(8,128)(2,1)S(1)} %copy.10), kind=kLoop, calls=%fused_computation.18 | loop fusion | flops 3276800 | bytes 3932161 | tf_op jit(solution)/shard_map/jit(_where)/select_n | solution.py:177
  104.5 11.6 %shard_map.85 = (bf16[256,2048]{1,0:T(8,128)(2,1)}, bf16[256,2048]{1,0:T(8,128)(2,1)}, f32[256,2048]{1,0:T(8,128)}, f32[256,2048]{1,0:T(8,128)}) custom-call(bf16[512,1280]{1,0:T(8,128)(2,1)} %maximum_select_fusion.2.features_ref, bf16[160,4096]{1,0:T(8,128)(2,1)} %copy-done.1, bf16[160,4096]{1,0:T(8,128)(2,1)} %collective-permute-done.1.refs_1_, ...), custom_call_target="tpu_custom_call" | custom-call | flops 5368709120 | bytes 18087936 | tf_op jit(solution)/shard_map/pallas_call | solution.py:111
  116.1 1.5 %fusion.26 = bf16[2,160,512]{2,1,0:T(8,128)(2,1)S(1)} fusion(bf16[2,160,512]{2,1,0:T(8,128)(2,1)} %collective-permute-done.14, bf16[2,160,512]{2,1,0:T(8,128)(2,1)} %collective-permute-done.13, bf16[2,160,512]{2,1,0:T(8,128)(2,1)S(1)} %collective-permute-done.12, bf16[4,2,160,512]{3,2,1,0:T(8,128)(2,1)} %bitcast.68, s32[]{:T(128)S(6)} %select_n.96), kind=kLoop, calls=%fused_computation.47 | loop fusion | flops 1310720 | bytes 1638404 | tf_op jit(solution)/shard_map/add | solution.py:184
  117.8 0.5 collective-permute-start.22
  118.3 6.5 %collective-permute-start.19 = (bf16[160,512]{1,0:T(8,128)(2,1)S(1)}, bf16[160,512]{1,0:T(8,128)(2,1)S(1)}, u32[]{:S(2)}, u32[]{:S(2)}) collective-permute-start(bf16[160,512]{1,0:T(8,128)(2,1)S(1)} %get-tuple-element.45), channel_id=1, source_target_pairs={{0,0},{1,16},{2,32},{3,48},{4,64},{5,80},{6,96},{7,112},{8,8},{9,2... | collective-permute-start | bytes 491528 | tf_op jit(solution)/shard_map/ppermute | solution.py:188
  124.8 3.6 %collective-permute-start.20 = (bf16[160,512]{1,0:T(8,128)(2,1)S(1)}, bf16[160,512]{1,0:T(8,128)(2,1)S(1)}, u32[]{:S(2)}, u32[]{:S(2)}) collective-permute-start(bf16[160,512]{1,0:T(8,128)(2,1)S(1)} %get-tuple-element.46), channel_id=1, source_target_pairs={{0,16},{1,0},{2,48},{3,32},{4,80},{5,64},{6,112},{7,96},{8,24},{9,... | collective-permute-start | bytes 491528 | tf_op jit(solution)/shard_map/ppermute | solution.py:189
  128.4 1.3 add_convert_fusion.1
  129.7 0.7 copy-done.5
  130.4 1.3 add_convert_fusion
  131.6 0.4 collective-permute-done.19
  132.0 5.1 %collective-permute-done.20 = bf16[160,512]{1,0:T(8,128)(2,1)S(1)} collective-permute-done((bf16[160,512]{1,0:T(8,128)(2,1)S(1)}, bf16[160,512]{1,0:T(8,128)(2,1)S(1)}, u32[]{:S(2)}, u32[]{:S(2)}) %collective-permute-start.20) | collective-permute-done | bytes 163872 | tf_op jit(solution)/shard_map/ppermute | solution.py:189
  137.1 0.7 add_convert_fusion.2
  (63 shorter events, 1.8 us)
Async XLA Ops:
  0.6 8.6 %collective-permute-start.3 = (bf16[256,2048]{1,0:T(8,128)(2,1)}, bf16[256,2048]{1,0:T(8,128)(2,1)}, u32[]{:S(2)}, u32[]{:S(2)}) collective-permute-start(bf16[256,2048]{1,0:T(8,128)(2,1)} %param.10), channel_id=1, source_target_pairs={{0,8},{8,0},{1,9},{9,1},{2,10},{10,2},{3,11},{11,3},{4,12},{12,4},... | collective-permute-start | bytes 3145736 | tf_op jit(solution)/shard_map/ppermute | solution.py:54
  0.7 14.5 %collective-permute-start.4 = (bf16[256,2048]{1,0:T(8,128)(2,1)}, bf16[256,2048]{1,0:T(8,128)(2,1)}, u32[]{:S(2)}, u32[]{:S(2)}) collective-permute-start(bf16[256,2048]{1,0:T(8,128)(2,1)} %param.11), channel_id=1, source_target_pairs={{0,8},{8,0},{1,9},{9,1},{2,10},{10,2},{3,11},{11,3},{4,12},{12,4},... | collective-permute-start | bytes 3145736 | tf_op jit(solution)/shard_map/ppermute | solution.py:54
  3.4 4.3 %copy-start.8 = (bf16[256,2048]{1,0:T(8,128)(2,1)S(1)}, bf16[256,2048]{1,0:T(8,128)(2,1)}, u32[]{:S(2)}) copy-start(bf16[256,2048]{1,0:T(8,128)(2,1)} %param.10) | copy-start | bytes 3145732
  3.5 41.4 %copy-start.1 = (bf16[160,4096]{1,0:T(8,128)(2,1)}, bf16[160,4096]{1,0:T(8,128)(2,1)S(1)}, u32[]{:S(2)}) copy-start(bf16[160,4096]{1,0:T(8,128)(2,1)S(1)} %pad_maximum_fusion.refs_0_) | copy-start | bytes 3932164
  3.6 31.0 %collective-permute-start.2 = (bf16[160,4096]{1,0:T(8,128)(2,1)S(1)}, bf16[160,4096]{1,0:T(8,128)(2,1)}, u32[]{:S(2)}, u32[]{:S(2)}) collective-permute-start(bf16[160,4096]{1,0:T(8,128)(2,1)S(1)} %pad_maximum_fusion.refs_0_), channel_id=1, source_target_pairs={{0,64},{64,0},{1,65},{65,1},{2,66},{66,2},{3,67},{67,3},{4,68},{68... | collective-permute-start | bytes 3932168 | tf_op jit(solution)/shard_map/ppermute | solution.py:50
  4.9 35.5 %collective-permute-start.1 = (bf16[160,4096]{1,0:T(8,128)(2,1)S(1)}, bf16[160,4096]{1,0:T(8,128)(2,1)}, u32[]{:S(2)}, u32[]{:S(2)}) collective-permute-start(bf16[160,4096]{1,0:T(8,128)(2,1)S(1)} %pad_maximum_fusion.refs_0_), channel_id=1, source_target_pairs={{0,48},{16,0},{32,16},{48,32},{1,49},{17,1},{33,17},{49,33},{2,50}... | collective-permute-start | bytes 3932168 | tf_op jit(solution)/shard_map/ppermute | solution.py:46
  7.7 32.7 %collective-permute-start = (bf16[160,4096]{1,0:T(8,128)(2,1)S(1)}, bf16[160,4096]{1,0:T(8,128)(2,1)}, u32[]{:S(2)}, u32[]{:S(2)}) collective-permute-start(bf16[160,4096]{1,0:T(8,128)(2,1)S(1)} %pad_maximum_fusion.refs_0_), channel_id=1, source_target_pairs={{0,16},{16,32},{32,48},{48,0},{1,17},{17,33},{33,49},{49,1},{2,18}... | collective-permute-start | bytes 3932168 | tf_op jit(solution)/shard_map/ppermute | solution.py:42
  7.9 1.4 copy-start.9
  9.2 38.1 %collective-permute-start.10 = (bf16[160,512]{1,0:T(8,128)(2,1)S(1)}, bf16[160,512]{1,0:T(8,128)(2,1)S(1)}, u32[]{:S(2)}, u32[]{:S(2)}) collective-permute-start(bf16[160,512]{1,0:T(8,128)(2,1)S(1)} %copy-done.9), channel_id=1, source_target_pairs={{0,0},{16,1},{32,2},{48,3},{64,4},{80,5},{96,6},{112,7},{8,8},{24,... | collective-permute-start | bytes 491528 | tf_op jit(solution)/shard_map/ppermute | solution.py:151
  40.4 30.5 %collective-permute-start.7 = (bf16[160,4096]{1,0:T(8,128)(2,1)}, bf16[160,4096]{1,0:T(8,128)(2,1)S(1)}, u32[]{:S(2)}, u32[]{:S(2)}) collective-permute-start(bf16[160,4096]{1,0:T(8,128)(2,1)} %collective-permute-done.refs_3_), channel_id=1, source_target_pairs={{0,64},{64,0},{1,65},{65,1},{2,66},{66,2},{3,67},{67,3},{4,68},{68... | collective-permute-start | bytes 3932168 | tf_op jit(solution)/shard_map/ppermute | solution.py:50
  41.1 30.1 %collective-permute-start.5 = (bf16[160,4096]{1,0:T(8,128)(2,1)}, bf16[160,4096]{1,0:T(8,128)(2,1)S(1)}, u32[]{:S(2)}, u32[]{:S(2)}) collective-permute-start(bf16[160,4096]{1,0:T(8,128)(2,1)} %collective-permute-done.refs_3_), channel_id=1, source_target_pairs={{0,16},{16,32},{32,48},{48,0},{1,17},{17,33},{33,49},{49,1},{2,18}... | collective-permute-start | bytes 3932168 | tf_op jit(solution)/shard_map/ppermute | solution.py:42
  41.1 29.8 %collective-permute-start.6 = (bf16[160,4096]{1,0:T(8,128)(2,1)}, bf16[160,4096]{1,0:T(8,128)(2,1)S(1)}, u32[]{:S(2)}, u32[]{:S(2)}) collective-permute-start(bf16[160,4096]{1,0:T(8,128)(2,1)} %collective-permute-done.2.refs_4_), channel_id=1, source_target_pairs={{0,48},{16,0},{32,16},{48,32},{1,49},{17,1},{33,17},{49,33},{2,50}... | collective-permute-start | bytes 3932168 | tf_op jit(solution)/shard_map/ppermute | solution.py:46
  70.9 6.5 %copy-start.3 = (bf16[160,4096]{1,0:T(8,128)(2,1)}, bf16[160,4096]{1,0:T(8,128)(2,1)S(1)}, u32[]{:S(2)}) copy-start(bf16[160,4096]{1,0:T(8,128)(2,1)S(1)} %collective-permute-done.6.refs_5_) | copy-start | bytes 3932164
  70.9 12.7 %copy-start.2 = (bf16[160,4096]{1,0:T(8,128)(2,1)}, bf16[160,4096]{1,0:T(8,128)(2,1)S(1)}, u32[]{:S(2)}) copy-start(bf16[160,4096]{1,0:T(8,128)(2,1)S(1)} %collective-permute-done.7.refs_7_) | copy-start | bytes 3932164
  71.3 4.5 %copy-start.7 = (bf16[160,4096]{1,0:T(8,128)(2,1)}, bf16[160,4096]{1,0:T(8,128)(2,1)S(1)}, u32[]{:S(2)}) copy-start(bf16[160,4096]{1,0:T(8,128)(2,1)S(1)} %collective-permute-done.5.refs_2_) | copy-start | bytes 3932164
  71.3 7.0 %collective-permute-start.11 = (bf16[160,512]{1,0:T(8,128)(2,1)S(1)}, bf16[160,512]{1,0:T(8,128)(2,1)S(1)}, u32[]{:S(2)}, u32[]{:S(2)}) collective-permute-start(bf16[160,512]{1,0:T(8,128)(2,1)S(1)} %collective-permute-done.10), channel_id=1, source_target_pairs={{0,1},{1,0},{2,3},{3,2},{4,5},{5,4},{6,7},{7,6},{8,9},{9,8},{10,11... | collective-permute-start | bytes 491528 | tf_op jit(solution)/shard_map/ppermute | solution.py:164
  71.4 21.0 %collective-permute-start.8 = (bf16[80,4096]{1,0:T(8,128)(2,1)S(1)}, bf16[80,4096]{1,0:T(8,128)(2,1)S(1)}, u32[]{:S(2)}, u32[]{:S(2)}) collective-permute-start(bf16[80,4096]{1,0:T(8,128)(2,1)S(1)} %slice.31), channel_id=1, source_target_pairs={{0,16},{16,32},{32,48},{48,0},{1,17},{17,33},{33,49},{49,1},{2,18}... | collective-permute-start | bytes 1966088 | tf_op jit(solution)/shard_map/ppermute | solution.py:42
  77.4 15.4 %collective-permute-start.9 = (bf16[80,4096]{1,0:T(8,128)(2,1)S(1)}, bf16[80,4096]{1,0:T(8,128)(2,1)S(1)}, u32[]{:S(2)}, u32[]{:S(2)}) collective-permute-start(bf16[80,4096]{1,0:T(8,128)(2,1)S(1)} %slice.32), channel_id=1, source_target_pairs={{0,48},{16,0},{32,16},{48,32},{1,49},{17,1},{33,17},{49,33},{2,50}... | collective-permute-start | bytes 1966088 | tf_op jit(solution)/shard_map/ppermute | solution.py:46
  78.4 11.8 %collective-permute-start.16 = (bf16[2,160,512]{2,1,0:T(8,128)(2,1)S(1)}, bf16[2,160,512]{2,1,0:T(8,128)(2,1)S(1)}, u32[]{:S(2)}, u32[]{:S(2)}) collective-permute-start(bf16[2,160,512]{2,1,0:T(8,128)(2,1)S(1)} %get-tuple-element.56), channel_id=1, source_target_pairs={{0,6},{2,0},{4,2},{6,4},{1,7},{3,1},{5,3},{7,5},{8,14},{10,8},{12,... | collective-permute-start | bytes 983048 | tf_op jit(solution)/shard_map/ppermute | solution.py:58
  81.7 8.6 %collective-permute-start.15 = (bf16[2,160,512]{2,1,0:T(8,128)(2,1)S(1)}, bf16[2,160,512]{2,1,0:T(8,128)(2,1)S(1)}, u32[]{:S(2)}, u32[]{:S(2)}) collective-permute-start(bf16[2,160,512]{2,1,0:T(8,128)(2,1)S(1)} %get-tuple-element.56), channel_id=1, source_target_pairs={{0,2},{2,4},{4,6},{6,0},{1,3},{3,5},{5,7},{7,1},{8,10},{10,12},{12... | collective-permute-start | bytes 983048 | tf_op jit(solution)/shard_map/ppermute | solution.py:58
  90.2 11.5 %collective-permute-start.18 = (bf16[1,160,512]{2,1,0:T(8,128)(2,1)S(1)}, bf16[1,160,512]{2,1,0:T(8,128)(2,1)S(1)}, u32[]{:S(2)}, u32[]{:S(2)}) collective-permute-start(bf16[1,160,512]{2,1,0:T(8,128)(2,1)S(1)} %slice.40), channel_id=1, source_target_pairs={{0,6},{2,0},{4,2},{6,4},{1,7},{3,1},{5,3},{7,5},{8,14},{10,8},{12,... | collective-permute-start | bytes 491528 | tf_op jit(solution)/shard_map/ppermute | solution.py:58
  90.4 11.3 %collective-permute-start.17 = (bf16[1,160,512]{2,1,0:T(8,128)(2,1)S(1)}, bf16[1,160,512]{2,1,0:T(8,128)(2,1)S(1)}, u32[]{:S(2)}, u32[]{:S(2)}) collective-permute-start(bf16[1,160,512]{2,1,0:T(8,128)(2,1)S(1)} %slice.39), channel_id=1, source_target_pairs={{0,2},{2,4},{4,6},{6,0},{1,3},{3,5},{5,7},{7,1},{8,10},{10,12},{12... | collective-permute-start | bytes 491528 | tf_op jit(solution)/shard_map/ppermute | solution.py:58
  92.9 1.6 %copy-start.4 = (bf16[160,4096]{1,0:T(8,128)(2,1)}, bf16[160,4096]{1,0:T(8,128)(2,1)S(1)}, u32[]{:S(2)}) copy-start(bf16[160,4096]{1,0:T(8,128)(2,1)S(1)} %constant_dynamic-update-slice_fusion.4.refs_6_) | copy-start | bytes 3932164
  94.4 7.3 %copy-start = (bf16[8,160,512]{2,1,0:T(8,128)(2,1)}, bf16[8,160,512]{2,1,0:T(8,128)(2,1)S(1)}, u32[]{:S(2)}) copy-start(bf16[8,160,512]{2,1,0:T(8,128)(2,1)S(1)} %fusion.23) | copy-start | bytes 3932164
  95.5 20.5 %collective-permute-start.12 = (bf16[2,160,512]{2,1,0:T(8,128)(2,1)}, bf16[2,160,512]{2,1,0:T(8,128)(2,1)S(1)}, u32[]{:S(2)}, u32[]{:S(2)}) collective-permute-start(bf16[2,160,512]{2,1,0:T(8,128)(2,1)} %get-tuple-element.61), channel_id=1, source_target_pairs={{0,2},{2,4},{4,6},{6,0},{1,3},{3,5},{5,7},{7,1},{8,10},{10,12},{12... | collective-permute-start | bytes 983048 | tf_op jit(solution)/shard_map/ppermute | solution.py:58
  98.3 17.8 %collective-permute-start.14 = (bf16[2,160,512]{2,1,0:T(8,128)(2,1)}, bf16[2,160,512]{2,1,0:T(8,128)(2,1)}, u32[]{:S(2)}, u32[]{:S(2)}) collective-permute-start(bf16[2,160,512]{2,1,0:T(8,128)(2,1)} %get-tuple-element.62), channel_id=1, source_target_pairs={{0,4},{2,6},{4,0},{6,2},{1,5},{3,7},{5,1},{7,3},{8,12},{10,14},{12... | collective-permute-start | bytes 983048 | tf_op jit(solution)/shard_map/ppermute | solution.py:58
  99.1 17.0 %collective-permute-start.13 = (bf16[2,160,512]{2,1,0:T(8,128)(2,1)S(1)}, bf16[2,160,512]{2,1,0:T(8,128)(2,1)}, u32[]{:S(2)}, u32[]{:S(2)}) collective-permute-start(bf16[2,160,512]{2,1,0:T(8,128)(2,1)S(1)} %get-tuple-element.63), channel_id=1, source_target_pairs={{0,6},{2,0},{4,2},{6,4},{1,7},{3,1},{5,3},{7,5},{8,14},{10,8},{12,... | collective-permute-start | bytes 983048 | tf_op jit(solution)/shard_map/ppermute | solution.py:58
  116.0 12.4 %copy-start.6 = (f32[256,2048]{1,0:T(8,128)S(1)}, f32[256,2048]{1,0:T(8,128)}, u32[]{:S(2)}) copy-start(f32[256,2048]{1,0:T(8,128)} %get-tuple-element.47) | copy-start | bytes 6291460
  117.7 10.7 %collective-permute-start.21 = (bf16[256,2048]{1,0:T(8,128)(2,1)}, bf16[256,2048]{1,0:T(8,128)(2,1)S(1)}, u32[]{:S(2)}, u32[]{:S(2)}) collective-permute-start(bf16[256,2048]{1,0:T(8,128)(2,1)} %get-tuple-element.48), channel_id=1, source_target_pairs={{0,8},{8,0},{1,9},{9,1},{2,10},{10,2},{3,11},{11,3},{4,12},{12,4},... | collective-permute-start | bytes 3145736 | tf_op jit(solution)/shard_map/ppermute | solution.py:54
  117.8 11.9 %collective-permute-start.22 = (bf16[256,2048]{1,0:T(8,128)(2,1)}, bf16[256,2048]{1,0:T(8,128)(2,1)S(1)}, u32[]{:S(2)}, u32[]{:S(2)}) collective-permute-start(bf16[256,2048]{1,0:T(8,128)(2,1)} %get-tuple-element.50), channel_id=1, source_target_pairs={{0,8},{8,0},{1,9},{9,1},{2,10},{10,2},{3,11},{11,3},{4,12},{12,4},... | collective-permute-start | bytes 3145736 | tf_op jit(solution)/shard_map/ppermute | solution.py:54
  118.3 13.8 %collective-permute-start.19 = (bf16[160,512]{1,0:T(8,128)(2,1)S(1)}, bf16[160,512]{1,0:T(8,128)(2,1)S(1)}, u32[]{:S(2)}, u32[]{:S(2)}) collective-permute-start(bf16[160,512]{1,0:T(8,128)(2,1)S(1)} %get-tuple-element.45), channel_id=1, source_target_pairs={{0,0},{1,16},{2,32},{3,48},{4,64},{5,80},{6,96},{7,112},{8,8},{9,2... | collective-permute-start | bytes 491528 | tf_op jit(solution)/shard_map/ppermute | solution.py:188
  124.8 12.3 %collective-permute-start.20 = (bf16[160,512]{1,0:T(8,128)(2,1)S(1)}, bf16[160,512]{1,0:T(8,128)(2,1)S(1)}, u32[]{:S(2)}, u32[]{:S(2)}) collective-permute-start(bf16[160,512]{1,0:T(8,128)(2,1)S(1)} %get-tuple-element.46), channel_id=1, source_target_pairs={{0,16},{1,0},{2,48},{3,32},{4,80},{5,64},{6,112},{7,96},{8,24},{9,... | collective-permute-start | bytes 491528 | tf_op jit(solution)/shard_map/ppermute | solution.py:189
  128.4 2.0 %copy-start.5 = (f32[256,2048]{1,0:T(8,128)S(1)}, f32[256,2048]{1,0:T(8,128)}, u32[]{:S(2)}) copy-start(f32[256,2048]{1,0:T(8,128)} %get-tuple-element.49) | copy-start | bytes 6291460
